TPU v7x, 32 devices: a whole 2x2x4 slice. The times are simulated.
32 devices in a mesh: dp: 16 (over z, y, x), seq: 2 (over core).
Axes of the slice: x: 2, y: 2, z: 4, core: 2. Of those that a mesh axis runs over, the one named last changes fastest.
Arguments:
- inputs: bfloat16 [16, 512, 2048], P('dp', 'seq'), may hold values from -6 to 6
- starts: int32 [16, 512], P('dp', 'seq'), may hold values from 0 to 1, as said below
- norm_attn: bfloat16 [2048], P('dp'), may hold values from 0.5 to 1.5
- w_query: bfloat16 [2048, 2048], P('dp'), may hold values from -0.25 to 0.25
- w_key: bfloat16 [2048, 2048], P('dp'), may hold values from -0.25 to 0.25
- w_value: bfloat16 [2048, 2048], P('dp'), may hold values from -0.125 to 0.125
- w_forget: bfloat16 [2048, 256], P('dp'), may hold values from -0.125 to 0.125
- gate_bias: bfloat16 [256], P('dp'), may hold values from -1 to 6
- w_out: bfloat16 [2048, 2048], P('dp'), may hold values from -0.5 to 0.5
- norm_ffn: bfloat16 [2048], P('dp'), may hold values from 0.5 to 1.5
- w_gate: bfloat16 [2048, 5632], P('dp'), may hold values from -0.125 to 0.125
- w_up: bfloat16 [2048, 5632], P('dp'), may hold values from -0.125 to 0.125
- w_down: bfloat16 [5632, 2048], P('dp'), may hold values from -0.15625 to 0.15625
- cotangent: bfloat16 [16, 512, 2048], P('dp', 'seq'), may hold values from -6 to 6
Outputs:
- output: bfloat16 [16, 512, 2048], P('dp', 'seq')
- grad_input: float32 [16, 512, 2048], P('dp', 'seq')
- grad_norm_attn: float32 [2048], P('dp')
- grad_w_query: float32 [2048, 2048], P('dp')
- grad_w_key: float32 [2048, 2048], P('dp')
- grad_w_value: float32 [2048, 2048], P('dp')
- grad_w_forget: float32 [2048, 256], P('dp')
- grad_gate_bias: float32 [256], P('dp')
- grad_w_out: float32 [2048, 2048], P('dp')
- grad_norm_ffn: float32 [2048], P('dp')
- grad_w_gate: float32 [2048, 5632], P('dp')
- grad_w_up: float32 [2048, 5632], P('dp')
- grad_w_down: float32 [5632, 2048], P('dp')
Inputs may be any that keep to these rules, and one draw needn't show every extreme that they name: 1 marks the first position of a document, 0 any other; position 0 of every row is 1, and no document starts at positions 192 to 319 of a row.
All inputs are finite; a program needn't handle non-finite values.
Results may differ from a plain program's by a relative error of at most 0.013.
Values may be sent and summed in bfloat16 or wider, within the bound.
A program may use at most 448 MiB of HBM per device.

v0:
```python
import jax
import jax.numpy as jnp
from jax import lax
from jax.sharding import PartitionSpec as P

HEADS = 4
SLOTS = 64
BLOCK = 64


EPSILON = 1e-06
EXACT_PRECISION = lax.Precision.HIGHEST


def carried_in(part, axis, combine, identity):
    place = lax.axis_index(axis)
    gathered = jax.tree.map(lambda a: lax.all_gather(a, axis), part)
    state = jax.tree.map(lambda a, e: jnp.zeros_like(a) + jnp.asarray(e, a.dtype), part, identity)

    def one(turn, state):
        return combine(
            state, jax.tree.map(lambda a: lax.dynamic_index_in_dim(a, turn, 0, False), gathered)
        )

    return lax.fori_loop(0, place, one, state)


def prefix(array, axis, combine, identity):
    devices, here = (lax.axis_size(axis), lax.axis_index(axis))
    everything = jax.tree.map(
        lambda part, kind: lax.all_gather(part.astype(kind), axis),
        array,
        jax.tree.map(lambda a: jnp.bfloat16 if a.dtype == jnp.float32 else a.dtype, array),
    )
    start = jax.tree.map(
        lambda part, zero: jnp.broadcast_to(jnp.asarray(zero, part.dtype), part.shape),
        array,
        identity,
    )

    def turn(k, before):
        at = devices - 1 - k
        reached = at > here
        new = combine(
            before, jax.tree.map(lambda part, own: part[at].astype(own.dtype), everything, array)
        )
        return jax.tree.map(lambda a, b: jnp.where(reached, a, b), new, before)

    return lax.fori_loop(0, devices, turn, start)


def rms_scale(features, scale_gain):
    return (
        features
        * lax.rsqrt(jnp.mean(features * features, axis=-1, keepdims=True) + EPSILON)
        * scale_gain
    )


def rounded(values_in):
    return lax.optimization_barrier(values_in.astype(jnp.bfloat16)).astype(jnp.float32)


def silu_slope(values_in):
    sigmoid_v = jax.nn.sigmoid(values_in)
    return sigmoid_v * (1.0 + values_in * (1.0 - sigmoid_v))


def block_weights(log_forget, begins):
    positions = log_forget.shape[0]
    cumulative = jnp.cumsum(log_forget, axis=0)
    doc_count = jnp.cumsum(begins.astype(jnp.float32))
    places = jnp.arange(positions)
    same_doc = (doc_count[:, None] == doc_count[None, :]) & (places[None, :] <= places[:, None])
    spread = jnp.minimum(cumulative[:, None] - cumulative[None, :], 0.0)
    weight = (
        jnp.where(same_doc[:, :, None, None], jnp.exp(spread), 0.0) * (-jnp.expm1(log_forget))[None]
    )
    incoming_share = jnp.where((doc_count == 0.0)[:, None, None], jnp.exp(cumulative), 0.0)
    return (weight, incoming_share)


def mix_block(carry_state, pieces):
    slot_key_state, slot_value_state = carry_state
    query_rows, key_matrix, value_matrix, log_forget, begins = pieces
    weight, incoming_share = block_weights(log_forget, begins)
    logit_scale = query_rows.shape[-1] ** (-0.5)
    inner_prod = jnp.einsum("thd,shd->tsh", query_rows, key_matrix, precision=EXACT_PRECISION)
    slot_logits = jnp.einsum("tshm,tsh->thm", weight, inner_prod, precision=EXACT_PRECISION)
    slot_logits = logit_scale * (
        slot_logits
        + incoming_share
        * jnp.einsum("ugj,auj->aug", slot_key_state, query_rows, precision=EXACT_PRECISION)
    )
    slot_weights = jax.nn.softmax(slot_logits, axis=-1)
    paired = jnp.einsum("thm,tshm->tsh", slot_weights, weight, precision=EXACT_PRECISION)
    blended_output = jnp.einsum("tsh,shd->thd", paired, value_matrix, precision=EXACT_PRECISION)
    blended_output = blended_output + jnp.einsum(
        "cfx,fxv->cfv", slot_weights * incoming_share, slot_value_state, precision=EXACT_PRECISION
    )
    closing_row = weight[-1]
    final_incoming = incoming_share[-1][:, :, None]
    slot_key_state = (
        jnp.einsum("xek,xeu->eku", closing_row, key_matrix, precision=EXACT_PRECISION)
        + final_incoming * slot_key_state
    )
    slot_value_state = (
        jnp.einsum("xek,xeu->eku", closing_row, value_matrix, precision=EXACT_PRECISION)
        + final_incoming * slot_value_state
    )
    return ((slot_key_state, slot_value_state), blended_output)


def run_blocks(carry_state, query_rows, key_matrix, value_matrix, log_forget, begins):
    block_count = query_rows.shape[0] // BLOCK
    pieces = tuple(
        (
            member.reshape((block_count, BLOCK) + member.shape[1:])
            for member in (query_rows, key_matrix, value_matrix, log_forget, begins)
        )
    )
    carry_state, blended_output = lax.scan(jax.checkpoint(mix_block), carry_state, pieces)
    return (carry_state, blended_output.reshape(query_rows.shape))


def mix_one(query_rows, key_matrix, value_matrix, log_forget, key_in, value_in, begins):
    return run_blocks((key_in, value_in), query_rows, key_matrix, value_matrix, log_forget, begins)[
        1
    ]


def end_block(carry_state, pieces):
    slot_key_state, slot_value_state = carry_state
    key_matrix, value_matrix, log_forget, begins = pieces
    cumulative = jnp.cumsum(log_forget, axis=0)
    doc_count = jnp.cumsum(begins.astype(jnp.float32))
    closing_row = jnp.where(
        (doc_count == doc_count[-1])[:, None, None],
        jnp.exp(jnp.minimum(cumulative[-1][None] - cumulative, 0.0)),
        0.0,
    ) * -jnp.expm1(log_forget)
    final_incoming = jnp.where(doc_count[-1] == 0.0, jnp.exp(cumulative[-1]), 0.0)[:, :, None]
    slot_key_state = (
        jnp.einsum("xek,xeu->eku", closing_row, key_matrix, precision=EXACT_PRECISION)
        + final_incoming * slot_key_state
    )
    slot_value_state = (
        jnp.einsum("xek,xeu->eku", closing_row, value_matrix, precision=EXACT_PRECISION)
        + final_incoming * slot_value_state
    )
    return ((slot_key_state, slot_value_state), None)


def summary(key_matrix, value_matrix, log_forget, begins):
    block_count = key_matrix.shape[0] // BLOCK
    pieces = tuple(
        (
            member.reshape((block_count, BLOCK) + member.shape[1:])
            for member in (key_matrix, value_matrix, log_forget, begins)
        )
    )
    zero_state = jnp.zeros(
        (log_forget.shape[1], log_forget.shape[2], key_matrix.shape[-1]), jnp.float32
    )
    end_states, ignored = lax.scan(jax.checkpoint(end_block), (zero_state, zero_state), pieces)
    decay = jnp.where(jnp.sum(begins) == 0, jnp.exp(jnp.sum(log_forget, axis=0)), 0.0)
    return (decay, end_states[0], end_states[1])


def chain_forward(earlier, later_one):
    factor = later_one[0][..., None]
    return (
        later_one[0] * earlier[0],
        factor * earlier[1] + later_one[1],
        factor * earlier[2] + later_one[2],
    )


def chain_backward(earlier, later_one):
    factor = later_one[0][..., None]
    return (
        later_one[0] * earlier[0],
        later_one[1] + factor * earlier[1],
        later_one[2] + factor * earlier[2],
    )


def body(
    inputs,
    starts,
    norm_attn,
    w_query,
    w_key,
    w_value,
    w_forget,
    gate_bias,
    w_out,
    norm_ffn,
    w_gate,
    w_up,
    w_down,
    cotangent,
):
    row_count, positions, features = inputs.shape
    head_dim = features // HEADS
    tokens_here = row_count * positions
    split_heads = (row_count, positions, HEADS, head_dim)
    f32 = jnp.float32
    bf16 = jnp.bfloat16
    attn_full = (
        lax.all_gather(norm_attn, "dp", axis=0, tiled=True),
        lax.all_gather(w_query, "dp", axis=0, tiled=True),
        lax.all_gather(w_key, "dp", axis=0, tiled=True),
        lax.all_gather(w_value, "dp", axis=0, tiled=True),
        lax.all_gather(w_forget, "dp", axis=0, tiled=True),
        lax.all_gather(gate_bias, "dp", axis=0, tiled=True),
        lax.all_gather(w_out, "dp", axis=0, tiled=True),
    )
    gain_attn, full_query, full_key, full_value, full_forget, full_bias, full_out = attn_full
    flat_input = inputs.reshape(tokens_here, features).astype(f32)
    normed_f32, attn_norm_pull = jax.vjp(rms_scale, flat_input, gain_attn.astype(f32))
    normed_attn = normed_f32.astype(bf16)
    query_pre = jnp.dot(normed_attn, full_query, preferred_element_type=f32)
    key_pre = jnp.dot(normed_attn, full_key, preferred_element_type=f32)
    value_pre = jnp.dot(normed_attn, full_value, preferred_element_type=f32)
    z_total = jnp.dot(normed_attn, full_forget, preferred_element_type=f32) + full_bias.astype(f32)
    query_rows = rounded(jax.nn.silu(query_pre)).reshape(split_heads)
    key_matrix = rounded(jax.nn.silu(key_pre)).reshape(split_heads)
    value_matrix = rounded(value_pre).reshape(split_heads)
    log_forget = (jax.nn.log_sigmoid(z_total) / 8.0).reshape(row_count, positions, HEADS, SLOTS)

    def summary_rows(key_part, value_part, forget_part):
        return jax.vmap(summary)(key_part, value_part, forget_part, starts)

    carried, summary_pull = jax.vjp(summary_rows, key_matrix, value_matrix, log_forget)
    decay, end_keys, end_values = carried
    identity = (jnp.ones_like(decay), jnp.zeros_like(end_keys), jnp.zeros_like(end_values))
    incoming = carried_in((decay, end_keys, end_values), "seq", chain_forward, identity)
    key_in = incoming[1]
    value_in = incoming[2]

    def mixer_rows(query_part, key_part, value_part, forget_part, key_start, value_start):
        return jax.vmap(mix_one)(
            query_part, key_part, value_part, forget_part, key_start, value_start, starts
        )

    mixed_rows, mix_pull = jax.vjp(
        mixer_rows, query_rows, key_matrix, value_matrix, log_forget, key_in, value_in
    )
    mixed_low = mixed_rows.reshape(tokens_here, features).astype(bf16)
    attended = flat_input + jnp.dot(mixed_low, full_out, preferred_element_type=f32)
    ffn_full = (
        lax.all_gather(norm_ffn, "dp", axis=0, tiled=True),
        lax.all_gather(w_gate, "dp", axis=0, tiled=True),
        lax.all_gather(w_up, "dp", axis=0, tiled=True),
        lax.all_gather(w_down, "dp", axis=0, tiled=True),
    )
    gain_ffn, full_gate, full_up, full_down = ffn_full
    normed_ffn_f32, ffn_norm_pull = jax.vjp(rms_scale, attended, gain_ffn.astype(f32))
    normed_ffn = normed_ffn_f32.astype(bf16)
    gate_pre = jnp.dot(normed_ffn, full_gate, preferred_element_type=f32)
    up_pre = jnp.dot(normed_ffn, full_up, preferred_element_type=f32)
    silu_gate = jax.nn.silu(gate_pre)
    hidden = (silu_gate * up_pre).astype(bf16)
    output = (
        (attended + jnp.dot(hidden, full_down, preferred_element_type=f32))
        .astype(bf16)
        .reshape(inputs.shape)
    )
    again_ffn = (
        lax.all_gather(w_gate, "dp", axis=0, tiled=True),
        lax.all_gather(w_up, "dp", axis=0, tiled=True),
        lax.all_gather(w_down, "dp", axis=0, tiled=True),
    )
    back_gate, back_up, back_down = again_ffn
    cot_flat = cotangent.reshape(tokens_here, features)
    grad_down_w = jnp.einsum("tf,td->fd", hidden, cot_flat, preferred_element_type=f32)
    grad_hidden = jnp.einsum("td,fd->tf", cot_flat, back_down, preferred_element_type=f32)
    grad_gate = (grad_hidden * up_pre * silu_slope(gate_pre)).astype(bf16)
    grad_up = (grad_hidden * silu_gate).astype(bf16)
    grad_gate_w = jnp.einsum("td,tf->df", normed_ffn, grad_gate, preferred_element_type=f32)
    grad_up_w = jnp.einsum("td,tf->df", normed_ffn, grad_up, preferred_element_type=f32)
    grad_normed_ffn = jnp.einsum("tf,df->td", grad_gate, back_gate, preferred_element_type=f32)
    grad_normed_ffn = grad_normed_ffn + jnp.einsum(
        "tf,df->td", grad_up, back_up, preferred_element_type=f32
    )
    grad_from_ffn, grad_gain_ffn = ffn_norm_pull(grad_normed_ffn)
    grad_attended = cot_flat.astype(f32) + grad_from_ffn
    ffn_shares = (
        lax.psum_scatter(grad_gain_ffn, "dp", scatter_dimension=0, tiled=True),
        lax.psum_scatter(grad_gate_w, "dp", scatter_dimension=0, tiled=True),
        lax.psum_scatter(grad_up_w, "dp", scatter_dimension=0, tiled=True),
        lax.psum_scatter(grad_down_w, "dp", scatter_dimension=0, tiled=True),
    )
    again_attn = (
        lax.all_gather(w_query, "dp", axis=0, tiled=True),
        lax.all_gather(w_key, "dp", axis=0, tiled=True),
        lax.all_gather(w_value, "dp", axis=0, tiled=True),
        lax.all_gather(w_forget, "dp", axis=0, tiled=True),
        lax.all_gather(w_out, "dp", axis=0, tiled=True),
    )
    back_query, back_key, back_value, back_forget, back_out = again_attn
    grad_branch = grad_attended.astype(bf16)
    grad_out_w = jnp.einsum("td,te->de", mixed_low, grad_branch, preferred_element_type=f32)
    grad_mixed = jnp.einsum("te,de->td", grad_branch, back_out, preferred_element_type=f32).reshape(
        split_heads
    )
    grad_queries, grad_keys, grad_values, grad_log, grad_key_in, grad_value_in = mix_pull(
        grad_mixed
    )
    back_identity = (
        jnp.ones_like(decay),
        jnp.zeros_like(grad_key_in),
        jnp.zeros_like(grad_value_in),
    )
    outgoing = prefix((decay, grad_key_in, grad_value_in), "seq", chain_backward, back_identity)
    grad_key_out = outgoing[1]
    grad_value_out = outgoing[2]
    grad_decay = jnp.sum(grad_key_out * key_in + grad_value_out * value_in, axis=-1)
    more_keys, more_values, more_log = summary_pull((grad_decay, grad_key_out, grad_value_out))
    grad_keys = grad_keys + more_keys
    grad_values = grad_values + more_values
    grad_log = grad_log + more_log
    grad_query_pre = (grad_queries.reshape(tokens_here, features) * silu_slope(query_pre)).astype(
        bf16
    )
    grad_key_pre = (grad_keys.reshape(tokens_here, features) * silu_slope(key_pre)).astype(bf16)
    grad_value_pre = grad_values.reshape(tokens_here, features).astype(bf16)
    grad_z = grad_log.reshape(tokens_here, HEADS * SLOTS) * jax.nn.sigmoid(-z_total) / 8.0
    grad_bias = jnp.sum(grad_z, axis=0)
    grad_z_low = grad_z.astype(bf16)
    grad_query_w = jnp.einsum("td,te->de", normed_attn, grad_query_pre, preferred_element_type=f32)
    grad_key_w = jnp.einsum("td,te->de", normed_attn, grad_key_pre, preferred_element_type=f32)
    grad_value_w = jnp.einsum("td,te->de", normed_attn, grad_value_pre, preferred_element_type=f32)
    grad_forget_w = jnp.einsum("td,tz->dz", normed_attn, grad_z_low, preferred_element_type=f32)
    grad_normed_attn = jnp.einsum(
        "te,de->td", grad_query_pre, back_query, preferred_element_type=f32
    )
    grad_normed_attn = grad_normed_attn + jnp.einsum(
        "te,de->td", grad_key_pre, back_key, preferred_element_type=f32
    )
    grad_normed_attn = grad_normed_attn + jnp.einsum(
        "te,de->td", grad_value_pre, back_value, preferred_element_type=f32
    )
    grad_normed_attn = grad_normed_attn + jnp.einsum(
        "tz,dz->td", grad_z_low, back_forget, preferred_element_type=f32
    )
    grad_from_attn, grad_gain_attn = attn_norm_pull(grad_normed_attn)
    grad_input = (grad_attended + grad_from_attn).reshape(inputs.shape)
    attn_shares = (
        lax.psum_scatter(grad_gain_attn, "dp", scatter_dimension=0, tiled=True),
        lax.psum_scatter(grad_query_w, "dp", scatter_dimension=0, tiled=True),
        lax.psum_scatter(grad_key_w, "dp", scatter_dimension=0, tiled=True),
        lax.psum_scatter(grad_value_w, "dp", scatter_dimension=0, tiled=True),
        lax.psum_scatter(grad_forget_w, "dp", scatter_dimension=0, tiled=True),
        lax.psum_scatter(grad_bias, "dp", scatter_dimension=0, tiled=True),
        lax.psum_scatter(grad_out_w, "dp", scatter_dimension=0, tiled=True),
    )
    final = (
        lax.psum(attn_shares[0].astype(jnp.bfloat16), "seq").astype(jnp.float32),
        lax.psum(attn_shares[1].astype(jnp.bfloat16), "seq").astype(jnp.float32),
        lax.psum(attn_shares[2].astype(jnp.bfloat16), "seq").astype(jnp.float32),
        lax.psum(attn_shares[3].astype(jnp.bfloat16), "seq").astype(jnp.float32),
        lax.psum(attn_shares[4].astype(jnp.bfloat16), "seq").astype(jnp.float32),
        lax.psum(attn_shares[5].astype(jnp.bfloat16), "seq").astype(jnp.float32),
        lax.psum(attn_shares[6].astype(jnp.bfloat16), "seq").astype(jnp.float32),
        lax.psum(ffn_shares[0].astype(jnp.bfloat16), "seq").astype(jnp.float32),
        lax.psum(ffn_shares[1].astype(jnp.bfloat16), "seq").astype(jnp.float32),
        lax.psum(ffn_shares[2].astype(jnp.bfloat16), "seq").astype(jnp.float32),
        lax.psum(ffn_shares[3].astype(jnp.bfloat16), "seq").astype(jnp.float32),
    )
    return (
        output,
        grad_input,
        final[0],
        final[1],
        final[2],
        final[3],
        final[4],
        final[5],
        final[6],
        final[7],
        final[8],
        final[9],
        final[10],
    )


def solution(mesh):
    in_specs = (
        P("dp", "seq", None),
        P("dp", "seq"),
        P("dp"),
        P("dp", None),
        P("dp", None),
        P("dp", None),
        P("dp", None),
        P("dp"),
        P("dp", None),
        P("dp"),
        P("dp", None),
        P("dp", None),
        P("dp", None),
        P("dp", "seq", None),
    )
    out_specs = (
        P("dp", "seq", None),
        P("dp", "seq", None),
        P("dp"),
        P("dp", None),
        P("dp", None),
        P("dp", None),
        P("dp", None),
        P("dp"),
        P("dp", None),
        P("dp"),
        P("dp", None),
        P("dp", None),
        P("dp", None),
    )
    return jax.shard_map(body, mesh=mesh, in_specs=in_specs, out_specs=out_specs, check_vma=False)
```

profile of v0, /device:TPU:0, one launch (start us, length us, event | category | flops | bytes accessed | tf_op | source)
XLA Modules:
  0.0 6340.2 jit_solution(5184838668369506382)
XLA Ops:
  12.9 43.6 all-reduce.4
  56.6 35.5 all-gather.4
  99.7 83.6 %all-gather.19.cloned.1.call-done = bf16[2048,2048]{1,0:T(8,128)(2,1)} async-done(((bf16[128,2048]{1,0:T(8,128)(2,1)}), bf16[2048,2048]{1,0:T(8,128)(2,1)}) %all-gather.19.cloned.1.call-update) | async-done | bytes 8388624 | tf_op jit(solution)/shard_map/all_gather | solution.py:213
  196.8 100.4 %all-gather.21.cloned.1.call-done = bf16[2048,2048]{1,0:T(8,128)(2,1)} async-done(((bf16[128,2048]{1,0:T(8,128)(2,1)}), bf16[2048,2048]{1,0:T(8,128)(2,1)}) %all-gather.21.cloned.1.call-update) | async-done | bytes 8388624 | tf_op jit(solution)/shard_map/all_gather | solution.py:214
  312.6 38.0 while.120
  355.6 38.2 all-gather.5
  397.5 15.8 all_gather.76
  435.8 195.6 %while.119 = (s32[]{:T(128)}, f32[1,4,64,512]{3,2,1,0:T(8,128)S(1)}, f32[1,4,64,512]{3,2,1,0:T(8,128)S(1)}, bf16[4,1,64,4,512]{4,2,3,1,0:T(8,128)(2,1)}, f32[4,1...) while((s32[]{:T(128)}, f32[1,4,64,512]{3,2,1,0:T(8,128)S(1)}, ...), condition=%wide.region_14.15_spmd.clone, body=%wide.region_9.14_spmd.clone.sunk | while | flops 629079616 | bytes 29852780 | solution.py:122
  444.6 10.7 multiply_reduce_fusion.23
  467.1 13.0 fusion.412
  493.4 10.7 multiply_reduce_fusion.23
  515.9 13.0 fusion.412
  542.2 10.7 multiply_reduce_fusion.23
  564.8 13.0 fusion.412
  591.0 10.7 multiply_reduce_fusion.23
  613.5 13.0 fusion.412
  641.3 160.1 %all-gather.27.cloned.1.call-done = bf16[2048,5632]{1,0:T(8,128)(2,1)} async-done(((bf16[128,5632]{1,0:T(8,128)(2,1)}), bf16[2048,5632]{1,0:T(8,128)(2,1)}) %all-gather.27.cloned.1.call-update) | async-done | bytes 23068688 | tf_op jit(solution)/shard_map/all_gather | solution.py:254
  801.4 13.1 fusion.230
  814.5 239.1 %all-gather.29.cloned.1.call-done = bf16[2048,5632]{1,0:T(8,128)(2,1)} async-done(((bf16[128,5632]{1,0:T(8,128)(2,1)}), bf16[2048,5632]{1,0:T(8,128)(2,1)}) %all-gather.29.cloned.1.call-update) | async-done | bytes 23068688 | tf_op jit(solution)/shard_map/all_gather | solution.py:255
  1053.6 13.2 fusion.231
  1066.9 238.8 %all-gather.31.cloned.1.call-done = bf16[5632,2048]{1,0:T(8,128)(2,1)} async-done(((bf16[352,2048]{1,0:T(8,128)(2,1)}), bf16[5632,2048]{1,0:T(8,128)(2,1)}) %all-gather.31.cloned.1.call-update) | async-done | bytes 23068688 | tf_op jit(solution)/shard_map/all_gather | solution.py:256
  1305.7 18.4 multiply_convert_fusion
  1324.0 12.7 fusion.232
  1336.7 13.8 multiply_reduce_fusion.10
  1368.1 438.5 %while.121 = (s32[]{:T(128)}, f32[1,4,64,512]{3,2,1,0:T(8,128)}, f32[1,4,64,512]{3,2,1,0:T(8,128)}, f32[4,1,64,4,512]{4,3,2,0,1:T(4,128)}, f32[4,1,64,4,512]{4,2...) while((s32[]{:T(128)}, f32[1,4,64,512]{3,2,1,0:T(8,128)}, ...), condition=%wide.region_29.30_spmd.clone, body=%wide.region_17.29_spmd.clone.sunk | while | flops 1465073408 | bytes 81651288 | solution.py:122
  1381.2 11.2 multiply_reduce_fusion.24
  1423.1 18.3 multiply_reduce_fusion.26
  1453.2 9.6 fusion.466
  1489.3 11.2 multiply_reduce_fusion.24
  1531.1 18.3 multiply_reduce_fusion.26
  1597.2 11.2 multiply_reduce_fusion.24
  1639.1 18.3 multiply_reduce_fusion.26
  1705.2 11.2 multiply_reduce_fusion.24
  1747.1 18.3 multiply_reduce_fusion.26
  1777.2 9.6 fusion.466
  1818.7 49.6 while.118
  1929.5 20.0 fusion.234
  1949.6 20.3 fusion.235
  1970.0 19.5 fusion.190
  1991.3 308.8 %reduce-scatter.9.cloned.1.call-done = f32[128,2048]{1,0:T(8,128)} async-done(((f32[2048,2048]{1,0:T(8,128)}), f32[128,2048]{1,0:T(8,128)}) %reduce-scatter.9.cloned.1.call-update) | async-done | bytes 1048592 | tf_op jit(solution)/shard_map/reduce_scatter | solution.py:352
  2302.2 352.2 %reduce-scatter.11.cloned.1.call-done = f32[128,2048]{1,0:T(8,128)} async-done(((f32[2048,2048]{1,0:T(8,128)}), f32[128,2048]{1,0:T(8,128)}) %reduce-scatter.11.cloned.1.call-update) | async-done | bytes 1048592 | tf_op jit(solution)/shard_map/reduce_scatter | solution.py:353
  2656.6 352.1 %reduce-scatter.13.cloned.1.call-done = f32[128,2048]{1,0:T(8,128)} async-done(((f32[2048,2048]{1,0:T(8,128)}), f32[128,2048]{1,0:T(8,128)}) %reduce-scatter.13.cloned.1.call-update) | async-done | bytes 1048592 | tf_op jit(solution)/shard_map/reduce_scatter | solution.py:354
  3010.7 352.1 %reduce-scatter.17.cloned.1.call-done = f32[128,2048]{1,0:T(8,128)} async-done(((f32[2048,2048]{1,0:T(8,128)}), f32[128,2048]{1,0:T(8,128)}) %reduce-scatter.17.cloned.1.call-update) | async-done | bytes 1048592 | tf_op jit(solution)/shard_map/reduce_scatter | solution.py:357
  3364.9 943.9 %reduce-scatter.19.cloned.1.call-done = f32[128,5632]{1,0:T(8,128)} async-done(((f32[2048,5632]{1,0:T(8,128)}), f32[128,5632]{1,0:T(8,128)}) %reduce-scatter.19.cloned.1.call-update) | async-done | bytes 2883600 | tf_op jit(solution)/shard_map/reduce_scatter | solution.py:291
  4311.9 942.4 %reduce-scatter.21.cloned.1.call-done = f32[128,5632]{1,0:T(8,128)} async-done(((f32[2048,5632]{1,0:T(8,128)}), f32[128,5632]{1,0:T(8,128)}) %reduce-scatter.21.cloned.1.call-update) | async-done | bytes 2883600 | tf_op jit(solution)/shard_map/reduce_scatter | solution.py:292
  5257.4 942.4 %reduce-scatter.23.cloned.1.call-done = f32[352,2048]{1,0:T(8,128)} async-done(((f32[5632,2048]{1,0:T(8,128)}), f32[352,2048]{1,0:T(8,128)}) %reduce-scatter.23.cloned.1.call-update) | async-done | bytes 2883600 | tf_op jit(solution)/shard_map/reduce_scatter | solution.py:293
  6220.9 79.4 %all-reduce.8 = (bf16[2048]{0:T(1024)(128)(2,1)S(1)}, bf16[256]{0:T(256)(128)(2,1)S(1)}, bf16[2048]{0:T(1024)(128)(2,1)S(1)}) all-reduce(f32[2048]{0:T(1024)S(1)} %get-tuple-element.1391, f32[256]{0:T(256)S(1)} %copy-done.79, f32[2048]{0:T(1024)S(1)} %copy-done.78), channel_id=6, replica_groups=mesh['dp'=16,'seq'=2] {'dp'}, use_global_device_ids=true, to_apply=%region_43.44.clone | all-reduce | flops 4352 | bytes 26112
  6308.4 12.1 fusion.177
  (1025 shorter events, 702.5 us)
Async XLA Ops:
  7.2 88.1 %copy-start.23 = (bf16[1,256,2048]{2,1,0:T(8,128)(2,1)S(1)}, bf16[1,256,2048]{2,1,0:T(8,128)(2,1)}, u32[]{:S(2)}) copy-start(bf16[1,256,2048]{2,1,0:T(8,128)(2,1)} %param.26) | copy-start | bytes 3145732
  7.2 88.4 %all-gather.17.cloned.1.call-start = ((), (), s32[]{:S(2)}) async-start(), calls=%async_computation.8 | async-start | bytes 1114112 | tf_op jit(solution)/shard_map/all_gather | solution.py:215
  7.9 175.4 %all-gather.19.cloned.1.call-start = ((), (), s32[]{:S(2)}) async-start(), calls=%async_computation.9 | async-start | bytes 8912896 | tf_op jit(solution)/shard_map/all_gather | solution.py:213
  8.7 288.5 %all-gather.21.cloned.1.call-start = ((), (), s32[]{:S(2)}) async-start(), calls=%async_computation.10 | async-start | bytes 8912896 | tf_op jit(solution)/shard_map/all_gather | solution.py:214
  9.4 403.8 %all-gather.23.cloned.1.call-start = ((), (), s32[]{:S(2)}) async-start(), calls=%async_computation.11 | async-start | bytes 8912896 | tf_op jit(solution)/shard_map/all_gather | solution.py:212
  10.0 414.2 %all-gather.33.cloned.1.call-start = ((), (), s32[]{:S(2)}) async-start(), calls=%async_computation.24 | async-start | bytes 1572864 | tf_op jit(solution)/shard_map/all_gather | solution.py:17
  92.1 321.2 %copy-start.68 = (f32[16,1,128]{2,1,0:T(1,128)}, f32[16,1,128]{2,1,0:T(1,128)S(1)}, u32[]{:S(2)}) copy-start(f32[16,1,128]{2,1,0:T(1,128)S(1)} %convert_element_type.332) | copy-start | bytes 24580
  95.6 317.7 %copy-start.70 = (f32[256]{0:T(256)}, f32[256]{0:T(256)S(1)}, u32[]{:S(2)}) copy-start(f32[256]{0:T(256)S(1)} %fusion.205) | copy-start | bytes 3076
  98.7 296.8 %copy-start.80 = (f32[256]{0:T(256)}, f32[256]{0:T(256)S(1)}, u32[]{:S(2)}) copy-start(f32[256]{0:T(256)S(1)} %get-tuple-element.1538) | copy-start | bytes 3076
  351.4 81.0 %all-gather.35.cloned.1.call-start = ((), (), s32[]{:S(2)}) async-start(), calls=%async_computation.25 | async-start | bytes 1572864 | tf_op jit(solution)/shard_map/all_gather | solution.py:17
  352.0 282.8 %all-gather.25.cloned.1.call-start = ((), (), s32[]{:S(2)}) async-start(), calls=%async_computation.12 | async-start | bytes 8912896 | tf_op jit(solution)/shard_map/all_gather | solution.py:217
  352.8 448.7 %all-gather.27.cloned.1.call-start = ((), (), s32[]{:S(2)}) async-start(), calls=%async_computation.13 | async-start | bytes 24510464 | tf_op jit(solution)/shard_map/all_gather | solution.py:254
  353.5 700.1 %all-gather.29.cloned.1.call-start = ((), (), s32[]{:S(2)}) async-start(), calls=%async_computation.14 | async-start | bytes 24510464 | tf_op jit(solution)/shard_map/all_gather | solution.py:255
  354.3 951.4 %all-gather.31.cloned.1.call-start = ((), (), s32[]{:S(2)}) async-start(), calls=%async_computation.15 | async-start | bytes 24510464 | tf_op jit(solution)/shard_map/all_gather | solution.py:256
  354.8 1634.9 %reduce-scatter.15.cloned.1.call-start = ((), (), s32[]{:S(2)}) async-start(), calls=%async_computation.19 | async-start | bytes 2228224 | tf_op jit(solution)/shard_map/reduce_scatter | solution.py:355
  564.8 14.7 copy-start.54
  641.0 709.5 %copy-start.43 = (f32[256,2048]{1,0:T(8,128)}, f32[256,2048]{1,0:T(8,128)S(1)}, u32[]{:S(2)}) copy-start(f32[256,2048]{1,0:T(8,128)S(1)} %get-tuple-element.1588) | copy-start | bytes 6291460
  641.3 412.3 %copy-start.42 = (bf16[256,2048]{1,0:T(8,128)(2,1)}, bf16[256,2048]{1,0:T(8,128)(2,1)S(1)}, u32[]{:S(2)}) copy-start(bf16[256,2048]{1,0:T(8,128)(2,1)S(1)} %multiply_convert_fusion.5) | copy-start | bytes 3145732
  1370.4 50.3 copy-start.6
  1373.0 46.4 copy-start
  1375.3 29.2 copy-start.8
  1377.1 40.8 copy-start.2
  1422.3 19.1 copy-start.31
  1477.2 51.6 copy-start.6
  1479.7 47.7 copy-start
  1482.1 30.5 copy-start.8
  1485.1 40.8 copy-start.2
  1530.3 19.1 copy-start.31
  1585.2 51.6 copy-start.6
  1587.7 47.7 copy-start
  1590.0 30.5 copy-start.8
  1593.1 40.8 copy-start.2
  1638.3 19.1 copy-start.31
  1693.1 51.6 copy-start.6
  1695.7 47.7 copy-start
  1698.0 30.5 copy-start.8
  1701.1 40.8 copy-start.2
  1746.3 19.1 copy-start.31
  1818.7 52.6 copy-start.81
  1875.5 424.6 %reduce-scatter.9.cloned.1.call-start = ((), (), s32[]{:S(2)}) async-start(), calls=%async_computation.16 | async-start | bytes 17825792 | tf_op jit(solution)/shard_map/reduce_scatter | solution.py:352
  1887.3 767.2 %reduce-scatter.11.cloned.1.call-start = ((), (), s32[]{:S(2)}) async-start(), calls=%async_computation.17 | async-start | bytes 17825792 | tf_op jit(solution)/shard_map/reduce_scatter | solution.py:353
  1904.0 1104.6 %reduce-scatter.13.cloned.1.call-start = ((), (), s32[]{:S(2)}) async-start(), calls=%async_computation.18 | async-start | bytes 17825792 | tf_op jit(solution)/shard_map/reduce_scatter | solution.py:354
  1918.0 1444.9 %reduce-scatter.17.cloned.1.call-start = ((), (), s32[]{:S(2)}) async-start(), calls=%async_computation.20 | async-start | bytes 17825792 | tf_op jit(solution)/shard_map/reduce_scatter | solution.py:357
  1929.1 2379.8 %reduce-scatter.19.cloned.1.call-start = ((), (), s32[]{:S(2)}) async-start(), calls=%async_computation.21 | async-start | bytes 49020928 | tf_op jit(solution)/shard_map/reduce_scatter | solution.py:291
  1949.6 3304.7 %reduce-scatter.21.cloned.1.call-start = ((), (), s32[]{:S(2)}) async-start(), calls=%async_computation.22 | async-start | bytes 49020928 | tf_op jit(solution)/shard_map/reduce_scatter | solution.py:292
  1970.0 4229.8 %reduce-scatter.23.cloned.1.call-start = ((), (), s32[]{:S(2)}) async-start(), calls=%async_computation.23 | async-start | bytes 49020928 | tf_op jit(solution)/shard_map/reduce_scatter | solution.py:293
  1989.5 4331.0 %all-reduce.13.cloned.1.call-start = ((), (), s32[]{:S(2)}) async-start(), calls=%async_computation.26 | async-start | bytes 12976128 | tf_op jit(solution)/shard_map/psum | solution.py:361
  6218.8 86.0 %copy-start.77 = (f32[256]{0:T(256)S(1)}, f32[256]{0:T(256)}, u32[]{:S(2)}) copy-start(f32[256]{0:T(256)} %copy-done.76) | copy-start | bytes 3076
  (155 other events, 728.8 us)
Sparse Core Ops, SparseCore 0:
  10.8 58.0 all-gather.16
  71.7 111.6 all-gather.18
  186.1 111.0 all-gather.20
  299.8 111.1 all-gather.22
  412.9 7.2 all-gather.32
  422.2 10.1 all-gather.34
  435.2 113.9 all-gather.24
  551.9 249.4 all-gather.26
  804.1 249.4 all-gather.28
  1056.2 249.4 all-gather.30
  1875.6 78.7 reduce-scatter.14
  1956.5 343.5 reduce-scatter.8
  2302.4 351.9 reduce-scatter.10
  2656.6 351.9 reduce-scatter.12
  3010.8 352.0 reduce-scatter.16
  3365.1 943.7 reduce-scatter.18
  4311.0 943.2 reduce-scatter.20
  5256.5 943.2 reduce-scatter.22
  6203.7 38.0 all-reduce.12
where the time goes:
time: 6350 us; the launch traced here: 6340 us
  waiting for transfers between devices  5030 us (79%)
  matrix products  459 us (7%)
  other arithmetic  362 us (6%)
  local copies, waits for them, and re-layouts  232 us (4%)
  blocking collectives  221 us (3%)
    reduce_scatter x1, waiting for transfers between devices, body(): lax.psum_scatter(grad_gate_w, 'dp', scatter_dimension=0, tiled=True)  944 us
    reduce_scatter x1, waiting for transfers between devices, body(): lax.psum_scatter(grad_up_w, 'dp', scatter_dimension=0, tiled=True)  942 us
    reduce_scatter x1, waiting for transfers between devices, body(): lax.psum_scatter(grad_down_w, 'dp', scatter_dimension=0, tiled=True)  942 us
    reduce_scatter x1, waiting for transfers between devices, body(): lax.psum_scatter(grad_key_w, 'dp', scatter_dimension=0, tiled=True)  352 us
    reduce_scatter x1, waiting for transfers between devices, body(): lax.psum_scatter(grad_out_w, 'dp', scatter_dimension=0, tiled=True)  352 us
    reduce_scatter x1, waiting for transfers between devices, body(): lax.psum_scatter(grad_value_w, 'dp', scatter_dimension=0, tiled=True)  352 us
    reduce_scatter x1, waiting for transfers between devices, body(): lax.psum_scatter(grad_query_w, 'dp', scatter_dimension=0, tiled=True)  309 us
    all_gather x1, waiting for transfers between devices, body(): lax.all_gather(w_up, 'dp', axis=0, tiled=True)  239 us
  transfers between devices with their start and end apart: 19, of which 13 were waited for; matrix products, arithmetic and copies ran while one was open for 7% of the time, Pallas kernels for 0%

commit v1 on v0

v1 whole, which is shorter than its diff:
```python
import functools

import jax
import jax.numpy as jnp
from jax import lax
from jax.sharding import Mesh
from jax.sharding import PartitionSpec as P
from jax.experimental import pallas as pl
from jax.experimental.pallas import tpu as pltpu

SLOTS = 64
TILE = 128
F32, BF16 = jnp.float32, jnp.bfloat16
NN = (((1,), (0,)), ((), ()))
NT = (((1,), (1,)), ((), ()))
TN = (((0,), (0,)), ((), ()))
HALVES = (64, 32, 16, 8, 4, 2, 1)


def dot(a, b, dims):
    return lax.dot_general(a, b, dims, preferred_element_type=F32)


def parts_of(a):
    high = a.astype(BF16)
    return high, (a - high.astype(F32)).astype(BF16)


def dot_parts(a, b, dims):
    return dot(a[0], b[0], dims) + (dot(a[1], b[0], dims) + dot(a[0], b[1], dims))


def dot_ones(ones, a):
    high = a.astype(BF16)
    rest = a - high.astype(F32)
    middle = rest.astype(BF16)
    low = (rest - middle.astype(F32)).astype(BF16)
    return dot(ones, high, NN) + (dot(ones, middle, NN) + dot(ones, low, NN))


def places():
    shape = (TILE, TILE)
    return lax.broadcasted_iota(jnp.int32, shape, 0), lax.broadcasted_iota(jnp.int32, shape, 1)


def ones_where(mask):
    return jnp.where(mask, 1.0, 0.0).astype(BF16)


def steps_to_middle(half):
    t, s = places()
    block = 2 * half
    same = (t // block) == (s // block)
    t_right, s_right = (t % block) >= half, (s % block) >= half
    right = t_right & s_right & (s <= t)
    left = jnp.logical_not(t_right | s_right) & (s > t)
    return ones_where(same & (right | left))


def pair_mask(half, turned=False):
    t, s = places()
    if turned:
        t, s = s, t
    block = 2 * half
    return ((t // block) == (s // block)) & ((t % block) >= half) & ((s % block) < half)


def first_row(rows):
    return lax.broadcasted_iota(jnp.int32, (rows, 2 * SLOTS), 1) < SLOTS


def row_sums(a, first):
    return (
        jnp.sum(jnp.where(first, a, 0.0), axis=1, keepdims=True),
        jnp.sum(jnp.where(first, 0.0, a), axis=1, keepdims=True),
    )


def tile_rows(j):
    return pl.ds(pl.multiple_of(j * TILE, TILE), TILE)


def prepare(lf_ref, decay_ref, reach_ref, e_ref, tiles):
    t, s = places()

    @pl.loop(0, tiles)
    def _(j):
        rows = tile_rows(j)
        lf = lf_ref[rows, :]
        decay_ref[rows, :] = dot_ones(ones_where(s <= t), lf)
        reach_ref[rows, :] = dot_ones(ones_where(s > t), lf)
        for level, half in enumerate(HALVES):
            e_ref[level, rows, :] = jnp.exp(dot_ones(steps_to_middle(half), lf))


def far_pairs(tiles):
    out, half = [], tiles // 2
    while half >= 1:
        for start in range(0, tiles, 2 * half):
            out.append((start + half, start, half))
        half //= 2
    return out


def far_decays(right, left, half, decay_ref, reach_ref):
    after, total = [], None
    for j in range(right, right + half):
        part = decay_ref[j * TILE:(j + 1) * TILE, :]
        after.append(jnp.exp(part if total is None else part + total))
        last = part[TILE - 1:TILE, :]
        total = last if total is None else total + last
    before, total = [], None
    for j in range(left + half - 1, left - 1, -1):
        part = reach_ref[j * TILE:(j + 1) * TILE, :]
        before.append(jnp.exp(part if total is None else part + total))
        whole = decay_ref[(j + 1) * TILE - 1:(j + 1) * TILE, :]
        total = whole if total is None else total + whole
    if half == 1:
        return after[0], before[0]
    return jnp.concatenate(after, axis=0), jnp.concatenate(before[::-1], axis=0)


def diagonal_of(block):
    t, s = places()
    return jnp.sum(jnp.where(t == s, block, 0.0), axis=1, keepdims=True)


def weighted_sums(a_ref, out_ref, gain_ref, decay_ref, reach_ref, e_ref, tiles):
    first = first_row(TILE)

    @pl.loop(0, tiles)
    def _(j):
        rows = tile_rows(j)
        gain = gain_ref[rows, :]
        blocks = [a_ref[r, rows, rows] for r in range(2)]
        total = jnp.where(first, diagonal_of(blocks[0]), diagonal_of(blocks[1])) * gain
        for level, half in enumerate(HALVES):
            e = e_ref[level, rows, :]
            x = parts_of(e * gain)
            pairs = pair_mask(half)
            y = [dot_parts(parts_of(jnp.where(pairs, a, 0.0)), x, NN) for a in blocks]
            total = total + e * jnp.where(first, y[0], y[1])
        out_ref[rows, :] = total

    for right, left, half in far_pairs(tiles):
        after, before = far_decays(right, left, half, decay_ref, reach_ref)
        here = slice(right * TILE, (right + half) * TILE)
        there = slice(left * TILE, (left + half) * TILE)
        x = parts_of(before * gain_ref[there, :])
        y = [dot_parts(parts_of(a_ref[r, here, there]), x, NN) for r in range(2)]
        out_ref[here, :] += after * jnp.where(first_row(half * TILE), y[0], y[1])


def split_rows(a, first):
    return parts_of(jnp.where(first, a, 0.0)), parts_of(jnp.where(first, 0.0, a))


def paired_weights(p_ref, out_ref, gain_ref, decay_ref, reach_ref, e_ref, tiles):
    first = first_row(TILE)
    t, s = places()

    @pl.loop(0, tiles)
    def _(j):
        rows = tile_rows(j)
        gain, p = gain_ref[rows, :], p_ref[rows, :]
        sums = row_sums(p * gain, first)
        total = [jnp.where(t == s, sums[r], 0.0) for r in range(2)]
        for level, half in enumerate(HALVES):
            e = e_ref[level, rows, :]
            x = parts_of(e * gain)
            pairs = pair_mask(half)
            pe = split_rows(p * e, first)
            total = [total[r] + jnp.where(pairs, dot_parts(pe[r], x, NT), 0.0) for r in range(2)]
        for r in range(2):
            out_ref[r, rows, rows] = total[r]

    for right, left, half in far_pairs(tiles):
        after, before = far_decays(right, left, half, decay_ref, reach_ref)
        here = slice(right * TILE, (right + half) * TILE)
        there = slice(left * TILE, (left + half) * TILE)
        x = parts_of(before * gain_ref[there, :])
        pe = split_rows(p_ref[here, :] * after, first_row(half * TILE))
        for r in range(2):
            out_ref[r, here, there] = dot_parts(pe[r], x, NT)
            out_ref[r, there, here] = jnp.zeros((half * TILE, half * TILE), F32)


def inner(a_ref, b_ref, r):
    return dot(a_ref[0, r], b_ref[0, r], NT) + dot(a_ref[1, r], b_ref[1, r], NT)


def forward_kernel(q_ref, k_ref, v_ref, lf_ref, gain_ref, dcol_ref, drow_ref,
                   mixed_ref, s_ref, p_ref, b_ref, a_ref, decay_ref, reach_ref, e_ref):
    length, depth = q_ref.shape[2:]
    tiles = length // TILE
    scale = (2 * depth) ** -0.5
    for r in range(2):
        same = dcol_ref[r] == drow_ref[r]
        a_ref[r] = jnp.where(same, inner(q_ref, k_ref, r), 0.0)
    prepare(lf_ref, decay_ref, reach_ref, e_ref, tiles)
    weighted_sums(a_ref, s_ref, gain_ref, decay_ref, reach_ref, e_ref, tiles)
    first = first_row(length)
    logits = s_ref[...] * scale
    low = -jnp.inf
    top = jnp.where(
        first,
        jnp.max(jnp.where(first, logits, low), axis=1, keepdims=True),
        jnp.max(jnp.where(first, low, logits), axis=1, keepdims=True),
    )
    grown = jnp.exp(logits - top)
    sums = row_sums(grown, first)
    p_ref[...] = grown / jnp.where(first, sums[0], sums[1])
    paired_weights(p_ref, b_ref, gain_ref, decay_ref, reach_ref, e_ref, tiles)
    for r in range(2):
        b = jnp.where(dcol_ref[r] == drow_ref[r], b_ref[r], 0.0)
        b_ref[r] = b
        high, rest = parts_of(b)
        for f in range(2):
            mixed = (dot(high, v_ref[f, r], NN) + dot(rest, v_ref[f, r], NN)).astype(BF16)
            for place in range(2):
                mixed_ref[r, place, f] = mixed[place * length // 2:(place + 1) * length // 2]


def backward_kernel(q_ref, k_ref, v_ref, g_ref, lf_ref, gain_ref, dcol_ref, drow_ref, s_ref, p_ref, b_ref,
                    gq_ref, gk_ref, gv_ref, gl_ref,
                    a_ref, at_ref, dot_ref, h_ref, back_ref, decay_ref, reach_ref, e_ref):
    length, depth = q_ref.shape[2:]
    tiles = length // TILE
    scale = (2 * depth) ** -0.5
    first_all, first = first_row(length), first_row(TILE)
    t, s = places()
    grads = [[g_ref[r, :, f].reshape(length, depth) for r in range(2)] for f in range(2)]
    for r in range(2):
        same = dcol_ref[r] == drow_ref[r]
        by_t = dot(grads[0][r], v_ref[0, r], NT) + dot(grads[1][r], v_ref[1, r], NT)
        by_s = dot(v_ref[0, r], grads[0][r], NT) + dot(v_ref[1, r], grads[1][r], NT)
        a_ref[r] = jnp.where(same, by_t, 0.0)
        at_ref[0, r] = jnp.where(same, inner(k_ref, q_ref, r), 0.0)
        at_ref[1, r] = jnp.where(same, by_s, 0.0)
    prepare(lf_ref, decay_ref, reach_ref, e_ref, tiles)
    weighted_sums(a_ref, dot_ref, gain_ref, decay_ref, reach_ref, e_ref, tiles)
    p, dots = p_ref[...], dot_ref[...]
    sums = row_sums(p * dots, first_all)
    h = scale * (p * (dots - jnp.where(first_all, sums[0], sums[1])))
    h_ref[...] = h
    dot_ref[...] = h * s_ref[...] + p * dots
    paired_weights(h_ref, a_ref, gain_ref, decay_ref, reach_ref, e_ref, tiles)
    @pl.loop(0, tiles)
    def _(j):
        rows = tile_rows(j)
        h, p = h_ref[rows, :], p_ref[rows, :]
        keys = [at_ref[0, r, rows, rows] for r in range(2)]
        values = [at_ref[1, r, rows, rows] for r in range(2)]
        total = (
            jnp.where(first, diagonal_of(keys[0]), diagonal_of(keys[1])) * h
            + jnp.where(first, diagonal_of(values[0]), diagonal_of(values[1])) * p
        )
        for level, half in enumerate(HALVES):
            e = e_ref[level, rows, :]
            he, pe = parts_of(h * e), parts_of(p * e)
            pairs = pair_mask(half, turned=True)
            y = [
                dot_parts(parts_of(jnp.where(pairs, keys[r], 0.0)), he, NN)
                + dot_parts(parts_of(jnp.where(pairs, values[r], 0.0)), pe, NN)
                for r in range(2)
            ]
            total = total + e * jnp.where(first, y[0], y[1])
        back_ref[rows, :] = total

    for right, left, half in far_pairs(tiles):
        after, before = far_decays(right, left, half, decay_ref, reach_ref)
        here = slice(right * TILE, (right + half) * TILE)
        there = slice(left * TILE, (left + half) * TILE)
        he, pe = parts_of(h_ref[here, :] * after), parts_of(p_ref[here, :] * after)
        y = [
            dot_parts(parts_of(at_ref[0, r, there, here]), he, NN)
            + dot_parts(parts_of(at_ref[1, r, there, here]), pe, NN)
            for r in range(2)
        ]
        back_ref[there, :] += before * jnp.where(first_row(half * TILE), y[0], y[1])

    for r in range(2):
        c = jnp.where(dcol_ref[r] == drow_ref[r], a_ref[r], 0.0)
        high, rest = parts_of(c)
        for f in range(2):
            gq_ref[f, r] = dot(high, k_ref[f, r], NN) + dot(rest, k_ref[f, r], NN)
            gk_ref[f, r] = dot(high, q_ref[f, r], TN) + dot(rest, q_ref[f, r], TN)
        high, rest = parts_of(b_ref[r])
        for f in range(2):
            gv_ref[f, r] = dot(high, grads[f][r], TN) + dot(rest, grads[f][r], TN)
    carried = jnp.zeros((1, 2 * SLOTS), F32)
    for j in range(tiles - 1, -1, -1):
        rows = slice(j * TILE, (j + 1) * TILE)
        back = back_ref[rows, :]
        change = dot_ref[rows, :] - gain_ref[rows, :] * back
        upward = dot_ones(ones_where(s >= t), change) + carried
        gl_ref[rows, :] = upward - jnp.exp(lf_ref[rows, :]) * back
        carried = upward[0:1, :]


def mix_forward(q, k, v, lf, gain, doc):
    rows, length, depth = q.shape[1:]
    lanes = (length, 2 * SLOTS)
    whole = jax.ShapeDtypeStruct((rows, length, length), F32)
    return pl.pallas_call(
        forward_kernel,
        name="mix_forward",
        out_shape=(
            jax.ShapeDtypeStruct((rows, 2, 2, length // 2, depth), BF16), jax.ShapeDtypeStruct(lanes, F32),
            jax.ShapeDtypeStruct(lanes, F32), whole,
        ),
        scratch_shapes=[
            pltpu.VMEM((2, length, length), F32), pltpu.VMEM(lanes, F32), pltpu.VMEM(lanes, F32),
            pltpu.VMEM((len(HALVES),) + lanes, F32),
        ],
        compiler_params=pltpu.CompilerParams(vmem_limit_bytes=40 << 20),
    )(q, k, v, lf, gain, doc[:, :, None], doc[:, None, :])


def mix_backward(q, k, v, g, lf, gain, doc, s, p, b):
    length = q.shape[2]
    lanes = (length, 2 * SLOTS)
    square = (2, length, length)
    return pl.pallas_call(
        backward_kernel,
        name="mix_backward",
        out_shape=(jax.ShapeDtypeStruct(q.shape, F32),) * 3 + (jax.ShapeDtypeStruct(lanes, F32),),
        scratch_shapes=[
            pltpu.VMEM(square, F32), pltpu.VMEM((2,) + square, F32),
            pltpu.VMEM(lanes, F32), pltpu.VMEM(lanes, F32), pltpu.VMEM(lanes, F32),
            pltpu.VMEM(lanes, F32), pltpu.VMEM(lanes, F32), pltpu.VMEM((len(HALVES),) + lanes, F32),
        ],
        compiler_params=pltpu.CompilerParams(vmem_limit_bytes=48 << 20),
    )(q, k, v, g, lf, gain, doc[:, :, None], doc[:, None, :], s, p, b)


HEADS = 4
EPSILON = 1e-06
PLANE = ("y", "x")
MESH = pl.DeviceIdType.MESH


def exchange_kernel(to_homes, same, a_ref, out_ref, send, recv, local):
    y, x, c = (lax.axis_index(name) for name in ("y", "x", "c"))
    barrier = pltpu.get_barrier_semaphore()
    for flip in range(1, 8):
        peer = {
            "y": lax.rem(y + flip // 4, 2), "x": lax.rem(x + (flip // 2) % 2, 2), "c": lax.rem(c + flip % 2, 2)
        }
        pl.semaphore_signal(barrier, inc=1, device_id=peer, device_id_type=MESH)
    pl.semaphore_wait(barrier, 7)
    slot = y * 2 + x if to_homes else x * 2 + c
    for i in range(4):
        if to_homes:
            peer = {"y": c, "x": i // 2, "c": i % 2}
        else:
            peer = {"y": i // 2, "x": i % 2, "c": y}
        mine = (peer["y"] == y) & (peer["x"] == x) & (peer["c"] == c)
        source = a_ref if same else a_ref.at[i]

        @pl.when(mine)
        def _():
            pltpu.make_async_copy(source, out_ref.at[slot], local).start()

        @pl.when(jnp.logical_not(mine))
        def _():
            pltpu.make_async_remote_copy(
                src_ref=source, dst_ref=out_ref.at[slot], send_sem=send.at[i], recv_sem=recv.at[slot],
                device_id=peer, device_id_type=MESH,
            ).start()

    for i in range(4):
        if to_homes:
            peer = {"y": c, "x": i // 2, "c": i % 2}
            giver = {"y": i // 2, "x": i % 2, "c": y}
        else:
            peer = {"y": i // 2, "x": i % 2, "c": y}
            giver = {"y": c, "x": i // 2, "c": i % 2}
        source = a_ref if same else a_ref.at[i]
        sent_here = (peer["y"] == y) & (peer["x"] == x) & (peer["c"] == c)
        from_here = (giver["y"] == y) & (giver["x"] == x) & (giver["c"] == c)

        def whole(device):
            return pltpu.make_async_remote_copy(
                src_ref=source, dst_ref=out_ref.at[i], send_sem=send.at[i], recv_sem=recv.at[i],
                device_id=device, device_id_type=MESH,
            )

        @pl.when(jnp.logical_not(sent_here))
        def _():
            whole(peer).wait_send()

        @pl.when(jnp.logical_not(from_here))
        def _():
            whole(peer).wait_recv()

        @pl.when(from_here)
        def _():
            pltpu.make_async_copy(source, out_ref.at[i], local).wait()


def exchange(a, collective, to_homes, same=False):
    block = a.shape if same else a.shape[1:]
    return pl.pallas_call(
        functools.partial(exchange_kernel, to_homes, same),
        name="to_homes" if to_homes else "from_homes",
        out_shape=jax.ShapeDtypeStruct((4,) + block, a.dtype),
        in_specs=[pl.BlockSpec(memory_space=pl.ANY)],
        out_specs=pl.BlockSpec(memory_space=pl.ANY),
        scratch_shapes=[pltpu.SemaphoreType.DMA((4,)), pltpu.SemaphoreType.DMA((4,)), pltpu.SemaphoreType.DMA],
        compiler_params=pltpu.CompilerParams(collective_id=collective, has_side_effects=True),
    )(a)


def share(a):
    mine = lax.all_to_all(a, PLANE, split_axis=0, concat_axis=0, tiled=True)
    mine = mine.reshape((-1,) + a.shape[2:])
    return lax.all_gather(mine, ("c", "z"), axis=0, tiled=True).reshape((2, -1) + a.shape[2:])


def sum_over(a, axes):
    return lax.psum_scatter(a.astype(BF16), axes, scatter_dimension=0, tiled=True)


def slope(v):
    s = jax.nn.sigmoid(v)
    return s * (1.0 + v * (1.0 - s))


def scaled(features):
    return lax.rsqrt(jnp.mean(features * features, axis=-1, keepdims=True) + EPSILON)


def norm_back(grad, gain, features, ratio):
    u, xh = grad * gain, features * ratio
    return ratio * (u - xh * jnp.mean(u * xh, axis=-1, keepdims=True))


def body(inputs, starts, norm_attn, w_query, w_key, w_value, w_forget, gate_bias, w_out, norm_ffn, w_gate, w_up,
         w_down, cotangent):
    positions, features = inputs.shape[1:]
    depth = features // HEADS
    y, x, c, z = (lax.axis_index(name) for name in ("y", "x", "c", "z"))
    planes = lax.axis_size("z")
    head = y * 2 + x
    rows_here = w_query.shape[0]
    hidden_here = w_down.shape[0]

    def own_half(a, axis):
        return lax.dynamic_index_in_dim(a, c, axis, keepdims=False)

    bias_here = gate_bias.shape[0]
    small = jnp.concatenate([norm_attn, norm_ffn, gate_bias, starts[0].astype(BF16)])
    small = lax.all_gather(small, ("z", "y", "x", "c"), axis=0)
    small = small.reshape((planes, 2, 2, 2, small.shape[-1]))
    cuts = [rows_here, 2 * rows_here, 2 * rows_here + bias_here]
    gain_attn, gain_ffn, bias = (
        part[:, :, :, 0].reshape(-1).astype(F32) for part in jnp.split(small[..., :cuts[2]], cuts[:2], axis=-1)
    )
    begins = lax.dynamic_index_in_dim(small[..., cuts[2]:], z, 0, keepdims=False)
    begins = lax.dynamic_index_in_dim(begins, c, 0, keepdims=False).reshape(2, 2 * positions).astype(F32)
    doc = jnp.cumsum(begins, axis=1)
    bias = lax.dynamic_slice_in_dim(bias, head * SLOTS, SLOTS)

    def columns(w):
        w = w.reshape(rows_here, HEADS, 2, -1)
        return own_half(w, 2).transpose(1, 0, 2)

    mixer_w = share(jnp.concatenate([columns(w) for w in (w_query, w_key, w_value, w_forget)], axis=-1))

    def hidden_columns(w):
        w = own_half(w.reshape(rows_here, planes, 4, 2, hidden_here // 2), 3)
        return w.transpose(2, 0, 1, 3).reshape(4, rows_here, -1)

    full_gate, full_up = share(hidden_columns(w_gate)), share(hidden_columns(w_up))
    down_half = own_half(w_down.reshape(2, hidden_here // 2, features), 0)
    full_down = lax.all_gather(down_half, ("c", "z"), axis=0, tiled=True).reshape(2, -1, features)
    out_half = own_half(w_out.reshape(2, rows_here // 2, features), 0)
    full_out = lax.all_gather(out_half, ("z", "y", "x", "c"), axis=0, tiled=True)

    x_here = inputs.reshape(positions, features)
    cot_here = cotangent.reshape(positions, features)
    x_rows = exchange(x_here, 1, False, same=True).reshape(4 * positions, features).astype(F32)
    cot = exchange(cot_here, 2, False, same=True).reshape(4 * positions, features)
    normed = (x_rows * scaled(x_rows) * gain_attn).astype(BF16)
    pre = jnp.einsum("td,cdf->ctf", normed, mixer_w, preferred_element_type=F32)
    by_row = (2, 2, 2 * positions, depth // 2)
    query_pre, key_pre, value_pre = (
        pre[:, :, i * depth // 2:(i + 1) * depth // 2].reshape(by_row) for i in range(3)
    )
    z_total = pre[:, :, 3 * depth // 2:].reshape(2, 2, 2 * positions, SLOTS // 2)
    z_total = z_total.transpose(2, 1, 0, 3).reshape(2 * positions, 2 * SLOTS) + jnp.tile(bias, 2)
    log_forget = jax.nn.log_sigmoid(z_total) / 8.0
    gain = -jnp.expm1(log_forget)
    queries, keys, values = jax.nn.silu(query_pre).astype(BF16), jax.nn.silu(key_pre).astype(BF16), value_pre.astype(BF16)
    mixed, scores, probs, paired = mix_forward(queries, keys, values, log_forget, gain, doc)
    mixed = exchange(mixed.reshape(4, 2 * positions, depth // 2), 3, True)
    mixed = mixed.reshape(2 * HEADS, positions, depth // 2).transpose(1, 0, 2).reshape(positions, features)
    attended = x_here.astype(F32) + jnp.dot(mixed, full_out, preferred_element_type=F32)

    ratio_f = scaled(attended)
    normed_ffn = exchange((attended * ratio_f * gain_ffn).astype(BF16), 4, False, same=True)
    normed_ffn = normed_ffn.reshape(4 * positions, features)
    gate_pre = jnp.einsum("td,cdf->ctf", normed_ffn, full_gate, preferred_element_type=F32)
    up_pre = jnp.einsum("td,cdf->ctf", normed_ffn, full_up, preferred_element_type=F32)
    silu_gate = jax.nn.silu(gate_pre)
    hidden = (silu_gate * up_pre).astype(BF16)
    grad_hidden = jnp.einsum("td,cfd->ctf", cot, full_down, preferred_element_type=F32)
    grad_gate = (grad_hidden * up_pre * slope(gate_pre)).astype(BF16)
    grad_up = (grad_hidden * silu_gate).astype(BF16)
    grad_down_w = jnp.einsum("ctf,td->cfd", hidden, cot, preferred_element_type=F32)
    grad_down_w = sum_over(grad_down_w.reshape(-1, features), ("c", "z"))
    grad_normed_ffn = (
        jnp.einsum("ctf,cdf->td", grad_gate, full_gate, preferred_element_type=F32)
        + jnp.einsum("ctf,cdf->td", grad_up, full_up, preferred_element_type=F32)
    ).astype(BF16)
    grad_normed_ffn = exchange(grad_normed_ffn.reshape(4, positions, features), 5, True)
    grad_normed_ffn = jnp.sum(grad_normed_ffn.astype(F32), axis=0)
    grad_gate_w = jnp.einsum("td,ctf->cdf", normed_ffn, grad_gate, preferred_element_type=F32)
    grad_gate_w = sum_over(grad_gate_w.reshape(2 * features, -1), ("c", "z"))
    grad_up_w = jnp.einsum("td,ctf->cdf", normed_ffn, grad_up, preferred_element_type=F32)
    grad_up_w = sum_over(grad_up_w.reshape(2 * features, -1), ("c", "z"))
    block_out = jnp.einsum("ctf,cfd->td", hidden, full_down, preferred_element_type=F32).astype(BF16)
    block_out = exchange(block_out.reshape(4, positions, features), 6, True)
    output = (attended + jnp.sum(block_out.astype(F32), axis=0)).astype(BF16)
    grad_gain_ffn = jnp.sum(grad_normed_ffn * attended * ratio_f, axis=0)
    grad_attended = cot_here.astype(F32) + norm_back(grad_normed_ffn, gain_ffn, attended, ratio_f)

    grad_branch = grad_attended.astype(BF16)
    grad_out_w = jnp.einsum("td,te->de", mixed, grad_branch, preferred_element_type=F32)
    grad_out_w = sum_over(grad_out_w, ("z", "y", "x", "c"))
    grad_mixed = jnp.einsum("te,de->td", grad_branch, full_out, preferred_element_type=F32).astype(BF16)
    grad_mixed = grad_mixed.reshape(positions, HEADS, 2, depth // 2).transpose(1, 2, 0, 3)
    grad_mixed = exchange(grad_mixed.reshape(4, 2 * positions, depth // 2), 7, False)
    grad_mixed = grad_mixed.reshape(2, 2, 2, positions, depth // 2)
    grad_queries, grad_keys, grad_values, grad_log = mix_backward(
        queries, keys, values, grad_mixed, log_forget, gain, doc, scores, probs, paired
    )
    grad_z = grad_log * jax.nn.sigmoid(-z_total) / 8.0
    grad_bias = jnp.sum(jnp.sum(grad_z, axis=0).reshape(2, SLOTS), axis=0)
    grad_z = grad_z.reshape(2 * positions, 2, 2, SLOTS // 2).transpose(2, 1, 0, 3)
    tokens = (2, 4 * positions, -1)
    grad_pre = jnp.concatenate([
        (grad_queries * slope(query_pre)).astype(BF16).reshape(tokens),
        (grad_keys * slope(key_pre)).astype(BF16).reshape(tokens),
        grad_values.astype(BF16).reshape(tokens),
        grad_z.astype(BF16).reshape(tokens),
    ], axis=-1)
    grad_mixer_w = jnp.einsum("td,ctf->cdf", normed, grad_pre, preferred_element_type=F32)
    grad_mixer_w = sum_over(grad_mixer_w.reshape(2 * features, -1), ("c", "z"))
    grad_normed = jnp.einsum("ctf,cdf->td", grad_pre, mixer_w, preferred_element_type=F32).astype(BF16)
    grad_normed = exchange(grad_normed.reshape(4, positions, features), 8, True)
    grad_normed = jnp.sum(grad_normed.astype(F32), axis=0)
    x_here = x_here.astype(F32)
    ratio_a = scaled(x_here)
    grad_gain_attn = jnp.sum(grad_normed * x_here * ratio_a, axis=0)
    grad_input = grad_attended + norm_back(grad_normed, gain_attn, x_here, ratio_a)

    bias_all = lax.dynamic_update_slice_in_dim(jnp.zeros((HEADS * SLOTS,), F32), grad_bias, head * SLOTS, 0)
    small = lax.psum(jnp.concatenate([grad_gain_attn, grad_gain_ffn, bias_all]), ("z", "y", "x", "c"))
    block = z * 4 + head
    grad_gain_attn = lax.dynamic_slice_in_dim(small, block * rows_here, rows_here)
    grad_gain_ffn = lax.dynamic_slice_in_dim(small, features + block * rows_here, rows_here)
    grad_bias = lax.dynamic_slice_in_dim(small, 2 * features + block * bias_here, bias_here)

    def to_rows(a):
        a = lax.all_to_all(a.reshape(4, rows_here, -1), PLANE, split_axis=0, concat_axis=0, tiled=True)
        return lax.all_gather(a, "c", axis=0)

    grad_mixer_w = to_rows(grad_mixer_w).transpose(2, 1, 0, 3)
    grad_w = [
        grad_mixer_w[..., i * depth // 2:(i + 1) * depth // 2].reshape(rows_here, features).astype(F32) for i in range(3)
    ]
    grad_forget_w = grad_mixer_w[..., 3 * depth // 2:].reshape(rows_here, HEADS * SLOTS).astype(F32)

    def from_hidden(a):
        a = to_rows(a).reshape(2, 4, rows_here, planes, hidden_here // 2)
        return a.transpose(2, 3, 1, 0, 4).reshape(rows_here, -1).astype(F32)

    def both_halves(a):
        return lax.all_gather(a, "c", axis=0, tiled=True).astype(F32)

    return (
        output.reshape(inputs.shape), grad_input.reshape(inputs.shape), grad_gain_attn, grad_w[0], grad_w[1], grad_w[2],
        grad_forget_w, grad_bias, both_halves(grad_out_w), grad_gain_ffn, from_hidden(grad_gate_w),
        from_hidden(grad_up_w), both_halves(grad_down_w),
    )


def solution(mesh):
    planes = mesh.shape["dp"] // 4
    fine = Mesh(mesh.devices.reshape(planes, 2, 2, 2), ("z", "y", "x", "c"))
    dp = ("z", "y", "x")
    tokens, vector, matrix = P(dp, "c", None), P(dp), P(dp, None)
    in_specs = (
        tokens, P(dp, "c"), vector, matrix, matrix, matrix, matrix, vector, matrix, vector, matrix, matrix, matrix, tokens
    )
    out_specs = (
        tokens, tokens, vector, matrix, matrix, matrix, matrix, vector, matrix, vector, matrix, matrix, matrix
    )
    return jax.shard_map(body, mesh=fine, in_specs=in_specs, out_specs=out_specs, check_vma=False)
```

time: 6350 us -> 1140 us (0.18)
  waiting for transfers between devices: 5030 us -> 253 us
  Pallas kernels: 0 us -> 406 us
  matrix products: 459 us -> 147 us
  other arithmetic: 362 us -> 51 us
  local copies, waits for them, and re-layouts: 232 us -> 88.2 us
    reduce_scatter x8 -> x5, waiting for transfers between devices: 4190 us -> 219 us  [sum_over(): lax.psum_scatter(a.astype(BF16), axes, scatter_dimension=0, tiled=True)]
    all_gather x10 -> x9, waiting for transfers between devices: 830 us -> 32.9 us  [the longest x1 32.9 us: body(): lax.all_gather(down_half, ('c', 'z'), axis=0, tiled=True)]
    pallas_call x0 -> x10, Pallas kernels: none -> 406 us  [the longest x8 370 us: exchange(): pl.pallas_call(functools.partial(exchange_kernel, to_homes, same), name='...]
    dot_general x136 -> x15, matrix products: 459 us -> 147 us  [the longest x1 15.9 us: body(): jnp.einsum('td,cfd->ctf', cot, full_down, preferred_element_type=F32)]
    while x16 -> x0, other arithmetic: 165 us -> none
    all_gather x6 -> x1, blocking collectives: 95.7 us -> 2.38 us  [both_halves(): return lax.all_gather(a, 'c', axis=0, tiled=True).astype(F32)]
    all_to_all x0 -> x6, blocking collectives: none -> 87.9 us  [the longest x3 47.4 us: to_rows(): lax.all_to_all(a.reshape(4, rows_here, -1), PLANE, split_axis=0, concat_a...]
    unnamed x2 -> x1, blocking collectives: 123 us -> 43 us
  transfers between devices with their start and end apart: 19 -> 14, of which waited for: 13 -> 4; matrix products, arithmetic and copies ran while one was open for 7% -> 23% of each run, Pallas kernels for 0% -> 36%
where the time goes in v1:
time: 1140 us
  Pallas kernels  406 us (36%)
  waiting for transfers between devices  253 us (22%)
  blocking collectives  176 us (15%)
  matrix products  147 us (13%)
  local copies, waits for them, and re-layouts  88.2 us (8%)
  other arithmetic  51 us (4%)
  between operations  15.5 us (1%)
    pallas_call x8, Pallas kernels, exchange(): pl.pallas_call(functools.partial(exchange_kernel, to_homes, same), name='...  370 us
    reduce_scatter x5, waiting for transfers between devices, sum_over(): lax.psum_scatter(a.astype(BF16), axes, scatter_dimension=0, tiled=True)  219 us
    all_to_all x3, blocking collectives, to_rows(): lax.all_to_all(a.reshape(4, rows_here, -1), PLANE, split_axis=0, concat_a...  47.4 us
    unnamed x1, blocking collectives  43 us
    psum x1, blocking collectives, body(): lax.psum(jnp.concatenate([grad_gain_attn, grad_gain_ffn, bias_all]), ('z'...  42.7 us
    all_to_all x3, blocking collectives, share(): mine = lax.all_to_all(a, PLANE, split_axis=0, concat_axis=0, tiled=True)  40.5 us
    unnamed x125, local copies, waits for them, and re-layouts  38.4 us
    all_gather x1, waiting for transfers between devices, body(): lax.all_gather(down_half, ('c', 'z'), axis=0, tiled=True)  32.9 us
  transfers between devices with their start and end apart: 14, of which 4 were waited for; matrix products, arithmetic and copies ran while one was open for 23% of the time, Pallas kernels for 36%

profile of v1, /device:TPU:0, one launch (start us, length us, event | category | flops | bytes accessed | tf_op | source)
XLA Modules:
  0.0 1137.6 jit_solution(16888744446564808204)
XLA Ops:
  12.9 17.0 %all_to_all.30 = bf16[4,128,800]{1,2,0:T(8,128)(2,1)S(1)} all-to-all(bf16[4,128,800]{1,2,0:T(8,128)(2,1)S(1)} %copy.136), channel_id=1, replica_groups=mesh['z'=4,'y'=2,'x'=2,'c'=2] {'y','x'}, dimensions={0} | all-to-all | bytes 1638400 | tf_op jit(solution)/shard_map/all_to_all | solution.py:416
  38.3 12.3 %all_to_all.31 = bf16[4,128,704]{1,2,0:T(8,128)(2,1)S(1)} all-to-all(bf16[4,128,704]{1,2,0:T(8,128)(2,1)S(1)} %bitcast.305), channel_id=1, replica_groups=mesh['z'=4,'y'=2,'x'=2,'c'=2] {'y','x'}, dimensions={0} | all-to-all | bytes 1441792 | tf_op jit(solution)/shard_map/all_to_all | solution.py:416
  51.7 11.2 all_to_all.32
  65.3 43.0 %all-reduce = bf16[16896]{0:T(1024)(128)(2,1)S(1)} all-reduce(bf16[16896]{0:T(1024)(128)(2,1)S(1)} %dynamic-update-slice), channel_id=2, replica_groups=mesh['z'=4,'y'=2,'x'=2,'c'=2] {'z','y','x','c'}, use_global_device_ids=true, to_apply=%add | all-reduce | flops 16896 | bytes 67584
  108.6 55.1 %from_homes.4 = bf16[4,256,2048]{2,1,0:T(8,128)(2,1)} custom-call(bf16[256,2048]{1,0:T(8,128)(2,1)} %bitcast.271), custom_call_target="tpu_custom_call" | custom-call | tf_op jit(solution)/shard_map/from_homes/pallas_call | solution.py:404
  163.7 3.1 multiply_reduce_fusion
  168.4 64.3 %from_homes.6 = bf16[4,256,2048]{2,1,0:T(8,128)(2,1)} custom-call(bf16[256,2048]{1,0:T(8,128)(2,1)} %bitcast.284), custom_call_target="tpu_custom_call" | custom-call | tf_op jit(solution)/shard_map/from_homes/pallas_call | solution.py:404
  232.7 5.2 multiply_convert_fusion
  237.9 10.4 fusion.40
  252.2 4.1 fusion.71
  266.4 12.3 %mix_forward.1 = (bf16[2,2,2,256,256]{4,3,2,1,0:T(8,128)(2,1)S(1)}, f32[512,128]{1,0:T(8,128)S(1)}, f32[512,128]{1,0:T(8,128)S(1)}, f32[2,512,512]{2,1,0:T(8,128)S(1)}) custom-call(bf16[2,2,512,256]{3,2,1,0:T(8,128)(2,1)S(1)} %multiply_convert_fusion.6.q_ref, bf16[2,2,512,256]{3,2,1,0:T(8,128)(2,1)S(1)} %multiply_convert_fusion.5.k_ref, ...), custom_call_target="tpu_custom_call" | custom-call | tf_op jit(solution)/shard_map/mix_forward/pallas_call | solution.py:305
  282.4 15.6 %to_homes.4 = bf16[4,512,256]{2,1,0:T(8,128)(2,1)} custom-call(bf16[4,512,256]{2,1,0:T(8,128)(2,1)} %bitcast.267), custom_call_target="tpu_custom_call" | custom-call | tf_op jit(solution)/shard_map/to_homes/pallas_call | solution.py:404
  299.6 6.4 multiply_reduce_fusion.3
  307.2 48.6 %from_homes.5 = bf16[4,256,2048]{2,1,0:T(8,128)(2,1)} custom-call(bf16[256,2048]{1,0:T(8,128)(2,1)} %multiply_convert_fusion.4.a_ref), custom_call_target="tpu_custom_call" | custom-call | tf_op jit(solution)/shard_map/from_homes/pallas_call | solution.py:404
  355.9 11.4 %fusion.19 = f32[2,704,1024]{2,1,0:T(8,128)} fusion(bf16[1024,2048,1]{1,0,2:T(8,128)(2,1)} %bitcast.287, bf16[88,2,8,2048]{3,2,1,0:T(8,128)(2,1)} %bitcast.337), kind=kOutput, calls=%fused_computation.31 | convolution fusion | flops 5905580032 | bytes 15728640 | tf_op jit(solution)/shard_map/td,cdf->ctf/dot_general | solution.py:504
  367.3 14.0 %multiply_convert_fusion.1 = (bf16[2,704,1024]{2,1,0:T(8,128)(2,1)S(1)}, f32[2,704,1024]{2,1,0:T(8,128)}) fusion(f32[2,704,1024]{2,1,0:T(8,128)} %fusion.19, bf16[1024,2048,1]{1,0,2:T(8,128)(2,1)} %bitcast.288, bf16[88,2,8,2048]{3,2,1,0:T(8,128)(2,1)} %bitcast.339), kind=kOutput, calls=%fused_computation.48 | convolution fusion | flops 5914230784 | bytes 24379392 | tf_op jit(solution)/shard_map/td,cdf->ctf/dot_general | solution.py:505
  381.3 8.3 convolution_convert_fusion
  389.7 32.9 %all-gather.26.cloned.1.call-done = bf16[1,1408,2048]{2,1,0:T(8,128)(2,1)} async-done(((bf16[1,176,2048]{2,1,0:T(8,128)(2,1)}), bf16[1,1408,2048]{2,1,0:T(8,128)(2,1)}) %all-gather.26.cloned.1.call-update) | async-done | bytes 5767184 | tf_op jit(solution)/shard_map/all_gather | solution.py:477
  422.5 15.9 %fusion.22 = (bf16[2,1024,704]{1,2,0:T(8,128)(2,1)S(1)}, bf16[2,1024,704]{1,2,0:T(8,128)(2,1)}) fusion(f32[2,704,1024]{2,1,0:T(8,128)} %get-tuple-element.94, f32[2,704,1024]{2,1,0:T(8,128)} %fusion.19, bf16[2,704,2048]{2,1,0:T(8,128)(2,1)} %bitcast.341, bf16[1024,2048,1]{1,0,2:T(8,128)(2,1)} %bitcast.285), kind=kOutput, calls=%fused_computation.36 | convolution fusion | flops 5924323328 | bytes 27262976 | tf_op jit(solution)/shard_map/td,cfd->ctf/dot_general | solution.py:508
  438.4 6.4 convert_bitcast_fusion.2
  447.9 9.3 convert_bitcast_fusion.1
  460.3 5.4 fusion.1
  465.7 13.1 %bitcast_convert_fusion.1 = bf16[1024,2048]{1,0:T(8,128)(2,1)} fusion(bf16[2,704,2048]{2,1,0:T(8,128)(2,1)} %bitcast.342, f32[2,704,1024]{2,1,0:T(8,128)} %get-tuple-element.94, f32[2,704,1024]{2,1,0:T(8,128)} %fusion.19), kind=kOutput, calls=%fused_computation.6 | convolution fusion | flops 5916327936 | bytes 21495808 | tf_op jit(solution)/shard_map/ctf,cfd->td/dot_general | solution.py:523
  478.9 48.2 %to_homes.5 = bf16[4,256,2048]{2,1,0:T(8,128)(2,1)} custom-call(bf16[4,256,2048]{2,1,0:T(8,128)(2,1)} %bitcast.296), custom_call_target="tpu_custom_call" | custom-call | tf_op jit(solution)/shard_map/to_homes/pallas_call | solution.py:404
  527.1 9.8 fusion.13
  536.9 11.2 fusion.2
  548.2 48.5 %to_homes.6 = bf16[4,256,2048]{2,1,0:T(8,128)(2,1)} custom-call(bf16[4,256,2048]{2,1,0:T(8,128)(2,1)} %bitcast.297), custom_call_target="tpu_custom_call" | custom-call | tf_op jit(solution)/shard_map/to_homes/pallas_call | solution.py:404
  596.7 3.3 convert_reduce_fusion.1
  606.8 3.3 fusion.45
  615.3 15.1 %from_homes.7 = bf16[4,512,256]{2,1,0:T(8,128)(2,1)} custom-call(bf16[4,512,256]{2,1,0:T(8,128)(2,1)} %bitcast.299), custom_call_target="tpu_custom_call" | custom-call | tf_op jit(solution)/shard_map/from_homes/pallas_call | solution.py:404
  635.6 24.1 %mix_backward.1 = (f32[2,2,512,256]{3,2,1,0:T(8,128)}, f32[2,2,512,256]{3,2,1,0:T(8,128)}, f32[2,2,512,256]{3,2,1,0:T(8,128)}, f32[512,128]{1,0:T(8,128)S(1)}) custom-call(bf16[2,2,512,256]{3,2,1,0:T(8,128)(2,1)S(1)} %copy-done.5, bf16[2,2,512,256]{3,2,1,0:T(8,128)(2,1)S(1)} %copy-done.3, bf16[2,2,512,256]{3,2,1,0:T(8,128)(2,1)S(1)} %bitcast.265, ...), custom_call_target="tpu_custom_call" | custom-call | tf_op jit(solution)/shard_map/mix_backward/pallas_call | solution.py:324
  671.2 9.7 convert_bitcast_fusion
  680.9 3.3 copy.193
  686.1 16.4 %all_to_all.33 = bf16[4,128,704]{1,2,0:T(8,128)(2,1)} all-to-all(bf16[4,128,704]{1,2,0:T(8,128)(2,1)S(1)} %copy_bitcast_fusion.5), channel_id=1, replica_groups=mesh['z'=4,'y'=2,'x'=2,'c'=2] {'y','x'}, dimensions={0} | all-to-all | bytes 1441792 | tf_op jit(solution)/shard_map/all_to_all | solution.py:567
  702.6 80.6 %reduce-scatter.12.cloned.1.call-done = bf16[512,704]{0,1:T(8,128)(2,1)} async-done(((bf16[4096,704]{0,1:T(8,128)(2,1)}), bf16[512,704]{0,1:T(8,128)(2,1)}) %reduce-scatter.12.cloned.1.call-update) | async-done | bytes 720912 | tf_op jit(solution)/shard_map/reduce_scatter | solution.py:422
  784.5 15.1 %all_to_all.34 = bf16[4,128,704]{1,2,0:T(8,128)(2,1)} all-to-all(bf16[4,128,704]{1,2,0:T(8,128)(2,1)S(1)} %copy_bitcast_fusion.4), channel_id=1, replica_groups=mesh['z'=4,'y'=2,'x'=2,'c'=2] {'y','x'}, dimensions={0} | all-to-all | bytes 1441792 | tf_op jit(solution)/shard_map/all_to_all | solution.py:567
  799.6 119.1 %reduce-scatter.6.cloned.1.call-done = bf16[512,800]{0,1:T(8,128)(2,1)} async-done(((bf16[4096,800]{0,1:T(8,128)(2,1)}), bf16[512,800]{0,1:T(8,128)(2,1)}) %reduce-scatter.6.cloned.1.call-update) | async-done | bytes 819216 | tf_op jit(solution)/shard_map/reduce_scatter | solution.py:422
  920.0 15.9 %all_to_all.35 = bf16[4,128,800]{1,2,0:T(8,128)(2,1)} all-to-all(bf16[4,128,800]{1,2,0:T(8,128)(2,1)S(1)} %copy_bitcast_fusion.1), channel_id=1, replica_groups=mesh['z'=4,'y'=2,'x'=2,'c'=2] {'y','x'}, dimensions={0} | all-to-all | bytes 1638400 | tf_op jit(solution)/shard_map/all_to_all | solution.py:567
  936.2 5.7 convolution_convert_fusion.1
  943.5 12.4 %bitcast_convert_fusion = bf16[1024,2048]{1,0:T(8,128)(2,1)} fusion(bf16[100,2,8,2048]{3,2,1,0:T(8,128)(2,1)} %bitcast.336, bf16[2,1024,32]{1,2,0:T(8,128)(2,1)S(1)} %bitcast.332, bf16[2,1024,256]{1,2,0:T(8,128)(2,1)} %copy.162, bf16[2,1024,256]{1,2,0:T(8,128)(2,1)} %copy.161, bf16[2,1024,256]{1,2,0:T(8,128)(2,1)} %copy.160), kind=kOutput, calls=%fused_computation.3 | convolution fusion | flops 6726090752 | bytes 14024704 | tf_op jit(solution)/shard_map/ctf,cdf->td/dot_general | solution.py:551
  955.9 74.3 %to_homes.7 = bf16[4,256,2048]{2,1,0:T(8,128)(2,1)} custom-call(bf16[4,256,2048]{2,1,0:T(8,128)(2,1)} %bitcast.295), custom_call_target="tpu_custom_call" | custom-call | tf_op jit(solution)/shard_map/to_homes/pallas_call | solution.py:404
  1030.5 3.3 convert_reduce_fusion
  1036.0 42.7 %psum.7 = f32[4352]{0:T(1024)S(1)} all-reduce(f32[4352]{0:T(1024)S(1)} %pad_maximum_fusion.4), channel_id=1, replica_groups=mesh['z'=4,'y'=2,'x'=2,'c'=2] {'z','y','x','c'}, use_global_device_ids=true, to_apply=%region_14.15 | all-reduce | flops 4352 | bytes 34816 | tf_op jit(solution)/shard_map/psum | solution.py:560
  1079.9 3.5 fusion.54
  1083.4 3.3 convert_element_type.289
  1090.2 3.4 copy.180
  1097.0 3.4 copy.181
  1107.8 19.3 %reduce-scatter.8.cloned.1.call-done = bf16[64,2048]{1,0:T(8,128)(2,1)} async-done(((bf16[2048,2048]{1,0:T(8,128)(2,1)}), bf16[64,2048]{1,0:T(8,128)(2,1)}) %reduce-scatter.8.cloned.1.call-update) | async-done | bytes 262160 | tf_op jit(solution)/shard_map/reduce_scatter | solution.py:422
  (253 shorter events, 102.0 us)
Async XLA Ops:
  7.2 56.8 %copy-start = (bf16[352,2048]{1,0:T(8,128)(2,1)S(1)}, bf16[352,2048]{1,0:T(8,128)(2,1)}, u32[]{:S(2)}) copy-start(bf16[352,2048]{1,0:T(8,128)(2,1)} %param.26) | copy-start | bytes 4325380
  7.2 4.7 copy-start.44
  7.2 230.7 %all-gather.16.cloned.1.call-start = ((), (), s32[]{:S(2)}) async-start(), calls=%async_computation.11 | async-start | bytes 7372800 | tf_op jit(solution)/shard_map/all_gather | solution.py:418
  12.9 18.1 %copy-start.43 = (bf16[128,2048]{1,0:T(8,128)(2,1)S(1)}, bf16[128,2048]{1,0:T(8,128)(2,1)}, u32[]{:S(2)}) copy-start(bf16[128,2048]{1,0:T(8,128)(2,1)} %param.22) | copy-start | bytes 1572868
  30.9 268.7 %all-gather.24.cloned.1.call-start = ((), (), s32[]{:S(2)}) async-start(), calls=%async_computation.20 | async-start | bytes 8650752 | tf_op jit(solution)/shard_map/all_gather | solution.py:479
  31.7 324.2 %all-gather.18.cloned.1.call-start = ((), (), s32[]{:S(2)}) async-start(), calls=%async_computation.12 | async-start | bytes 6488064 | tf_op jit(solution)/shard_map/all_gather | solution.py:418
  38.3 13.4 %copy-start.39 = (bf16[4,128,4,176]{1,3,0,2:T(8,128)(2,1)S(1)}, bf16[4,128,4,176]{1,3,0,2:T(8,128)(2,1)}, u32[]{:S(2)}) copy-start(bf16[4,128,4,176]{1,3,0,2:T(8,128)(2,1)} %get-tuple-element.95) | copy-start | bytes 2162692
  51.6 315.7 %all-gather.20.cloned.1.call-start = ((), (), s32[]{:S(2)}) async-start(), calls=%async_computation.13 | async-start | bytes 6488064 | tf_op jit(solution)/shard_map/all_gather | solution.py:418
  51.6 13.3 %copy-start.50 = (s32[1,256]{1,0:T(1,128)S(1)}, s32[1,256]{1,0:T(1,128)}, u32[]{:S(2)}) copy-start(s32[1,256]{1,0:T(1,128)} %param.15) | copy-start | bytes 3076
  51.6 13.3 %copy-start.47 = (bf16[16]{0:T(256)(128)(2,1)S(1)}, bf16[16]{0:T(256)(128)(2,1)}, u32[]{:S(2)}) copy-start(bf16[16]{0:T(256)(128)(2,1)} %param.21) | copy-start | bytes 100
  51.7 13.3 %copy-start.48 = (bf16[128]{0:T(256)(128)(2,1)S(1)}, bf16[128]{0:T(256)(128)(2,1)}, u32[]{:S(2)}) copy-start(bf16[128]{0:T(256)(128)(2,1)} %param.23) | copy-start | bytes 772
  51.7 13.3 %copy-start.49 = (bf16[128]{0:T(256)(128)(2,1)S(1)}, bf16[128]{0:T(256)(128)(2,1)}, u32[]{:S(2)}) copy-start(bf16[128]{0:T(256)(128)(2,1)} %param.16) | copy-start | bytes 772
  63.9 358.6 %all-gather.26.cloned.1.call-start = ((), (), s32[]{:S(2)}) async-start(), calls=%async_computation.21 | async-start | bytes 6488064 | tf_op jit(solution)/shard_map/all_gather | solution.py:477
  64.9 619.3 %reduce-scatter.14.cloned.1.call-start = ((), (), s32[]{:S(2)}) async-start(), calls=%async_computation.18 | async-start | bytes 6488064 | tf_op jit(solution)/shard_map/reduce_scatter | solution.py:422
  167.0 95.5 %copy-start.45 = (f32[128]{0:T(128)}, f32[128]{0:T(128)S(1)}, u32[]{:S(2)}) copy-start(f32[128]{0:T(128)S(1)} %add.156) | copy-start | bytes 1540
  168.1 98.3 %copy-start.23 = (f32[2,4,128]{2,1,0:T(4,128)}, f32[2,4,128]{2,1,0:T(4,128)S(1)}, u32[]{:S(2)}) copy-start(f32[2,4,128]{2,1,0:T(4,128)S(1)} %broadcast_add_fusion) | copy-start | bytes 12292
  168.4 97.9 %copy-start.8 = (f32[2,512,1]{2,1,0:T(8,128)}, f32[2,512,1]{2,1,0:T(8,128)S(1)}, u32[]{:S(2)}) copy-start(f32[2,512,1]{2,1,0:T(8,128)S(1)} %reduce_window_sum.34.dcol_ref) | copy-start | bytes 12292
  252.2 10.4 copy-start.40
  262.9 15.8 %copy-start.11 = (f32[512,128]{1,0:T(8,128)}, f32[512,128]{1,0:T(8,128)S(1)}, u32[]{:S(2)}) copy-start(f32[512,128]{1,0:T(8,128)S(1)} %get-tuple-element.74.gain_ref) | copy-start | bytes 786436
  262.9 15.8 %copy-start.13 = (f32[512,128]{1,0:T(8,128)}, f32[512,128]{1,0:T(8,128)S(1)}, u32[]{:S(2)}) copy-start(f32[512,128]{1,0:T(8,128)S(1)} %get-tuple-element.75.lf_ref) | copy-start | bytes 786436
  265.8 12.9 %copy-start.2 = (bf16[2,2,512,256]{3,2,1,0:T(8,128)(2,1)}, bf16[2,2,512,256]{3,2,1,0:T(8,128)(2,1)S(1)}, u32[]{:S(2)}) copy-start(bf16[2,2,512,256]{3,2,1,0:T(8,128)(2,1)S(1)} %multiply_convert_fusion.5.k_ref) | copy-start | bytes 3145732
  266.4 16.0 %copy-start.4 = (bf16[2,2,512,256]{3,2,1,0:T(8,128)(2,1)}, bf16[2,2,512,256]{3,2,1,0:T(8,128)(2,1)S(1)}, u32[]{:S(2)}) copy-start(bf16[2,2,512,256]{3,2,1,0:T(8,128)(2,1)S(1)} %multiply_convert_fusion.6.q_ref) | copy-start | bytes 3145732
  299.5 6.5 copy-start.33
  367.3 14.0 %copy-start.37 = (bf16[4,256,2048]{2,1,0:T(8,128)(2,1)S(1)}, bf16[4,256,2048]{2,1,0:T(8,128)(2,1)}, u32[]{:S(2)}) copy-start(bf16[4,256,2048]{2,1,0:T(8,128)(2,1)} %from_homes.6) | copy-start | bytes 12582916
  389.6 295.2 %reduce-scatter.10.cloned.1.call-start = ((), (), s32[]{:S(2)}) async-start(), calls=%async_computation.16 | async-start | bytes 6488064 | tf_op jit(solution)/shard_map/reduce_scatter | solution.py:422
  422.5 15.9 %copy-start.38 = (bf16[4,256,2048]{2,1,0:T(8,128)(2,1)S(1)}, bf16[4,256,2048]{2,1,0:T(8,128)(2,1)}, u32[]{:S(2)}) copy-start(bf16[4,256,2048]{2,1,0:T(8,128)(2,1)} %from_homes.5) | copy-start | bytes 12582916
  438.4 6.4 copy-start.51
  447.8 335.4 %reduce-scatter.12.cloned.1.call-start = ((), (), s32[]{:S(2)}) async-start(), calls=%async_computation.17 | async-start | bytes 6488064 | tf_op jit(solution)/shard_map/reduce_scatter | solution.py:422
  460.3 458.4 %reduce-scatter.6.cloned.1.call-start = ((), (), s32[]{:S(2)}) async-start(), calls=%async_computation.14 | async-start | bytes 7372800 | tf_op jit(solution)/shard_map/reduce_scatter | solution.py:422
  527.1 9.9 copy-start.52
  602.2 3.9 slice-start
  610.1 20.3 %copy-start.3 = (bf16[2,2,512,256]{3,2,1,0:T(8,128)(2,1)S(1)}, bf16[2,2,512,256]{3,2,1,0:T(8,128)(2,1)}, u32[]{:S(2)}) copy-start(bf16[2,2,512,256]{3,2,1,0:T(8,128)(2,1)} %copy-done.2) | copy-start | bytes 3145732
  610.1 20.3 %copy-start.5 = (bf16[2,2,512,256]{3,2,1,0:T(8,128)(2,1)S(1)}, bf16[2,2,512,256]{3,2,1,0:T(8,128)(2,1)}, u32[]{:S(2)}) copy-start(bf16[2,2,512,256]{3,2,1,0:T(8,128)(2,1)} %copy-done.4) | copy-start | bytes 3145732
  610.1 20.3 %copy-start.7 = (bf16[2,1024,256]{2,1,0:T(8,128)(2,1)S(1)}, bf16[2,1024,256]{2,1,0:T(8,128)(2,1)}, u32[]{:S(2)}) copy-start(bf16[2,1024,256]{2,1,0:T(8,128)(2,1)} %copy-done.6) | copy-start | bytes 3145732
  610.1 20.4 %copy-start.12 = (f32[512,128]{1,0:T(8,128)S(1)}, f32[512,128]{1,0:T(8,128)}, u32[]{:S(2)}) copy-start(f32[512,128]{1,0:T(8,128)} %copy-done.11) | copy-start | bytes 786436
  610.1 20.4 %copy-start.24 = (f32[2,4,128]{2,1,0:T(4,128)S(1)}, f32[2,4,128]{2,1,0:T(4,128)}, u32[]{:S(2)}) copy-start(f32[2,4,128]{2,1,0:T(4,128)} %copy-done.23) | copy-start | bytes 12292
  635.6 24.8 %copy-start.31 = (f32[2,1024,256]{2,1,0:T(8,128)S(1)}, f32[2,1024,256]{2,1,0:T(8,128)}, u32[]{:S(2)}) copy-start(f32[2,1024,256]{2,1,0:T(8,128)} %copy.139) | copy-start | bytes 6291460
  666.4 4.5 copy-start.22
  666.4 4.4 copy-start.41
  666.4 4.4 copy-start.46
  684.2 399.2 %all-gather.22.cloned.1.call-start = ((), (), s32[]{:S(2)}) async-start(), calls=%async_computation.19 | async-start | bytes 2162688 | tf_op jit(solution)/shard_map/all_gather | solution.py:581
  684.8 401.9 %all-gather.30.cloned.1.call-start = ((), (), s32[]{:S(2)}) async-start(), calls=%async_computation.23 | async-start | bytes 2162688 | tf_op jit(solution)/shard_map/all_gather | solution.py:568
  702.6 391.0 %all-gather.32.cloned.1.call-start = ((), (), s32[]{:S(2)}) async-start(), calls=%async_computation.24 | async-start | bytes 2162688 | tf_op jit(solution)/shard_map/all_gather | solution.py:568
  784.5 151.7 %copy-start.27 = (f32[256,2048]{1,0:T(8,128)S(1)}, f32[256,2048]{1,0:T(8,128)}, u32[]{:S(2)}) copy-start(f32[256,2048]{1,0:T(8,128)} %copy-done.26) | copy-start | bytes 6291460
  784.5 151.7 %copy-start.34 = (bf16[8,256,256]{1,2,0:T(8,128)(2,1)S(1)}, bf16[8,256,256]{1,2,0:T(8,128)(2,1)}, u32[]{:S(2)}) copy-start(bf16[8,256,256]{1,2,0:T(8,128)(2,1)} %copy-done.33) | copy-start | bytes 3145732
  799.6 300.8 %all-gather.28.cloned.1.call-start = ((), (), s32[]{:S(2)}) async-start(), calls=%async_computation.22 | async-start | bytes 2457600 | tf_op jit(solution)/shard_map/all_gather | solution.py:568
  935.9 191.2 %reduce-scatter.8.cloned.1.call-start = ((), (), s32[]{:S(2)}) async-start(), calls=%async_computation.15 | async-start | bytes 8650752 | tf_op jit(solution)/shard_map/reduce_scatter | solution.py:422
  1104.8 25.7 %copy-start.1 = (bf16[352,2048]{1,0:T(8,128)(2,1)S(1)}, bf16[352,2048]{1,0:T(8,128)(2,1)}, u32[]{:S(2)}) copy-start(bf16[352,2048]{1,0:T(8,128)(2,1)} %param.26) | copy-start | bytes 4325380
  (21 other events, 38.4 us)
Sparse Core Ops, SparseCore 0:
  31.0 67.1 all-gather.15
  101.1 137.8 all-gather.23
  241.1 58.9 all-gather.17
  302.2 59.0 all-gather.19
  363.3 59.1 all-gather.25
  424.7 116.8 reduce-scatter.13
  543.9 118.4 reduce-scatter.9
  664.7 118.4 reduce-scatter.11
  785.6 133.1 reduce-scatter.5
  920.1 10.1 all-gather.21
  931.8 10.7 all-gather.29
  944.0 10.7 all-gather.31
  956.4 11.0 all-gather.27
  969.6 157.4 reduce-scatter.7

commit v2 on v1

v2 whole, which is shorter than its diff:
```python
import functools

import jax
import jax.numpy as jnp
from jax import lax
from jax.sharding import Mesh
from jax.sharding import PartitionSpec as P
from jax.experimental import pallas as pl
from jax.experimental.pallas import tpu as pltpu

HEADS = 4
SLOTS = 64
DEPTH = 512
TILE = 128
EPSILON = 1e-06
F32, BF16 = jnp.float32, jnp.bfloat16
NN = (((1,), (0,)), ((), ()))
NT = (((1,), (1,)), ((), ()))
TN = (((0,), (0,)), ((), ()))
HALVES = (64, 32, 16, 8, 4, 2, 1)


def dot(a, b, dims):
    return lax.dot_general(a, b, dims, preferred_element_type=F32)


def parts_of(a):
    high = a.astype(BF16)
    return high, (a - high.astype(F32)).astype(BF16)


def dot_parts(a, b, dims):
    return dot(a[0], b[0], dims) + (dot(a[1], b[0], dims) + dot(a[0], b[1], dims))


def dot_ones(ones, a):
    high = a.astype(BF16)
    rest = a - high.astype(F32)
    middle = rest.astype(BF16)
    low = (rest - middle.astype(F32)).astype(BF16)
    return dot(ones, high, NN) + (dot(ones, middle, NN) + dot(ones, low, NN))


def places():
    shape = (TILE, TILE)
    return lax.broadcasted_iota(jnp.int32, shape, 0), lax.broadcasted_iota(jnp.int32, shape, 1)


def ones_where(mask):
    return jnp.where(mask, 1.0, 0.0).astype(BF16)


def steps_to_middle(half):
    t, s = places()
    block = 2 * half
    same = (t // block) == (s // block)
    t_right, s_right = (t % block) >= half, (s % block) >= half
    right = t_right & s_right & (s <= t)
    left = jnp.logical_not(t_right | s_right) & (s > t)
    return ones_where(same & (right | left))


def pair_mask(half, turned=False):
    t, s = places()
    if turned:
        t, s = s, t
    block = 2 * half
    return ((t // block) == (s // block)) & ((t % block) >= half) & ((s % block) < half)


def first_row(rows):
    return lax.broadcasted_iota(jnp.int32, (rows, 2 * SLOTS), 1) < SLOTS


def row_sums(a, first):
    return (
        jnp.sum(jnp.where(first, a, 0.0), axis=1, keepdims=True),
        jnp.sum(jnp.where(first, 0.0, a), axis=1, keepdims=True),
    )


def tile_rows(j):
    return pl.ds(pl.multiple_of(j * TILE, TILE), TILE)


def prepare(lf_ref, decay_ref, reach_ref, e_ref, tiles):
    t, s = places()

    @pl.loop(0, tiles)
    def _(j):
        rows = tile_rows(j)
        lf = lf_ref[rows, :]
        decay_ref[rows, :] = dot_ones(ones_where(s <= t), lf)
        reach_ref[rows, :] = dot_ones(ones_where(s > t), lf)
        for level, half in enumerate(HALVES):
            e_ref[level, rows, :] = jnp.exp(dot_ones(steps_to_middle(half), lf))


def far_pairs(tiles):
    out, half = [], tiles // 2
    while half >= 1:
        for start in range(0, tiles, 2 * half):
            out.append((start + half, start, half))
        half //= 2
    return out


def far_decays(right, left, half, decay_ref, reach_ref):
    after, total = [], None
    for j in range(right, right + half):
        part = decay_ref[j * TILE:(j + 1) * TILE, :]
        after.append(jnp.exp(part if total is None else part + total))
        last = part[TILE - 1:TILE, :]
        total = last if total is None else total + last
    before, total = [], None
    for j in range(left + half - 1, left - 1, -1):
        part = reach_ref[j * TILE:(j + 1) * TILE, :]
        before.append(jnp.exp(part if total is None else part + total))
        whole = decay_ref[(j + 1) * TILE - 1:(j + 1) * TILE, :]
        total = whole if total is None else total + whole
    if half == 1:
        return after[0], before[0]
    return jnp.concatenate(after, axis=0), jnp.concatenate(before[::-1], axis=0)


def diagonal_of(block):
    t, s = places()
    return jnp.sum(jnp.where(t == s, block, 0.0), axis=1, keepdims=True)


def weighted_sums(a_ref, out_ref, gain_ref, decay_ref, reach_ref, e_ref, tiles):
    first = first_row(TILE)

    @pl.loop(0, tiles)
    def _(j):
        rows = tile_rows(j)
        gain = gain_ref[rows, :]
        blocks = [a_ref[r, rows, rows] for r in range(2)]
        total = jnp.where(first, diagonal_of(blocks[0]), diagonal_of(blocks[1])) * gain
        for level, half in enumerate(HALVES):
            e = e_ref[level, rows, :]
            x = parts_of(e * gain)
            pairs = pair_mask(half)
            y = [dot_parts(parts_of(jnp.where(pairs, a, 0.0)), x, NN) for a in blocks]
            total = total + e * jnp.where(first, y[0], y[1])
        out_ref[rows, :] = total

    for right, left, half in far_pairs(tiles):
        after, before = far_decays(right, left, half, decay_ref, reach_ref)
        here = slice(right * TILE, (right + half) * TILE)
        there = slice(left * TILE, (left + half) * TILE)
        x = parts_of(before * gain_ref[there, :])
        y = [dot_parts(parts_of(a_ref[r, here, there]), x, NN) for r in range(2)]
        out_ref[here, :] += after * jnp.where(first_row(half * TILE), y[0], y[1])


def split_rows(a, first):
    return parts_of(jnp.where(first, a, 0.0)), parts_of(jnp.where(first, 0.0, a))


def paired_weights(p_ref, out_ref, gain_ref, decay_ref, reach_ref, e_ref, tiles):
    first = first_row(TILE)
    t, s = places()

    @pl.loop(0, tiles)
    def _(j):
        rows = tile_rows(j)
        gain, p = gain_ref[rows, :], p_ref[rows, :]
        sums = row_sums(p * gain, first)
        total = [jnp.where(t == s, sums[r], 0.0) for r in range(2)]
        for level, half in enumerate(HALVES):
            e = e_ref[level, rows, :]
            x = parts_of(e * gain)
            pairs = pair_mask(half)
            pe = split_rows(p * e, first)
            total = [total[r] + jnp.where(pairs, dot_parts(pe[r], x, NT), 0.0) for r in range(2)]
        for r in range(2):
            out_ref[r, rows, rows] = total[r]

    for right, left, half in far_pairs(tiles):
        after, before = far_decays(right, left, half, decay_ref, reach_ref)
        here = slice(right * TILE, (right + half) * TILE)
        there = slice(left * TILE, (left + half) * TILE)
        x = parts_of(before * gain_ref[there, :])
        pe = split_rows(p_ref[here, :] * after, first_row(half * TILE))
        for r in range(2):
            out_ref[r, here, there] = dot_parts(pe[r], x, NT)
            out_ref[r, there, here] = jnp.zeros((half * TILE, half * TILE), F32)


def inner(a, b, r):
    return dot(a[0][r], b[0][r], NT) + dot(a[1][r], b[1][r], NT)


def sigmoid(v):
    return 1.0 / (1.0 + jnp.exp(-v))


def projections(pre_ref, which, length, act):
    depth = DEPTH // 2
    return [
        [act(pre_ref[f, r * length:(r + 1) * length, which * depth:(which + 1) * depth]) for r in range(2)]
        for f in range(2)
    ]


def silu_low(v):
    return (v * sigmoid(v)).astype(BF16)


def low(v):
    return v.astype(BF16)


def forward_kernel(pre_ref, lf_ref, gain_ref, dcol_ref, drow_ref,
                   mixed_ref, s_ref, p_ref, b_ref, a_ref, decay_ref, reach_ref, e_ref):
    length = lf_ref.shape[0]
    tiles = length // TILE
    scale = DEPTH ** -0.5
    q, k = projections(pre_ref, 0, length, silu_low), projections(pre_ref, 1, length, silu_low)
    for r in range(2):
        same = dcol_ref[r] == drow_ref[r]
        a_ref[r] = jnp.where(same, inner(q, k, r), 0.0)
    prepare(lf_ref, decay_ref, reach_ref, e_ref, tiles)
    weighted_sums(a_ref, s_ref, gain_ref, decay_ref, reach_ref, e_ref, tiles)
    first = first_row(length)
    logits = s_ref[...] * scale
    least = -jnp.inf
    top = jnp.where(
        first,
        jnp.max(jnp.where(first, logits, least), axis=1, keepdims=True),
        jnp.max(jnp.where(first, least, logits), axis=1, keepdims=True),
    )
    grown = jnp.exp(logits - top)
    sums = row_sums(grown, first)
    p_ref[...] = grown / jnp.where(first, sums[0], sums[1])
    paired_weights(p_ref, b_ref, gain_ref, decay_ref, reach_ref, e_ref, tiles)
    v = projections(pre_ref, 2, length, low)
    for r in range(2):
        b = jnp.where(dcol_ref[r] == drow_ref[r], b_ref[r], 0.0)
        b_ref[r] = b
        high, rest = parts_of(b)
        for f in range(2):
            mixed = (dot(high, v[f][r], NN) + dot(rest, v[f][r], NN)).astype(BF16)
            for place in range(2):
                mixed_ref[r, place, f] = mixed[place * length // 2:(place + 1) * length // 2]


def to_columns(r, f):
    t, s = places()
    half = SLOTS // 2
    return ones_where((s < half) & (t == s + r * SLOTS + f * half))


def backward_kernel(pre_ref, g_ref, lf_ref, gain_ref, rate_ref, dcol_ref, drow_ref, s_ref, p_ref, b_ref,
                    out_ref, bias_ref, a_ref, at_ref, dot_ref, h_ref, back_ref, decay_ref, reach_ref, e_ref):
    length = lf_ref.shape[0]
    tiles, depth = length // TILE, DEPTH // 2
    scale = DEPTH ** -0.5
    first_all, first = first_row(length), first_row(TILE)
    t, s = places()
    q, k = projections(pre_ref, 0, length, silu_low), projections(pre_ref, 1, length, silu_low)
    v = projections(pre_ref, 2, length, low)
    grads = [[g_ref[r, :, f].reshape(length, depth) for r in range(2)] for f in range(2)]
    for r in range(2):
        same = dcol_ref[r] == drow_ref[r]
        a_ref[r] = jnp.where(same, inner(grads, v, r), 0.0)
        at_ref[0, r] = jnp.where(same, inner(k, q, r), 0.0)
        at_ref[1, r] = jnp.where(same, inner(v, grads, r), 0.0)
    prepare(lf_ref, decay_ref, reach_ref, e_ref, tiles)
    weighted_sums(a_ref, dot_ref, gain_ref, decay_ref, reach_ref, e_ref, tiles)
    p, dots = p_ref[...], dot_ref[...]
    sums = row_sums(p * dots, first_all)
    h = scale * (p * (dots - jnp.where(first_all, sums[0], sums[1])))
    h_ref[...] = h
    dot_ref[...] = h * s_ref[...] + p * dots
    paired_weights(h_ref, a_ref, gain_ref, decay_ref, reach_ref, e_ref, tiles)
    @pl.loop(0, tiles)
    def _(j):
        rows = tile_rows(j)
        h, p = h_ref[rows, :], p_ref[rows, :]
        keys = [at_ref[0, r, rows, rows] for r in range(2)]
        values = [at_ref[1, r, rows, rows] for r in range(2)]
        total = (
            jnp.where(first, diagonal_of(keys[0]), diagonal_of(keys[1])) * h
            + jnp.where(first, diagonal_of(values[0]), diagonal_of(values[1])) * p
        )
        for level, half in enumerate(HALVES):
            e = e_ref[level, rows, :]
            he, pe = parts_of(h * e), parts_of(p * e)
            pairs = pair_mask(half, turned=True)
            y = [
                dot_parts(parts_of(jnp.where(pairs, keys[r], 0.0)), he, NN)
                + dot_parts(parts_of(jnp.where(pairs, values[r], 0.0)), pe, NN)
                for r in range(2)
            ]
            total = total + e * jnp.where(first, y[0], y[1])
        back_ref[rows, :] = total

    for right, left, half in far_pairs(tiles):
        after, before = far_decays(right, left, half, decay_ref, reach_ref)
        here = slice(right * TILE, (right + half) * TILE)
        there = slice(left * TILE, (left + half) * TILE)
        he, pe = parts_of(h_ref[here, :] * after), parts_of(p_ref[here, :] * after)
        y = [
            dot_parts(parts_of(at_ref[0, r, there, here]), he, NN)
            + dot_parts(parts_of(at_ref[1, r, there, here]), pe, NN)
            for r in range(2)
        ]
        back_ref[there, :] += before * jnp.where(first_row(half * TILE), y[0], y[1])

    for r in range(2):
        rows = slice(r * length, (r + 1) * length)
        c = parts_of(jnp.where(dcol_ref[r] == drow_ref[r], a_ref[r], 0.0))
        w = parts_of(b_ref[r])
        for f in range(2):
            gq = dot(c[0], k[f][r], NN) + dot(c[1], k[f][r], NN)
            out_ref[f, rows, :depth] = (gq * slope(pre_ref[f, rows, :depth])).astype(BF16)
            gk = dot(c[0], q[f][r], TN) + dot(c[1], q[f][r], TN)
            out_ref[f, rows, depth:2 * depth] = (gk * slope(pre_ref[f, rows, depth:2 * depth])).astype(BF16)
            gv = dot(w[0], grads[f][r], TN) + dot(w[1], grads[f][r], TN)
            out_ref[f, rows, 2 * depth:3 * depth] = gv.astype(BF16)
    carried = jnp.zeros((1, 2 * SLOTS), F32)
    for j in range(tiles - 1, -1, -1):
        rows = slice(j * TILE, (j + 1) * TILE)
        back = back_ref[rows, :]
        change = dot_ref[rows, :] - gain_ref[rows, :] * back
        upward = dot_ones(ones_where(s >= t), change) + carried
        h_ref[rows, :] = (upward - jnp.exp(lf_ref[rows, :]) * back) * rate_ref[rows, :]
        carried = upward[0:1, :]
    grad_z = h_ref[...]
    bias_ref[...] = jnp.broadcast_to(jnp.sum(grad_z, axis=0, keepdims=True), bias_ref.shape)
    for r in range(2):
        for f in range(2):
            out_ref[f, r * length:(r + 1) * length, 3 * depth:] = dot(grad_z.astype(BF16), to_columns(r, f), NN).astype(BF16)


def slope(v):
    s = sigmoid(v)
    return s * (1.0 + v * (1.0 - s))


def cost(us):
    return pl.CostEstimate(flops=0, bytes_accessed=us * 3_000_000, transcendentals=0)


def mix_forward(pre, lf, gain, doc):
    length = lf.shape[0]
    lanes = (length, 2 * SLOTS)
    square = (2, length, length)
    return pl.pallas_call(
        forward_kernel,
        name="mix_forward",
        out_shape=(
            jax.ShapeDtypeStruct((2, 2, 2, length // 2, DEPTH // 2), BF16), jax.ShapeDtypeStruct(lanes, F32),
            jax.ShapeDtypeStruct(lanes, F32), jax.ShapeDtypeStruct(square, F32),
        ),
        scratch_shapes=[
            pltpu.VMEM(square, F32), pltpu.VMEM(lanes, F32), pltpu.VMEM(lanes, F32),
            pltpu.VMEM((len(HALVES),) + lanes, F32),
        ],
        compiler_params=pltpu.CompilerParams(vmem_limit_bytes=50 << 20),
        cost_estimate=cost(16),
    )(pre, lf, gain, doc[:, :, None], doc[:, None, :])


def mix_backward(pre, g, lf, gain, rate, doc, s, p, b):
    length = lf.shape[0]
    lanes = (length, 2 * SLOTS)
    square = (2, length, length)
    return pl.pallas_call(
        backward_kernel,
        name="mix_backward",
        out_shape=(jax.ShapeDtypeStruct(pre.shape, BF16), jax.ShapeDtypeStruct((8, 2 * SLOTS), F32)),
        scratch_shapes=[
            pltpu.VMEM(square, F32), pltpu.VMEM((2,) + square, F32),
            pltpu.VMEM(lanes, F32), pltpu.VMEM(lanes, F32), pltpu.VMEM(lanes, F32),
            pltpu.VMEM(lanes, F32), pltpu.VMEM(lanes, F32), pltpu.VMEM((len(HALVES),) + lanes, F32),
        ],
        compiler_params=pltpu.CompilerParams(vmem_limit_bytes=60 << 20),
        cost_estimate=cost(28),
    )(pre, g, lf, gain, rate, doc[:, :, None], doc[:, None, :], s, p, b)


def hidden_kernel(nf_ref, wg_ref, wu_ref, hidden_ref, slope_ref, silu_ref):
    nf = nf_ref[...]
    gate, up = dot(nf, wg_ref[0], NN), dot(nf, wu_ref[0], NN)
    s = sigmoid(gate)
    silu = gate * s
    hidden_ref[0] = (silu * up).astype(BF16)
    slope_ref[0] = (up * (s * (1.0 + gate * (1.0 - s)))).astype(BF16)
    silu_ref[0] = silu.astype(BF16)


def unit_specs(tokens, features, units):
    rows = tokens // 2
    return (
        pl.BlockSpec((rows, features), lambda h, t: (t, 0)),
        pl.BlockSpec((1, features, units), lambda h, t: (h, 0, 0)),
        pl.BlockSpec((1, rows, units), lambda h, t: (h, t, 0)),
        jax.ShapeDtypeStruct((2, tokens, units), BF16),
    )


def hidden_units(nf, wg, wu):
    some, weight, unit, units_all = unit_specs(*nf.shape, wg.shape[2])
    return pl.pallas_call(
        hidden_kernel,
        name="hidden_units",
        grid=(2, 2),
        in_specs=[some, weight, weight],
        out_specs=[unit] * 3,
        out_shape=[units_all] * 3,
        compiler_params=pltpu.CompilerParams(vmem_limit_bytes=60 << 20),
        cost_estimate=cost(20),
    )(nf, wg, wu)


def hidden_grads_kernel(cot_ref, slope_ref, silu_ref, wg_ref, wu_ref, wd_ref, gg_ref, gu_ref, back_ref, total_ref):
    half, tile = pl.program_id(0), pl.program_id(1)
    rows = cot_ref.shape[0]
    here = pl.ds(pl.multiple_of(tile * rows, rows), rows)
    grad = dot(cot_ref[...], wd_ref[0], NT)
    gg = (grad * slope_ref[0].astype(F32)).astype(BF16)
    gu = (grad * silu_ref[0].astype(F32)).astype(BF16)
    gg_ref[0], gu_ref[0] = gg, gu
    back = dot(gg, wg_ref[0], NT) + dot(gu, wu_ref[0], NT)

    @pl.when(half == 0)
    def _():
        total_ref[here, :] = back

    @pl.when(half == 1)
    def _():
        back_ref[...] = (total_ref[here, :] + back).astype(BF16)


def hidden_grads(cot, slopes, silus, wg, wu, wd):
    tokens, features = cot.shape
    units = wg.shape[2]
    some, weight, unit, units_all = unit_specs(tokens, features, units)
    return pl.pallas_call(
        hidden_grads_kernel,
        name="hidden_grads",
        grid=(2, 2),
        in_specs=[some, unit, unit, weight, weight, pl.BlockSpec((1, units, features), lambda h, t: (h, 0, 0))],
        out_specs=[unit, unit, pl.BlockSpec((tokens // 2, features), lambda h, t: (h * t, 0))],
        out_shape=[units_all, units_all, jax.ShapeDtypeStruct(cot.shape, BF16)],
        scratch_shapes=[pltpu.VMEM((tokens, features), F32)],
        compiler_params=pltpu.CompilerParams(vmem_limit_bytes=60 << 20),
        cost_estimate=cost(32),
    )(cot, slopes, silus, wg, wu, wd)


def later(count, waits, body, *refs):
    body(*refs[:count], *refs[count + waits:])


def out_kernel(a_ref, b_ref, out_ref):
    grads = dot(a_ref[...], b_ref[0], TN).astype(BF16)
    wide = grads.shape[1] // 2
    for f in range(2):
        out_ref[0, f] = grads[:, f * wide:(f + 1) * wide]


def out_grads(a, b):
    planes = lax.axis_size("z")
    tokens, depth = a.shape
    features = b.shape[2]
    rows = max(depth // planes, TILE)
    grads = pl.pallas_call(
        out_kernel,
        name="out_grads",
        grid=(depth // rows,),
        in_specs=[
            pl.BlockSpec((tokens, rows), lambda i: (0, i)), pl.BlockSpec((1, tokens, features), lambda i: (0, 0, 0)),
        ],
        out_specs=pl.BlockSpec((1, 2, rows, features // 2), lambda i: (i, 0, 0, 0)),
        out_shape=jax.ShapeDtypeStruct((depth // rows, 2, rows, features // 2), BF16),
        compiler_params=pltpu.CompilerParams(vmem_limit_bytes=60 << 20),
        cost_estimate=cost(8),
    )(a, b)
    if rows * planes > depth:
        grads = grads.reshape(-1, 2, rows * planes // depth, depth // planes, features // 2).transpose(0, 2, 1, 3, 4)
    return grads.reshape(planes, 2, depth // planes, features // 2)


def weight_kernel(a_ref, *refs):
    for i, b_ref in enumerate(refs[:-1]):
        refs[-1][0, 0, i] = dot(a_ref[...], b_ref[0], TN).astype(BF16)


def weight_sums_kernel(a_ref, b_ref, sums_ref, out_ref):
    grads = dot(a_ref[...], b_ref[0], TN)
    wide = grads.shape[1]
    out_ref[0, 0, 0, :, :wide - TILE] = grads[:, :wide - TILE].astype(BF16)
    once = jnp.where(pl.program_id(0) == 0, 1.0, 0.0)
    out_ref[0, 0, 0, :, wide - TILE:] = (grads[:, wide - TILE:] + once * sums_ref[...]).astype(BF16)


def weight_grads(a, *others, sums=None, after=()):
    planes = lax.axis_size("z")
    tokens, features = a.shape
    rows = features // planes
    specs = [pl.BlockSpec((tokens, rows), lambda h, z: (0, z))]
    specs += [pl.BlockSpec((1,) + b.shape[1:], lambda h, z: (h, 0, 0)) for b in others]
    body, operands = weight_kernel, (a,) + others
    count, columns = len(others), others[0].shape[2]
    if sums is not None:
        body, operands = weight_sums_kernel, operands + (sums,)
        specs.append(pl.BlockSpec((rows, TILE), lambda h, z: (z, 0)))
    if after:
        body = functools.partial(later, len(operands), len(after), body)
        specs += [pl.BlockSpec(memory_space=pl.ANY)] * len(after)
    return pl.pallas_call(
        body,
        name="weight_grads",
        grid=(2, planes),
        in_specs=specs,
        out_specs=pl.BlockSpec((1, 1, count, rows, columns), lambda h, z: (z, h, 0, 0, 0)),
        out_shape=jax.ShapeDtypeStruct((planes, 2, count, rows, columns), BF16),
        compiler_params=pltpu.CompilerParams(vmem_limit_bytes=60 << 20),
        cost_estimate=cost(12 * len(others)),
    )(*operands, *after)


def down_kernel(hidden_ref, cot_ref, out_ref):
    grads = dot(hidden_ref[0], cot_ref[...], TN)
    rows = out_ref.shape[2]
    for z in range(out_ref.shape[0]):
        out_ref[z, 0] = grads[z * rows:(z + 1) * rows].astype(BF16)


def down_grads(hidden, cot):
    planes = lax.axis_size("z")
    tokens, features = cot.shape
    units = hidden.shape[2]
    wide = features // 2
    return pl.pallas_call(
        down_kernel,
        name="down_grads",
        grid=(2, 2),
        in_specs=[
            pl.BlockSpec((1, tokens, units), lambda h, i: (h, 0, 0)),
            pl.BlockSpec((tokens, wide), lambda h, i: (0, i)),
        ],
        out_specs=pl.BlockSpec((planes, 1, units // planes, wide), lambda h, i: (0, h, 0, i)),
        out_shape=jax.ShapeDtypeStruct((planes, 2, units // planes, features), BF16),
        compiler_params=pltpu.CompilerParams(vmem_limit_bytes=60 << 20),
        cost_estimate=cost(12),
    )(hidden, cot)


def input_kernel(grad_ref, w_ref, x_ref, out_ref, sums_ref):
    tile = pl.program_id(0)
    back = dot(grad_ref[0], w_ref[0], NT) + dot(grad_ref[1], w_ref[1], NT)
    out_ref[...] = back.astype(BF16)
    x = x_ref[...].astype(F32)
    xh = x * lax.rsqrt(jnp.mean(x * x, axis=1, keepdims=True) + EPSILON)
    sums = jnp.sum((back * xh).reshape(-1, 8, back.shape[1]), axis=0)
    sums_ref[...] = jnp.where(tile == 0, sums, sums_ref[...] + sums)


def input_grads(grad, w, x):
    tokens, features = x.shape
    rows = tokens // 4
    return pl.pallas_call(
        input_kernel,
        name="input_grads",
        grid=(4,),
        in_specs=[
            pl.BlockSpec((2, rows, grad.shape[2]), lambda t: (0, t, 0)), pl.BlockSpec(w.shape, lambda t: (0, 0, 0)),
            pl.BlockSpec((rows, features), lambda t: (t, 0)),
        ],
        out_specs=[pl.BlockSpec((rows, features), lambda t: (t, 0)), pl.BlockSpec((8, features), lambda t: (0, 0))],
        out_shape=[jax.ShapeDtypeStruct(x.shape, BF16), jax.ShapeDtypeStruct((8, features), F32)],
        compiler_params=pltpu.CompilerParams(vmem_limit_bytes=60 << 20),
        cost_estimate=cost(12),
    )(grad, w, x)


MESH = pl.DeviceIdType.MESH


def routes(kind, i, y, x, c):
    chip = {"y": i // 2 % 2, "x": i % 2}
    if kind == "to_homes":
        return {"y": c, "x": i // 2, "c": i % 2}, {**chip, "c": y}, y * 2 + x
    if kind in ("from_homes", "copy_homes"):
        return {**chip, "c": y}, {"y": c, "x": i // 2, "c": i % 2}, x * 2 + c
    if kind == "columns":
        return {**chip, "c": c}, {**chip, "c": c}, y * 2 + x
    return {**chip, "c": i // 4}, {**chip, "c": i // 4}, c * 4 + y * 2 + x


def enter_plane(y, x, c, more=()):
    barrier = pltpu.get_barrier_semaphore()
    peers = list(more)
    for flip in range(1, 8):
        peers.append({
            "y": lax.rem(y + flip // 4, 2), "x": lax.rem(x + (flip // 2) % 2, 2), "c": lax.rem(c + flip % 2, 2)
        })
    for peer in peers:
        pl.semaphore_signal(barrier, inc=1, device_id=peer, device_id_type=MESH)
    pl.semaphore_wait(barrier, len(peers))


def swap_kernel_sems(count):
    return [pltpu.SemaphoreType.DMA((count,)), pltpu.SemaphoreType.DMA((count,))]


def enter_pairs(y, x):
    barrier = pltpu.get_barrier_semaphore()
    for peer in ({"y": 1 - y}, {"x": 1 - x}):
        pl.semaphore_signal(barrier, inc=1, device_id=peer, device_id_type=MESH)
    pl.semaphore_wait(barrier, 2)


def remote(source, target, send, recv, peer):
    return pltpu.make_async_remote_copy(
        src_ref=source, dst_ref=target, send_sem=send, recv_sem=recv, device_id=peer, device_id_type=MESH
    )


class Gather:
    def __init__(self, a_ref, out_ref, y, x, send, recv, local):
        to_x, to_y = {"x": 1 - x}, {"y": 1 - y}
        self.places = here, at_x, at_y, _ = y * 2 + x, y * 2 + 1 - x, (1 - y) * 2 + x, (1 - y) * 2 + 1 - x
        half = a_ref.shape[0] // 2
        parts = [pl.ds(0, half), pl.ds(half, half)]

        def copy(source, place, part, n, peer):
            return remote(source.at[parts[part]], out_ref.at[place, parts[part]], send.at[n], recv.at[n], peer)

        self.own = pltpu.make_async_copy(a_ref, out_ref.at[here], local)
        self.first = [copy(a_ref, here, 0, 0, to_x), copy(a_ref, here, 1, 1, to_y)]
        self.second = [copy(a_ref, here, 1, 2, to_x), copy(a_ref, here, 0, 3, to_y)]
        self.passed = [copy(out_ref.at[at_x], at_x, 0, 4, to_y), copy(out_ref.at[at_y], at_y, 1, 5, to_x)]

    def start(self):
        for copy in [self.own] + self.first + self.second:
            copy.start()

    def go_on(self):
        for copy, onward in zip(self.first, self.passed):
            copy.wait_recv()
            onward.start()

    def wait(self):
        for copy in self.second + self.passed:
            copy.wait_recv()
        for copy in self.first + self.second + self.passed:
            copy.wait_send()
        self.own.wait()


def gather_kernel(count, *refs):
    outs, sems = refs[-4 * count:-3 * count], refs[-3 * count:]
    y, x = lax.axis_index("y"), lax.axis_index("x")
    enter_pairs(y, x)
    gathers = [Gather(refs[n], outs[n], y, x, *sems[3 * n:3 * n + 3]) for n in range(count)]
    for gather in gathers:
        gather.start()
    for gather in gathers:
        gather.go_on()
    for gather in gathers:
        gather.wait()


def gather_sems():
    return swap_kernel_sems(6) + [pltpu.SemaphoreType.DMA]


def gather_plane(collective, *arrays, after=()):
    any_place, count = pl.BlockSpec(memory_space=pl.ANY), len(arrays)
    return pl.pallas_call(
        functools.partial(gather_kernel, count),
        name="gather_plane",
        out_shape=[jax.ShapeDtypeStruct((4,) + a.shape, a.dtype) for a in arrays],
        in_specs=[any_place] * (count + len(after)),
        out_specs=[any_place] * count,
        scratch_shapes=gather_sems() * count,
        compiler_params=pltpu.CompilerParams(collective_id=collective, has_side_effects=True),
        cost_estimate=cost(38 * count),
    )(*arrays, *after)


class Moves:
    def __init__(self, kind, a_ref, out_ref, y, x, c, send, recv, local):
        self.copies = []
        for i in range(out_ref.shape[0]):
            peer, giver, slot = routes(kind, i, y, x, c)
            source = a_ref if kind == "copy_homes" else a_ref.at[:, i % 4] if kind == "spread" else a_ref.at[i]
            to_me, from_me = (
                (at["y"] == y) & (at["x"] == x) & (at["c"] == c) for at in (peer, giver)
            )
            self.copies.append((
                to_me, from_me,
                pltpu.make_async_copy(source, out_ref.at[slot], local),
                remote(source, out_ref.at[slot], send.at[i], recv.at[slot], peer),
                pltpu.make_async_copy(source, out_ref.at[i], local),
                remote(source, out_ref.at[i], send.at[i], recv.at[i], peer),
            ))

    def start(self):
        for to_me, _, here, there, _, _ in self.copies:
            pl.when(to_me)(here.start)
            pl.when(jnp.logical_not(to_me))(there.start)

    def wait(self):
        for to_me, from_me, _, _, here, there in self.copies:
            pl.when(jnp.logical_not(to_me))(there.wait_send)
            pl.when(jnp.logical_not(from_me))(there.wait_recv)
            pl.when(from_me)(here.wait)


def move_sems(kind):
    slots = 8 if kind == "spread" else 4
    return swap_kernel_sems(slots) + [pltpu.SemaphoreType.DMA]


def moved(kind, a):
    block = a.shape if kind == "copy_homes" else (a.shape[0],) + a.shape[2:] if kind == "spread" else a.shape[1:]
    return jax.ShapeDtypeStruct((8 if kind == "spread" else 4,) + block, a.dtype)


def move_kernel(kinds, waits, *refs):
    count = len(kinds)
    sources, results, sems = refs[:count], refs[count + waits:2 * count + waits], refs[2 * count + waits:]
    y, x, c = (lax.axis_index(name) for name in ("y", "x", "c"))
    enter_plane(y, x, c)
    moves = [
        Moves(kind, sources[n], results[n], y, x, c, *sems[3 * n:3 * n + 3]) for n, kind in enumerate(kinds)
    ]
    for one in moves:
        one.start()
    for one in moves:
        one.wait()


def move(collective, *items, after=(), us=48):
    kinds = tuple(kind for kind, _ in items)
    any_place = pl.BlockSpec(memory_space=pl.ANY)
    return pl.pallas_call(
        functools.partial(move_kernel, kinds, len(after)),
        name=kinds[0],
        out_shape=[moved(kind, a) for kind, a in items],
        in_specs=[any_place] * (len(items) + len(after)),
        out_specs=[any_place] * len(items),
        scratch_shapes=[sem for kind in kinds for sem in move_sems(kind)],
        compiler_params=pltpu.CompilerParams(collective_id=collective, has_side_effects=True),
        cost_estimate=cost(us),
    )(*(a for _, a in items), *after)


def start_kernel(kinds, planes, *refs):
    count = len(kinds)
    sources, w_ref, m_ref = refs[:count], refs[count], refs[count + 1]
    results, w_out_ref, m_out_ref = refs[count + 2:2 * count + 2], refs[2 * count + 2], refs[2 * count + 3]
    sems = refs[2 * count + 4:]
    y, x, c, z = (lax.axis_index(name) for name in ("y", "x", "c", "z"))
    up, down = lax.rem(z + 1, planes), lax.rem(z + planes - 1, planes)
    enter_plane(y, x, c, [{"z": up}, {"z": down}])
    moves = [
        Moves(kind, sources[n], results[n], y, x, c, *sems[3 * n:3 * n + 3]) for n, kind in enumerate(kinds)
    ]
    sems = sems[3 * count:]
    rows = Gather(w_ref, w_out_ref.at[c], y, x, *sems[:3])
    m_send, m_recv, core_send, core_recv, pass_send, pass_recv, local = sems[3:]
    other = {"c": 1 - c}

    def block(step):
        at = lax.rem(z + planes - step, planes)
        return m_ref if step == 0 else m_out_ref.at[c, at], m_out_ref.at[c, at]

    ring = [remote(*block(step), m_send.at[step], m_recv.at[step], {"z": up}) for step in range(planes - 1)]
    across = [remote(*block(step), core_send.at[step], core_recv.at[step], other) for step in range(planes)]
    own = pltpu.make_async_copy(m_ref, m_out_ref.at[c, z], local)
    passed = [
        remote(w_ref if n == 0 else w_out_ref.at[c, at], w_out_ref.at[c, at], pass_send.at[n], pass_recv.at[n], other)
        for n, at in enumerate(rows.places)
    ]
    ring[0].start()
    across[0].start()
    own.start()
    for one in moves:
        one.start()
    rows.start()
    passed[0].start()
    rows.go_on()
    for step in range(planes - 1):
        ring[step].wait_recv()
        if step < planes - 2:
            ring[step + 1].start()
        across[step + 1].start()
    for one in moves:
        one.wait()
    rows.wait()
    for copy in passed[1:]:
        copy.start()
    for copy in across + passed:
        copy.wait()
    for copy in ring:
        copy.wait_send()
    own.wait()


def start_moves(collective, items, w_half, mixer_part):
    planes = lax.axis_size("z")
    kinds = tuple(kind for kind, _ in items)
    any_place = pl.BlockSpec(memory_space=pl.ANY)
    shapes = [moved(kind, a) for kind, a in items]
    shapes.append(jax.ShapeDtypeStruct((2, 4) + w_half.shape, w_half.dtype))
    shapes.append(jax.ShapeDtypeStruct((2, planes) + mixer_part.shape, mixer_part.dtype))
    sems = [sem for kind in kinds for sem in move_sems(kind)] + gather_sems()
    sems += swap_kernel_sems(planes) + swap_kernel_sems(planes) + swap_kernel_sems(4) + [pltpu.SemaphoreType.DMA]
    return pl.pallas_call(
        functools.partial(start_kernel, kinds, planes),
        name="start_moves",
        out_shape=shapes,
        in_specs=[any_place] * (len(items) + 2),
        out_specs=[any_place] * len(shapes),
        scratch_shapes=sems,
        compiler_params=pltpu.CompilerParams(collective_id=collective, has_side_effects=True),
        cost_estimate=cost(85),
    )(*(a for _, a in items), w_half, mixer_part)


def reduce_kernel(a_ref, *refs):
    out_ref, got_ref, sum_ref, last_ref, send, recv = refs[-6:]
    y, x = lax.axis_index("y"), lax.axis_index("x")
    enter_pairs(y, x)
    half = out_ref.shape[0] // 2
    parts = [pl.ds(0, half), pl.ds(half, half)]
    places = [(1 - y, y), (1 - x, x)]
    peers = [{"x": 1 - x}, {"y": 1 - y}]

    def block(part, place, other):
        if part == 0:
            return place * 2 + (1 - x if other else x)
        return (1 - y if other else y) * 2 + place

    def copy(source, target, n, peer):
        return remote(source, target, send.at[n], recv.at[n], peer)

    first = [
        [copy(a_ref.at[block(part, places[part][i], True), parts[part]], got_ref.at[part, i], 2 * part + i, peers[part])
         for i in range(2)] for part in range(2)
    ]
    for i in range(2):
        for part in range(2):
            first[part][i].start()
    onward = [copy(sum_ref.at[part], last_ref.at[part], 4 + part, peers[1 - part]) for part in range(2)]

    def total(part, i):
        own = a_ref[block(part, places[part][i], False), parts[part], :]
        return own.astype(F32) + got_ref[part, i].astype(F32)

    for part in range(2):
        first[part][0].wait_recv()
        sum_ref[part] = total(part, 0).astype(BF16)
        onward[part].start()
    for part in range(2):
        first[part][1].wait_recv()
        out_ref[parts[part], :] = total(part, 1)
    for part in range(2):
        onward[part].wait_recv()
        out_ref[parts[part], :] += last_ref[part].astype(F32)
    for one in first[0] + first[1] + onward:
        one.wait_send()


def reduce_plane(collective, a, after=()):
    rows, features = a.shape[1:]
    half = (rows // 2, features)
    return pl.pallas_call(
        reduce_kernel,
        name="reduce_plane",
        out_shape=jax.ShapeDtypeStruct((rows, features), F32),
        in_specs=[pl.BlockSpec(memory_space=pltpu.VMEM)] + [pl.BlockSpec(memory_space=pl.ANY)] * len(after),
        out_specs=pl.BlockSpec(memory_space=pltpu.VMEM),
        scratch_shapes=[pltpu.VMEM((2, 2) + half, BF16), pltpu.VMEM((2,) + half, BF16), pltpu.VMEM((2,) + half, BF16)]
        + swap_kernel_sems(6),
        compiler_params=pltpu.CompilerParams(collective_id=collective, has_side_effects=True),
        cost_estimate=cost(38),
    )(a, *after)


def add_other(a, other):
    return (a.astype(F32) + other.astype(F32)).astype(BF16)


def halves_of(a, place, axis):
    here = lax.axis_index(axis)
    return [lax.dynamic_index_in_dim(a, at, place, keepdims=False) for at in (here, 1 - here)]


def gather_planes(a):
    return lax.all_gather(a, ("c", "z"), axis=0, tiled=True).reshape((2, -1) + a.shape[1:])


def sum_planes(a):
    return lax.psum_scatter(a.reshape((-1,) + a.shape[2:]), ("z", "c"), scatter_dimension=0, tiled=True)[0]


def swap(a, axis):
    return lax.ppermute(a, axis, [(0, 1), (1, 0)])


def both_of(a, axis):
    other = swap(a, axis)
    return jnp.where(lax.axis_index(axis) == 0, jnp.stack([a, other]), jnp.stack([other, a]))


def scaled(features):
    return lax.rsqrt(jnp.mean(features * features, axis=-1, keepdims=True) + EPSILON)


def norm_back(grad, gain, features, ratio):
    u, xh = grad * gain, features * ratio
    return ratio * (u - xh * jnp.mean(u * xh, axis=-1, keepdims=True))


def body(inputs, starts, norm_attn, w_query, w_key, w_value, w_forget, gate_bias, w_out, norm_ffn, w_gate, w_up,
         w_down, cotangent):
    positions, features = inputs.shape[1:]
    depth = features // HEADS
    y, x, c, z = (lax.axis_index(name) for name in ("y", "x", "c", "z"))
    planes = lax.axis_size("z")
    head = y * 2 + x
    rows_here = w_query.shape[0]
    hidden_here = w_down.shape[0]

    def own_half(a, axis):
        return lax.dynamic_index_in_dim(a, c, axis, keepdims=False)

    bias_here = gate_bias.shape[0]

    def columns(w):
        w = w.reshape(rows_here, HEADS, 2, -1)
        return own_half(w, 2).transpose(1, 0, 2)

    def column(v):
        v = jnp.pad(v, (0, rows_here - v.shape[0]))
        return jnp.broadcast_to(v[None, :, None], (HEADS, rows_here, 1))

    parts = [columns(w) for w in (w_query, w_key, w_value, w_forget)]
    parts += [column(v) for v in (norm_attn, norm_ffn, gate_bias)]
    width = sum(part.shape[-1] for part in parts)
    parts.append(jnp.zeros((HEADS, rows_here, -width % TILE), BF16))
    vectors = width - 3
    def hidden_columns(w):
        w = own_half(w.reshape(rows_here, planes, 4, 2, hidden_here // 2), 3)
        return w.transpose(2, 0, 1, 3).reshape(4, rows_here, -1)

    x_here = inputs.reshape(positions, features)
    cot_here = cotangent.reshape(positions, features)
    out_half = own_half(w_out.reshape(2, rows_here // 2, features), 0)
    out_half = lax.all_gather(out_half, "z", axis=0)
    (mine,) = move(1, ("columns", jnp.concatenate(parts, axis=-1)), us=14)
    full_down = gather_planes(own_half(w_down.reshape(2, hidden_here // 2, features), 0))
    begins, x_rows, gate_mine, up_mine, full_out, mixer_w = start_moves(
        2, (
            ("copy_homes", jnp.broadcast_to(starts, (8, positions))), ("copy_homes", x_here),
            ("columns", hidden_columns(w_gate)), ("columns", hidden_columns(w_up)),
        ), out_half, mine.reshape(4 * rows_here, -1),
    )
    full_gate = gather_planes(gate_mine.reshape(4 * rows_here, -1))
    full_up = gather_planes(up_mine.reshape(4 * rows_here, -1))
    full_out = full_out.reshape(2, 4, planes, rows_here // 2, features)
    full_out = full_out.transpose(2, 1, 0, 3, 4).reshape(features, features)
    mixer_w = mixer_w.reshape(2, features, -1)
    gain_attn, gain_ffn = (mixer_w[0, :, vectors + i].astype(F32) for i in range(2))
    bias = mixer_w[0, :, vectors + 2].reshape(4 * planes, rows_here)[:, :bias_here].reshape(-1).astype(F32)
    bias = lax.dynamic_slice_in_dim(bias, head * SLOTS, SLOTS)
    doc = jnp.cumsum(begins[:, 0].reshape(2, 2 * positions).astype(F32), axis=1)

    x_rows = x_rows.reshape(4 * positions, features)
    x_wide = x_rows.astype(F32)
    normed = (x_wide * scaled(x_wide) * gain_attn).astype(BF16)
    pre = jnp.einsum("td,cdf->ctf", normed, mixer_w, preferred_element_type=F32)
    z_total = pre[:, :, 3 * depth // 2:vectors].reshape(2, 2, 2 * positions, SLOTS // 2)
    z_total = z_total.transpose(2, 1, 0, 3).reshape(2 * positions, 2 * SLOTS) + jnp.tile(bias, 2)
    log_forget = jax.nn.log_sigmoid(z_total) / 8.0
    gain = -jnp.expm1(log_forget)
    mixed, scores, probs, paired = mix_forward(pre, log_forget, gain, doc)
    mixed_rows = mixed.reshape(4, 2, positions, depth // 2).transpose(0, 2, 1, 3).reshape(4 * positions, depth)
    (mixed,) = move(4, ("to_homes", mixed.reshape(4, 2 * positions, depth // 2)), us=14)
    mixed = mixed.reshape(2 * HEADS, positions, depth // 2).transpose(1, 0, 2).reshape(positions, features)
    attended = x_here.astype(F32) + jnp.dot(mixed, full_out, preferred_element_type=F32)

    ratio_f = scaled(attended)
    normed_ffn, cot = gather_plane(5, (attended * ratio_f * gain_ffn).astype(BF16), cot_here)
    cot = cot.reshape(4 * positions, features)
    normed_ffn = normed_ffn.reshape(4 * positions, features)
    hidden, slopes, silus = hidden_units(normed_ffn, full_gate, full_up)
    grad_down_w = down_grads(hidden, cot)
    grad_gate, grad_up, grad_normed_ffn = hidden_grads(cot, slopes, silus, full_gate, full_up, full_down)
    grad_hidden_w = weight_grads(normed_ffn, grad_gate, grad_up)
    grad_normed_ffn = reduce_plane(
        6, grad_normed_ffn.reshape(4, positions, features), after=(grad_down_w, grad_hidden_w)
    )
    grad_down_w, grad_hidden_w = sum_planes(grad_down_w), sum_planes(grad_hidden_w)
    block_out = jnp.einsum("ctf,cfd->td", hidden, full_down, preferred_element_type=F32).astype(BF16)
    grad_gain_ffn = jnp.sum(grad_normed_ffn * attended * ratio_f, axis=0)
    grad_attended = cot_here.astype(F32) + norm_back(grad_normed_ffn, gain_ffn, attended, ratio_f)

    grad_branch = grad_attended.astype(BF16)
    grad_mixed = jnp.einsum("te,de->td", grad_branch, full_out, preferred_element_type=F32).astype(BF16)
    grad_mixed = grad_mixed.reshape(positions, HEADS, 2, depth // 2).transpose(1, 2, 0, 3)
    grad_mixed, branch_rows = move(
        8, ("from_homes", grad_mixed.reshape(4, 2 * positions, depth // 2)), ("copy_homes", grad_branch),
        after=(grad_down_w,), us=60,
    )
    branch_rows = branch_rows.reshape(1, 4 * positions, features)
    grad_mixed = grad_mixed.reshape(2, 2, 2, positions, depth // 2)
    rate = jax.nn.sigmoid(-z_total) / 8.0
    grad_pre, grad_bias = mix_backward(pre, grad_mixed, log_forget, gain, rate, doc, scores, probs, paired)
    grad_bias = jnp.sum(grad_bias[0].reshape(2, SLOTS), axis=0)
    grad_out_w = out_grads(mixed_rows, branch_rows)
    grad_normed, sums = input_grads(grad_pre, mixer_w, x_rows)
    grad_bias = jnp.zeros((HEADS, SLOTS), F32).at[head].set(grad_bias).reshape(4 * planes, bias_here)
    grad_bias = jnp.pad(grad_bias, ((0, 0), (0, rows_here - bias_here))).reshape(-1)
    sums = jnp.stack([jnp.sum(sums, axis=0), grad_gain_ffn, grad_bias], axis=-1)
    first_sum = vectors + TILE - mixer_w.shape[-1]
    sums = jnp.pad(sums, ((0, 0), (first_sum, TILE - first_sum - 3)))
    grad_mixer_w = weight_grads(normed, grad_pre, sums=sums, after=(grad_hidden_w,))
    grad_out_w = sum_planes(grad_out_w)
    grad_normed, grad_hidden_w = move(
        9, ("to_homes", grad_normed.reshape(4, positions, features)),
        ("spread", grad_hidden_w.reshape(2, 4, rows_here, -1)), after=(grad_mixer_w, grad_out_w), us=75,
    )
    grad_mixer_w = sum_planes(grad_mixer_w)
    grad_normed_here = jnp.sum(grad_normed.astype(F32), axis=0)
    x_here = x_here.astype(F32)
    ratio_a = scaled(x_here)
    grad_input = grad_attended + norm_back(grad_normed_here, gain_attn, x_here, ratio_a)

    block_out = reduce_plane(7, block_out.reshape(4, positions, features), after=(grad_normed,))
    output = (attended + block_out).astype(BF16)

    def to_rows(collective, a):
        (a,) = move(collective, ("spread", a.reshape(a.shape[0], 4, rows_here, -1)), us=18)
        return a.reshape((2, 4) + a.shape[1:])

    def from_hidden(a):
        a = a.reshape(2, 4, rows_here, planes, hidden_here // 2)
        return a.transpose(2, 3, 1, 0, 4).reshape(rows_here, -1).astype(F32)

    grad_hidden_w = grad_hidden_w.reshape((2, 4) + grad_hidden_w.shape[1:])
    grad_gate_w, grad_up_w = from_hidden(grad_hidden_w[:, :, 0]), from_hidden(grad_hidden_w[:, :, 1])
    blocks = 4 * planes
    grad_out_w = lax.ppermute(
        grad_out_w, ("z", "y", "x"), [(at, at % 4 * planes + at // 4) for at in range(blocks)]
    )
    grad_out_w = both_of(grad_out_w, "c").transpose(1, 0, 2).reshape(rows_here, features).astype(F32)
    grad_down_w = both_of(grad_down_w, "c").reshape(hidden_here, features).astype(F32)
    grad_mixer_w = to_rows(12, grad_mixer_w)[:, :, 0]
    sums = jnp.sum(grad_mixer_w[0, :, :, vectors:width].astype(F32), axis=0)
    grad_mixer_w = grad_mixer_w.transpose(2, 1, 0, 3)
    grad_w = [
        grad_mixer_w[..., i * depth // 2:(i + 1) * depth // 2].reshape(rows_here, features).astype(F32) for i in range(3)
    ]
    grad_forget_w = grad_mixer_w[..., 3 * depth // 2:vectors].reshape(rows_here, HEADS * SLOTS).astype(F32)
    return (
        output.reshape(inputs.shape), grad_input.reshape(inputs.shape), sums[:, 0], grad_w[0], grad_w[1], grad_w[2],
        grad_forget_w, sums[:bias_here, 2], grad_out_w, sums[:, 1], grad_gate_w, grad_up_w, grad_down_w,
    )


def solution(mesh):
    planes = mesh.shape["dp"] // 4
    fine = Mesh(mesh.devices.reshape(planes, 2, 2, 2), ("z", "y", "x", "c"))
    dp = ("z", "y", "x")
    tokens, vector, matrix = P(dp, "c", None), P(dp), P(dp, None)
    in_specs = (
        tokens, P(dp, "c"), vector, matrix, matrix, matrix, matrix, vector, matrix, vector, matrix, matrix, matrix, tokens
    )
    out_specs = (
        tokens, tokens, vector, matrix, matrix, matrix, matrix, vector, matrix, vector, matrix, matrix, matrix
    )
    return jax.shard_map(body, mesh=fine, in_specs=in_specs, out_specs=out_specs, check_vma=False)
```

time: 1140 us -> 856 us (0.75)
  Pallas kernels: 406 us -> 661 us
  waiting for transfers between devices: 253 us -> 9.66 us
  blocking collectives: 176 us -> 0 us
  matrix products: 147 us -> 33.2 us
  other arithmetic: 51 us -> 37.6 us
    pallas_call x8 -> x16, Pallas kernels: 370 us -> 618 us  [the longest x5 215 us: move(): pl.pallas_call(functools.partial(move_kernel, kinds, len(after)), name=ki...]
    reduce_scatter x5 -> x4, waiting for transfers between devices: 219 us -> 0.01 us  [sum_planes(): lax.psum_scatter(a.reshape((-1,) + a.shape[2:]), ('z', 'c'), scatter_dime...]
    dot_general x11 -> x0, matrix products: 114 us -> none  [the longest x1 15.9 us: body(): jnp.einsum('td,cfd->ctf', cot, full_down, preferred_element_type=F32)]
    all_to_all x6 -> x0, blocking collectives: 87.9 us -> none  [the longest x3 47.4 us: to_rows(): lax.all_to_all(a.reshape(4, rows_here, -1), PLANE, split_axis=0, concat_a...]
    unnamed x1 -> x0, blocking collectives: 43 us -> none
    psum x1 -> x0, blocking collectives: 42.7 us -> none  [body(): lax.psum(jnp.concatenate([grad_gain_attn, grad_gain_ffn, bias_all]), ('z'...]
    all_gather x9 -> x4, waiting for transfers between devices: 32.9 us -> 8.85 us  [the longest x3 8.01 us: gather_planes(): lax.all_gather(a, ('c', 'z'), axis=0, tiled=True)]
    convert_element_type x14 -> x9, other arithmetic: 25.8 us -> 12.8 us  [the longest x2 6.18 us: body(): normed = (x_wide * scaled(x_wide) * gain_attn).astype(BF16)]
  transfers between devices with their start and end apart: 14 -> 11, of which waited for: 4 -> 2; matrix products, arithmetic and copies ran while one was open for 23% -> 15% of each run, Pallas kernels for 36% -> 60%
where the time goes in v2:
time: 856 us; the launch traced here: 848 us
  Pallas kernels  661 us (77%)
  local copies, waits for them, and re-layouts  87.3 us (10%)
  other arithmetic  37.6 us (4%)
  matrix products  33.2 us (4%)
  between operations  15 us (2%)
  waiting for transfers between devices  9.66 us (1%)
    pallas_call x5, Pallas kernels, move(): pl.pallas_call(functools.partial(move_kernel, kinds, len(after)), name=ki...  215 us
    pallas_call x1, Pallas kernels, start_moves(): pl.pallas_call(functools.partial(start_kernel, kinds, planes), name='star...  129 us
    pallas_call x2, Pallas kernels, reduce_plane(): pl.pallas_call(reduce_kernel, name='reduce_plane', out_shape=jax.ShapeDty...  81.6 us
    pallas_call x1, Pallas kernels, gather_plane(): pl.pallas_call(functools.partial(gather_kernel, count), name='gather_plan...  72.3 us
    unnamed x89, local copies, waits for them, and re-layouts  37.7 us
    pallas_call x2, Pallas kernels, weight_grads(): pl.pallas_call(body, name='weight_grads', grid=(2, planes), in_specs=spec...  34 us
    pallas_call x1, Pallas kernels, hidden_grads(): pl.pallas_call(hidden_grads_kernel, name='hidden_grads', grid=(2, 2), in_...  33.8 us
    pallas_call x1, Pallas kernels, mix_backward(): pl.pallas_call(backward_kernel, name='mix_backward', out_shape=(jax.Shape...  27.3 us
  transfers between devices with their start and end apart: 11, of which 2 were waited for; matrix products, arithmetic and copies ran while one was open for 15% of the time, Pallas kernels for 60%

profile of v2, /device:TPU:0, one launch (start us, length us, event | category | flops | bytes accessed | tf_op | source)
XLA Modules:
  0.0 848.2 jit_solution(15615485338231783243)
XLA Ops:
  10.9 2.5 copy.159
  13.5 2.1 dynamic-slice_bitcast_fusion
  21.8 2.5 concatenate.7.refs_0_
  24.3 15.7 %columns.1 = bf16[4,128,896]{2,1,0:T(8,128)(2,1)} custom-call(bf16[4,128,896]{2,1,0:T(8,128)(2,1)} %concatenate.7.refs_0_), custom_call_target="tpu_custom_call" | custom-call | bytes 42000000 | tf_op jit(solution)/shard_map/columns/pallas_call | solution.py:744
  41.4 128.8 %start_moves.1 = (s32[4,8,256]{2,1,0:T(8,128)}, bf16[4,256,2048]{2,1,0:T(8,128)(2,1)}, bf16[4,128,704]{2,1,0:T(8,128)(2,1)}, bf16[4,128,704]{2,1,0:T(8,128)(2,1)...) custom-call(s32[8,256]{1,0:T(8,128)} %broadcast_in_dim.15.refs_0_, bf16[256,2048]{1,0:T(8,128)(2,1)} %bitcast.168, ...), custom_call_target="tpu_custom_call" | custom-call | bytes 255000000 | tf_op jit(solution)/shard_map/start_moves/pallas_call | solution.py:817
  172.2 2.0 convert_reduce_fusion.1
  174.3 3.6 fusion
  179.7 2.0 copy-done.16
  181.8 7.7 convolution_bitcast_fusion.pre_ref
  189.5 2.9 copy-done.11
  198.0 16.2 %mix_forward.1 = (bf16[2,2,2,256,256]{4,3,2,1,0:T(8,128)(2,1)S(1)}, f32[512,128]{1,0:T(8,128)S(1)}, f32[512,128]{1,0:T(8,128)S(1)}, f32[2,512,512]{2,1,0:T(8,128)}) custom-call(f32[2,1024,896]{2,1,0:T(8,128)} %copy-done.11, f32[512,128]{1,0:T(8,128)S(1)} %get-tuple-element.136.lf_ref, f32[512,128]{1,0:T(8,128)S(1)} %get-tuple-element.135.gain_ref, ...), custom_call_target="tpu_custom_call" | custom-call | bytes 48000000 | tf_op jit(solution)/shard_map/mix_forward/pallas_call | solution.py:351
  216.0 13.3 %to_homes.2 = bf16[4,512,256]{2,1,0:T(8,128)(2,1)} custom-call(bf16[4,512,256]{2,1,0:T(8,128)(2,1)} %bitcast.158), custom_call_target="tpu_custom_call" | custom-call | bytes 42000000 | tf_op jit(solution)/shard_map/to_homes/pallas_call | solution.py:744
  229.3 2.3 copy.175
  231.5 8.4 copy.176
  240.0 6.7 multiply_reduce_fusion.2
  247.9 72.3 %gather_plane.1 = (bf16[4,256,2048]{2,1,0:T(8,128)(2,1)}, bf16[4,256,2048]{2,1,0:T(8,128)(2,1)}) custom-call(bf16[256,2048]{1,0:T(8,128)(2,1)} %multiply_convert_fusion.1.refs_0_, bf16[256,2048]{1,0:T(8,128)(2,1)} %bitcast.183), custom_call_target="tpu_custom_call" | custom-call | bytes 228000000 | tf_op jit(solution)/shard_map/gather_plane/pallas_call | solution.py:676
  320.3 19.7 %hidden_units.1 = (bf16[2,1024,704]{2,1,0:T(8,128)(2,1)}, bf16[2,1024,704]{2,1,0:T(8,128)(2,1)}, bf16[2,1024,704]{2,1,0:T(8,128)(2,1)}) custom-call(bf16[1024,2048]{1,0:T(8,128)(2,1)} %bitcast.175, bf16[2,2048,704]{2,1,0:T(8,128)(2,1)} %bitcast.169, bf16[2,2048,704]{2,1,0:T(8,128)(2,1)} %bitcast.171), custom_call_target="tpu_custom_call" | custom-call | bytes 60000000 | tf_op jit(solution)/shard_map/hidden_units/pallas_call | solution.py:407
  340.0 11.3 %down_grads.1.refs_0_ = bf16[4,2,176,2048]{3,2,1,0:T(8,128)(2,1)} custom-call(bf16[2,1024,704]{2,1,0:T(8,128)(2,1)} %get-tuple-element.59.hidden_ref, bf16[1024,2048]{1,0:T(8,128)(2,1)} %bitcast.173), custom_call_target="tpu_custom_call" | custom-call | bytes 36000000 | tf_op jit(solution)/shard_map/down_grads/pallas_call | solution.py:539
  351.4 8.0 all-gather.12.cloned.1.call-done
  359.4 33.8 %hidden_grads.1 = (bf16[2,1024,704]{2,1,0:T(8,128)(2,1)}, bf16[2,1024,704]{2,1,0:T(8,128)(2,1)}, bf16[1024,2048]{1,0:T(8,128)(2,1)}) custom-call(bf16[1024,2048]{1,0:T(8,128)(2,1)} %bitcast.174, bf16[2,1024,704]{2,1,0:T(8,128)(2,1)} %get-tuple-element.61.slope_ref, bf16[2,1024,704]{2,1,0:T(8,128)(2,1)} %get-tuple-element.62.silu_ref, ...), custom_call_target="tpu_custom_call" | custom-call | bytes 96000000 | tf_op jit(solution)/shard_map/hidden_grads/pallas_call | solution.py:442
  393.1 19.2 %weight_grads.2.refs_1_ = bf16[4,2,2,512,704]{4,3,2,1,0:T(8,128)(2,1)} custom-call(bf16[1024,2048]{1,0:T(8,128)(2,1)} %bitcast.176, bf16[2,1024,704]{2,1,0:T(8,128)(2,1)} %get-tuple-element.64.refs_0_, bf16[2,1024,704]{2,1,0:T(8,128)(2,1)} %get-tuple-element.65.refs_1_), custom_call_target="tpu_custom_call" | custom-call | bytes 72000000 | tf_op jit(solution)/shard_map/weight_grads/pallas_call | solution.py:515
  415.9 41.3 %reduce_plane.2 = f32[256,2048]{1,0:T(8,128)} custom-call(bf16[4,256,2048]{2,1,0:T(8,128)(2,1)} %bitcast.207, bf16[4,2,176,2048]{3,2,1,0:T(8,128)(2,1)} %down_grads.1.refs_0_, bf16[4,2,2,512,704]{4,3,2,1,0:T(8,128)(2,1)} %weight_grads.2.refs_1_), custom_call_target="tpu_custom_call" | custom-call | bytes 114000000 | tf_op jit(solution)/shard_map/reduce_plane/pallas_call | solution.py:876
  457.2 2.5 multiply_reduce_fusion
  461.4 6.8 convolution_convert_fusion
  471.2 58.8 %from_homes.1 = (bf16[4,512,256]{2,1,0:T(8,128)(2,1)}, bf16[4,256,2048]{2,1,0:T(8,128)(2,1)}) custom-call(bf16[4,512,256]{2,1,0:T(8,128)(2,1)} %bitcast.206, bf16[256,2048]{1,0:T(8,128)(2,1)} %copy-done.21, bf16[176,2048]{1,0:T(8,128)(2,1)} %bitcast.214), custom_call_target="tpu_custom_call" | custom-call | bytes 180000000 | tf_op jit(solution)/shard_map/from_homes/pallas_call | solution.py:744
  530.0 6.5 out_grads.1
  537.9 5.2 multiply_convert_fusion.refs_0_
  543.0 27.3 %mix_backward.1 = (bf16[2,1024,896]{2,1,0:T(8,128)(2,1)}, f32[8,128]{1,0:T(8,128)}) custom-call(f32[2,1024,896]{2,1,0:T(8,128)} %copy-done.11, bf16[2,2,2,256,256]{4,3,2,1,0:T(8,128)(2,1)} %bitcast.220, f32[512,128]{1,0:T(8,128)} %copy-done.6, f32[512,128]{1,0:T(8,128)} %copy-done.5, f32[512,128]{1,0:T(8,128)} %get-tuple-element.144.rate_ref, ...), custom_call_target="tpu_custom_call" | custom-call | bytes 84000000 | tf_op jit(solution)/shard_map/mix_backward/pallas_call | solution.py:371
  572.0 14.3 %input_grads.1 = (bf16[1024,2048]{1,0:T(8,128)(2,1)}, f32[8,2048]{1,0:T(8,128)}) custom-call(bf16[2,1024,896]{2,1,0:T(8,128)(2,1)} %get-tuple-element.70.grad_ref.refs_1_, bf16[2,2048,896]{2,1,0:T(8,128)(2,1)} %bitcast.181, bf16[1024,2048]{1,0:T(8,128)(2,1)} %bitcast.163), custom_call_target="tpu_custom_call" | custom-call | bytes 36000000 | tf_op jit(solution)/shard_map/input_grads/pallas_call | solution.py:567
  588.9 14.8 %weight_grads.3.refs_2_ = bf16[4,2,1,512,896]{4,3,2,1,0:T(8,128)(2,1)} custom-call(bf16[1024,2048]{1,0:T(8,128)(2,1)} %multiply_convert_fusion.refs_0_, bf16[2,1024,896]{2,1,0:T(8,128)(2,1)} %get-tuple-element.70.grad_ref.refs_1_, f32[2048,128]{1,0:T(8,128)} %pad.16.refs_2_, bf16[2,512,704]{2,1,0:T(8,128)(2,1)} %bitcast.190), custom_call_target="tpu_custom_call" | custom-call | bytes 36000000 | tf_op jit(solution)/shard_map/weight_grads/pallas_call | solution.py:515
  606.5 1.9 collective-permute-start
  608.4 12.0 %bitcast_convert_fusion = bf16[1024,2048]{1,0:T(8,128)(2,1)} fusion(bf16[2,1024,704]{2,1,0:T(8,128)(2,1)} %get-tuple-element.59.hidden_ref, bf16[2,704,2048]{2,1,0:T(8,128)(2,1)} %bitcast.194), kind=kOutput, calls=%fused_computation.5 | convolution fusion | flops 5907677184 | bytes 12845056 | tf_op jit(solution)/shard_map/ctf,cfd->td/dot_general | solution.py:1004
  622.1 2.0 bitcast_convert_fusion.1
  625.2 2.5 copy.184
  627.7 2.5 copy.193
  630.3 104.9 %to_homes.3 = (bf16[4,256,2048]{2,1,0:T(8,128)(2,1)}, bf16[8,2,128,704]{3,2,1,0:T(8,128)(2,1)}) custom-call(bf16[4,256,2048]{2,1,0:T(8,128)(2,1)} %bitcast.197, bf16[2,4,128,704]{3,2,1,0:T(8,128)(2,1)} %bitcast.191, bf16[4,2,1,512,896]{4,3,2,1,0:T(8,128)(2,1)} %weight_grads.3.refs_2_, bf16[128,1024]{1,0:T(8,128)(2,1)} %bitcast.226), custom_call_target="tpu_custom_call" | custom-call | bytes 225000000 | tf_op jit(solution)/shard_map/to_homes/pallas_call | solution.py:744
  735.2 3.8 fusion.18
  739.0 2.5 copy.202
  743.1 1.9 copy.186
  745.0 3.4 copy.194
  748.4 2.5 copy.203
  752.5 1.9 copy.188
  754.4 3.4 copy.195
  757.8 40.3 %reduce_plane.3 = f32[256,2048]{1,0:T(8,128)} custom-call(bf16[4,256,2048]{2,1,0:T(8,128)(2,1)} %bitcast.201, bf16[4,256,2048]{2,1,0:T(8,128)(2,1)} %get-tuple-element.75.refs_0_), custom_call_target="tpu_custom_call" | custom-call | bytes 114000000 | tf_op jit(solution)/shard_map/reduce_plane/pallas_call | solution.py:876
  798.1 3.4 convert_reduce_fusion
  803.3 2.9 fusion.9
  806.3 22.8 %spread.1 = bf16[8,1,128,896]{3,2,1,0:T(8,128)(2,1)} custom-call(bf16[1,4,128,896]{3,2,1,0:T(8,128)(2,1)} %bitcast.221), custom_call_target="tpu_custom_call" | custom-call | bytes 54000000 | tf_op jit(solution)/shard_map/spread/pallas_call | solution.py:744
  830.1 2.9 copy.183
  (183 shorter events, 57.0 us)
Async XLA Ops:
  7.2 163.9 %copy-start = (bf16[352,2048]{1,0:T(8,128)(2,1)S(1)}, bf16[352,2048]{1,0:T(8,128)(2,1)}, u32[]{:S(2)}) copy-start(bf16[352,2048]{1,0:T(8,128)(2,1)} %param.28) | copy-start | bytes 4325380
  7.2 33.6 %all-gather.6.cloned.1.call-start = ((), (), s32[]{:S(2)}) async-start(), calls=%async_computation.4 | async-start | bytes 1310720 | tf_op jit(solution)/shard_map/all_gather | solution.py:959
  9.0 311.2 %all-gather.8.cloned.1.call-start = ((), (), s32[]{:S(2)}) async-start(), calls=%async_computation.5 | async-start | bytes 7077888 | tf_op jit(solution)/shard_map/all_gather | solution.py:899
  15.5 1.2 copy-start.22
  15.6 2.4 copy-start.26
  18.0 1.0 copy-start.27
  18.4 1.1 copy-start.28
  19.8 1.3 copy-start.30
  19.9 1.6 copy-start.35
  19.9 1.6 copy-start.32
  19.9 1.7 copy-start.33
  21.8 19.1 %copy-start.31 = (s32[1,256]{1,0:T(1,128)S(1)}, s32[1,256]{1,0:T(1,128)}, u32[]{:S(2)}) copy-start(s32[1,256]{1,0:T(1,128)} %param.17) | copy-start | bytes 3076
  170.3 150.0 %all-gather.10.cloned.1.call-start = ((), (), s32[]{:S(2)}) async-start(), calls=%async_computation.6 | async-start | bytes 7077888 | tf_op jit(solution)/shard_map/all_gather | solution.py:899
  171.0 188.4 %all-gather.12.cloned.1.call-start = ((), (), s32[]{:S(2)}) async-start(), calls=%async_computation.11 | async-start | bytes 6488064 | tf_op jit(solution)/shard_map/all_gather | solution.py:899
  172.0 299.2 %reduce-scatter.5.cloned.1.call-start = ((), (), s32[]{:S(2)}) async-start(), calls=%async_computation.7 | async-start | bytes 6488064 | tf_op jit(solution)/shard_map/reduce_scatter | solution.py:903
  174.3 4.4 copy-start.10
  178.7 3.1 copy-start.16
  189.5 2.9 copy-start.11
  196.6 17.6 %copy-start.9 = (f32[2,4,128]{2,1,0:T(4,128)}, f32[2,4,128]{2,1,0:T(4,128)S(1)}, u32[]{:S(2)}) copy-start(f32[2,4,128]{2,1,0:T(4,128)S(1)} %broadcast_add_fusion) | copy-start | bytes 12292
  197.0 17.3 %copy-start.2 = (f32[2,512,1]{2,1,0:T(8,128)}, f32[2,512,1]{2,1,0:T(8,128)S(1)}, u32[]{:S(2)}) copy-start(f32[2,512,1]{2,1,0:T(8,128)S(1)} %reduce_window_sum.34.dcol_ref) | copy-start | bytes 12292
  198.0 16.3 %copy-start.5 = (f32[512,128]{1,0:T(8,128)}, f32[512,128]{1,0:T(8,128)S(1)}, u32[]{:S(2)}) copy-start(f32[512,128]{1,0:T(8,128)S(1)} %get-tuple-element.135.gain_ref) | copy-start | bytes 786436
  198.0 16.3 %copy-start.6 = (f32[512,128]{1,0:T(8,128)}, f32[512,128]{1,0:T(8,128)S(1)}, u32[]{:S(2)}) copy-start(f32[512,128]{1,0:T(8,128)S(1)} %get-tuple-element.136.lf_ref) | copy-start | bytes 786436
  214.3 1.0 copy-start.3
  215.3 0.7 copy-start.7
  216.0 15.6 %copy-start.8 = (f32[512,128]{1,0:T(8,128)}, f32[512,128]{1,0:T(8,128)S(1)}, u32[]{:S(2)}) copy-start(f32[512,128]{1,0:T(8,128)S(1)} %get-tuple-element.68.p_ref) | copy-start | bytes 786436
  231.5 8.4 copy-start.14
  231.5 8.4 copy-start.20
  351.3 237.6 %reduce-scatter.7.cloned.1.call-start = ((), (), s32[]{:S(2)}) async-start(), calls=%async_computation.8 | async-start | bytes 14155776 | tf_op jit(solution)/shard_map/reduce_scatter | solution.py:903
  412.3 1.2 copy-start.4
  412.4 194.1 %reduce-scatter.9.cloned.1.call-start = ((), (), s32[]{:S(2)}) async-start(), calls=%async_computation.9 | async-start | bytes 2359296 | tf_op jit(solution)/shard_map/reduce_scatter | solution.py:903
  457.2 2.5 copy-start.12
  457.2 2.6 copy-start.17
  460.5 1.0 copy-start.21
  536.5 0.7 copy-start.34
  536.5 269.7 %reduce-scatter.11.cloned.1.call-start = ((), (), s32[]{:S(2)}) async-start(), calls=%async_computation.10 | async-start | bytes 8257536 | tf_op jit(solution)/shard_map/reduce_scatter | solution.py:903
  603.7 1.2 copy-start.15
  605.2 15.1 %collective-permute-start.2 = (bf16[176,2048]{1,0:T(8,128)(2,1)}, bf16[176,2048]{1,0:T(8,128)(2,1)}, u32[]{:S(2)}, u32[]{:S(2)}) collective-permute-start(bf16[176,2048]{1,0:T(8,128)(2,1)} %bitcast.215), channel_id=1, source_target_pairs={{0,1},{1,0},{2,3},{3,2},{4,5},{5,4},{6,7},{7,6},{8,9},{9,8},{10,11... | collective-permute-start | bytes 2162696 | tf_op jit(solution)/shard_map/ppermute | solution.py:907
  606.5 13.9 %copy-start.23 = (bf16[1,176,2048]{2,1,0:T(8,128)(2,1)S(1)}, bf16[1,176,2048]{2,1,0:T(8,128)(2,1)}, u32[]{:S(2)}) copy-start(bf16[1,176,2048]{2,1,0:T(8,128)(2,1)} %reduce-scatter.5.cloned.1.call-done) | copy-start | bytes 2162692
  606.5 15.4 %collective-permute-start = (bf16[128,1024]{1,0:T(8,128)(2,1)}, bf16[128,1024]{1,0:T(8,128)(2,1)S(1)}, u32[]{:S(2)}, u32[]{:S(2)}) collective-permute-start(bf16[128,1024]{1,0:T(8,128)(2,1)} %bitcast.225), channel_id=1, source_target_pairs={{0,0},{2,8},{4,16},{6,24},{8,2},{10,10},{12,18},{14,26},{16,4},{18... | collective-permute-start | bytes 786440 | tf_op jit(solution)/shard_map/ppermute | solution.py:1053
  621.9 2.2 collective-permute-start.1
  798.1 3.9 copy-start.19
  801.5 1.6 copy-start.13
  801.5 1.8 copy-start.18
  834.7 2.8 copy-start.25
  837.5 1.4 copy-start.24
  837.6 3.5 copy-start.1
  839.0 1.4 copy-start.29
Sparse Core Ops, SparseCore 0:
  10.2 30.6 all-gather.5
  170.4 62.7 all-gather.7
  234.8 63.3 all-gather.9
  300.3 59.0 all-gather.11
  361.5 63.5 reduce-scatter.4
  427.3 127.5 reduce-scatter.6
  557.7 34.1 reduce-scatter.8
  603.9 91.2 reduce-scatter.10

commit v3 on v2

v3 whole, which is shorter than its diff:
```python
import functools

import jax
import jax.numpy as jnp
from jax import lax
from jax.sharding import Mesh
from jax.sharding import PartitionSpec as P
from jax.experimental import pallas as pl
from jax.experimental.pallas import tpu as pltpu

HEADS = 4
SLOTS = 64
DEPTH = 512
TILE = 128
EPSILON = 1e-06
F32, BF16 = jnp.float32, jnp.bfloat16
NN = (((1,), (0,)), ((), ()))
NT = (((1,), (1,)), ((), ()))
TN = (((0,), (0,)), ((), ()))
HALVES = (64, 32, 16, 8, 4, 2, 1)
MESH = pl.DeviceIdType.MESH


def cost(us):
    return pl.CostEstimate(flops=0, bytes_accessed=us * 3_000_000, transcendentals=0)


def routes(kind, i, y, x, c):
    chip = {"y": i // 2 % 2, "x": i % 2}
    if kind == "to_homes":
        return {"y": c, "x": i // 2, "c": i % 2}, {**chip, "c": y}, y * 2 + x
    if kind in ("from_homes", "copy_homes"):
        return {**chip, "c": y}, {"y": c, "x": i // 2, "c": i % 2}, x * 2 + c
    return {**chip, "c": c}, {**chip, "c": c}, y * 2 + x


def enter_plane(y, x, c, more=()):
    barrier = pltpu.get_barrier_semaphore()
    peers = list(more)
    for flip in range(1, 8):
        peers.append({
            "y": lax.rem(y + flip // 4, 2), "x": lax.rem(x + (flip // 2) % 2, 2), "c": lax.rem(c + flip % 2, 2)
        })
    for peer in peers:
        pl.semaphore_signal(barrier, inc=1, device_id=peer, device_id_type=MESH)
    pl.semaphore_wait(barrier, len(peers))


def swap_kernel_sems(count):
    return [pltpu.SemaphoreType.DMA((count,)), pltpu.SemaphoreType.DMA((count,))]


def enter_pairs(y, x):
    barrier = pltpu.get_barrier_semaphore()
    for peer in ({"y": 1 - y}, {"x": 1 - x}):
        pl.semaphore_signal(barrier, inc=1, device_id=peer, device_id_type=MESH)
    pl.semaphore_wait(barrier, 2)


def remote(source, target, send, recv, peer):
    return pltpu.make_async_remote_copy(
        src_ref=source, dst_ref=target, send_sem=send, recv_sem=recv, device_id=peer, device_id_type=MESH
    )


class Stay:
    def __init__(self, source, target, sem, buffer):
        self.load = pltpu.make_async_copy(source, buffer, sem)
        self.store = pltpu.make_async_copy(buffer, target, sem)

    def start(self):
        self.load.start()
        self.load.wait()
        self.store.start()

    def wait(self):
        self.store.wait()


class GatherNear:
    def __init__(self, a_ref, out_ref, y, x, send, recv, *local):
        to_x, to_y = {"x": 1 - x}, {"y": 1 - y}
        here = y * 2 + x
        parts = halves_at(a_ref.shape[0])

        def copy(part, n, peer):
            return remote(a_ref.at[parts[part]], out_ref.at[here, parts[part]], send.at[n], recv.at[n], peer)

        self.own = Stay(a_ref, out_ref.at[here], *local)
        self.first, self.second = [copy(0, 0, to_x), copy(1, 1, to_y)], [copy(1, 2, to_x), copy(0, 3, to_y)]
        self.all = self.first + self.second

    def start(self):
        for copy in self.all + [self.own]:
            copy.start()

    def wait(self):
        for copy in self.all:
            copy.wait()
        self.own.wait()


class GatherFar:
    def __init__(self, out_ref, y, x, send, recv):
        at_x, at_y = y * 2 + 1 - x, (1 - y) * 2 + x
        parts = halves_at(out_ref.shape[1])

        def copy(place, part, n, peer):
            block = out_ref.at[place, parts[part]]
            return remote(block, block, send.at[n], recv.at[n], peer)

        self.all = [copy(at_x, 0, 0, {"y": 1 - y}), copy(at_y, 1, 1, {"x": 1 - x})]

    def start(self):
        for copy in self.all:
            copy.start()

    def wait(self):
        for copy in self.all:
            copy.wait()


def halves_at(rows):
    return [pl.ds(0, rows // 2), pl.ds(rows // 2, rows // 2)]


class Gather:
    def __init__(self, a_ref, out_ref, y, x, send, recv, *local):
        self.near = GatherNear(a_ref, out_ref, y, x, send, recv, *local)
        self.far = GatherFar(out_ref, y, x, send.at[pl.ds(4, 2)], recv.at[pl.ds(4, 2)])

    def start(self):
        self.near.start()

    def wait(self):
        for copy, onward in zip(self.near.first, self.far.all):
            copy.wait_recv()
            onward.start()
        for copy in self.near.second + self.far.all:
            copy.wait_recv()
        for copy in self.near.all + self.far.all:
            copy.wait_send()
        self.near.own.wait()


class ReduceNear:
    def __init__(self, a_ref, out_ref, y, x, send, recv):
        parts = halves_at(a_ref.shape[1])
        self.all = []
        for i, (at_y, at_x) in enumerate(((1 - y, 1 - x), (y, x))):
            blocks = (at_y * 2 + 1 - x, (1 - y) * 2 + at_x)
            for part, peer in enumerate(({"x": 1 - x}, {"y": 1 - y})):
                n = 2 * part + i
                self.all.append(
                    remote(a_ref.at[blocks[part], parts[part]], out_ref.at[part, i], send.at[n], recv.at[n], peer)
                )

    def start(self):
        for copy in self.all:
            copy.start()

    def wait(self):
        for copy in self.all:
            copy.wait()


class ReduceFar:
    def __init__(self, a_ref, out_ref, y, x, send, recv):
        self.all = [
            remote(a_ref.at[n], out_ref.at[n], send.at[n], recv.at[n], peer)
            for n, peer in enumerate(({"y": 1 - y}, {"x": 1 - x}))
        ]

    def start(self):
        for copy in self.all:
            copy.start()

    def wait(self):
        for copy in self.all:
            copy.wait()


class Swap:
    def __init__(self, a_ref, out_ref, c, send, recv):
        self.copy = remote(a_ref, out_ref, send.at[0], recv.at[0], {"c": 1 - c})

    def start(self):
        self.copy.start()

    def wait(self):
        self.copy.wait()


class Moves:
    def __init__(self, kind, source, target, y, x, c, send, recv, *local):
        self.copies = []
        for i in range(4):
            peer, giver, slot = routes(kind, i, y, x, c)
            to_me, from_me = (
                (at["y"] == y) & (at["x"] == x) & (at["c"] == c) for at in (peer, giver)
            )
            self.copies.append((
                to_me, from_me,
                Stay(source(i), target(slot), *local),
                remote(source(i), target(slot), send.at[i], recv.at[slot], peer),
                Stay(source(i), target(i), *local),
                remote(source(i), target(i), send.at[i], recv.at[i], peer),
            ))

    def start(self):
        for to_me, _, _, there, _, _ in self.copies:
            pl.when(jnp.logical_not(to_me))(there.start)
        for to_me, _, here, _, _, _ in self.copies:
            pl.when(to_me)(here.start)

    def wait(self):
        for to_me, from_me, _, _, here, there in self.copies:
            pl.when(jnp.logical_not(to_me))(there.wait_send)
            pl.when(jnp.logical_not(from_me))(there.wait_recv)
            pl.when(from_me)(here.wait)


class Spread:
    def __init__(self, a_ref, out_ref, y, x, c, send, recv, *local):
        here, other = y * 2 + x, {"c": 1 - c}
        self.own = Stay(a_ref.at[:, here], out_ref.at[c, here], *local)
        self.across = [remote(a_ref.at[:, here], out_ref.at[c, here], send.at[0], recv.at[0], other)]
        self.sent = []
        for flip in (1, 2, 3):
            peer = {"y": lax.rem(y + flip // 2, 2), "x": lax.rem(x + flip % 2, 2)}
            chip = peer["y"] * 2 + peer["x"]
            self.sent.append(remote(a_ref.at[:, chip], out_ref.at[c, here], send.at[flip], recv.at[flip], peer))
            self.across.append(
                remote(out_ref.at[c, chip], out_ref.at[c, chip], send.at[3 + flip], recv.at[3 + flip], other)
            )

    def start(self):
        for copy in self.sent + [self.across[0], self.own]:
            copy.start()

    def wait(self):
        for copy, onward in zip(self.sent, self.across[1:]):
            copy.wait_recv()
            onward.start()
        for copy in self.across:
            copy.wait()
        for copy in self.sent:
            copy.wait_send()
        self.own.wait()


def move_scratch(kind, a):
    sems = swap_kernel_sems({"spread": 7, "copy_chips": 6}.get(kind, 4)) + [pltpu.SemaphoreType.DMA]
    if kind in ("copy_homes", "copy_chips", "gather_near", "keep"):
        block = a.shape
    elif kind == "spread":
        block = a.shape[:1] + a.shape[2:]
    else:
        block = a.shape[1:] if kind in ("to_homes", "from_homes", "columns") else (16, TILE)
    return sems + [pltpu.VMEM(block, a.dtype)]


def moved(kind, a):
    if kind == "spread":
        return jax.ShapeDtypeStruct((2, 4, a.shape[0]) + a.shape[2:], a.dtype)
    if kind == "reduce_near":
        return jax.ShapeDtypeStruct((2, 2, a.shape[1] // 2) + a.shape[2:], a.dtype)
    if kind in ("swap_core", "keep", "gather_far", "reduce_far"):
        return jax.ShapeDtypeStruct(a.shape, a.dtype)
    block = a.shape if kind in ("copy_homes", "copy_chips", "gather_near") else a.shape[1:]
    return jax.ShapeDtypeStruct((4,) + block, a.dtype)


def one_move(kind, a_ref, out_ref, y, x, c, *sems):
    if kind == "spread":
        return Spread(a_ref, out_ref, y, x, c, *sems)
    if kind == "copy_chips":
        return Gather(a_ref, out_ref, y, x, *sems)
    if kind == "gather_near":
        return GatherNear(a_ref, out_ref, y, x, *sems)
    if kind == "gather_far":
        return GatherFar(out_ref, y, x, *sems[:2])
    if kind in ("reduce_near", "reduce_far"):
        return (ReduceNear if kind == "reduce_near" else ReduceFar)(a_ref, out_ref, y, x, *sems[:2])
    if kind == "swap_core":
        return Swap(a_ref, out_ref, c, *sems[:2])
    if kind == "keep":
        return Stay(a_ref, out_ref, *sems[2:])

    def source(i):
        return a_ref if kind == "copy_homes" else a_ref.at[i]

    return Moves(kind, source, lambda slot: out_ref.at[slot], y, x, c, *sems)


def all_moves(kinds, sources, results, sems, y, x, c):
    return [one_move(kind, sources[n], results[n], y, x, c, *sems[4 * n:4 * n + 4]) for n, kind in enumerate(kinds)]


def compute_body(counts, kinds, grid, body, *refs):
    refs, parts = list(refs), []
    for count in counts:
        parts.append(refs[:count])
        refs = refs[count:]
    operands, sources, _, outs, results, scratch, sems = parts
    if kinds:
        y, x, c = (lax.axis_index(name) for name in ("y", "x", "c"))
        moves = all_moves(kinds, sources, results, sems, y, x, c)
        first, last = True, True
        for axis, size in enumerate(grid):
            first, last = first & (pl.program_id(axis) == 0), last & (pl.program_id(axis) == size - 1)

        def start():
            enter_plane(y, x, c)
            for one in moves:
                one.start()

        def finish():
            for one in moves:
                one.wait()

        pl.when(first)(start) if grid else start()
    body(*operands, *outs, *scratch)
    if kinds:
        pl.when(last)(finish) if grid else finish()


def compute(body, name, operands, in_specs, out_specs, out_shape, us, grid=(), scratch=(), moves=(), collective=None, after=()):
    any_place = pl.BlockSpec(memory_space=pl.ANY)
    kinds = tuple(kind for kind, _ in moves)
    sems = [sem for kind, a in moves for sem in move_scratch(kind, a)]
    counts = (len(operands), len(moves), len(after), len(out_shape), len(moves), len(scratch), len(sems))
    params = {"collective_id": collective, "has_side_effects": True} if moves else {}
    aliases = {len(operands) + n: len(out_shape) + n for n, kind in enumerate(kinds) if kind == "gather_far"}
    return pl.pallas_call(
        functools.partial(compute_body, counts, kinds, grid, body),
        name=name,
        grid=grid,
        in_specs=list(in_specs) + [any_place] * (len(moves) + len(after)),
        out_specs=list(out_specs) + [any_place] * len(moves),
        out_shape=list(out_shape) + [moved(kind, a) for kind, a in moves],
        scratch_shapes=list(scratch) + sems,
        input_output_aliases=aliases,
        compiler_params=pltpu.CompilerParams(vmem_limit_bytes=60 << 20, **params),
        cost_estimate=cost(us),
    )(*operands, *(a for _, a in moves), *after)


def move_kernel(kinds, waits, *refs):
    count = len(kinds)
    sources, results, sems = refs[:count], refs[count + waits:2 * count + waits], refs[2 * count + waits:]
    y, x, c = (lax.axis_index(name) for name in ("y", "x", "c"))
    enter_plane(y, x, c)
    moves = all_moves(kinds, sources, results, sems, y, x, c)
    for one in moves:
        one.start()
    for one in moves:
        one.wait()


def move(collective, *items, after=(), us=48):
    kinds = tuple(kind for kind, _ in items)
    any_place = pl.BlockSpec(memory_space=pl.ANY)
    return pl.pallas_call(
        functools.partial(move_kernel, kinds, len(after)),
        name=kinds[0],
        out_shape=[moved(kind, a) for kind, a in items],
        in_specs=[any_place] * (len(items) + len(after)),
        out_specs=[any_place] * len(items),
        scratch_shapes=[sem for kind, a in items for sem in move_scratch(kind, a)],
        compiler_params=pltpu.CompilerParams(collective_id=collective, has_side_effects=True),
        cost_estimate=cost(us),
    )(*(a for _, a in items), *after)


def start_kernel(kinds, planes, *refs):
    count = len(kinds)
    projections, rest_ref, sources = refs[:3], refs[3], refs[4:4 + count]
    results, m_ref, sems = refs[4 + count:4 + 2 * count], refs[4 + 2 * count], refs[5 + 2 * count:]
    y, x, c, z = (lax.axis_index(name) for name in ("y", "x", "c", "z"))
    up, down = lax.rem(z + 1, planes), lax.rem(z + planes - 1, planes)
    wide = DEPTH // 2
    enter_plane(y, x, c, [{"z": up}, {"z": down}])
    moves = all_moves(kinds, sources, results, sems, y, x, c)
    sems = sems[4 * count:]

    def part(n, source, columns):
        return Moves(
            "columns", source, lambda slot: m_ref.at[c, z, slot, :, columns], y, x, c, *sems[4 * n:4 * n + 4]
        )

    def columns_of(w_ref):
        return lambda i: w_ref.at[:, pl.ds(pl.multiple_of((2 * i + c) * wide, wide), wide)]

    parts = [part(n, columns_of(w_ref), pl.ds(n * wide, wide)) for n, w_ref in enumerate(projections)]
    parts.append(part(3, lambda i: rest_ref.at[i], pl.ds(3 * wide, TILE)))
    m_send, m_recv, core_send, core_recv = sems[16:]

    def block(step):
        return m_ref.at[c, lax.rem(z + planes - step, planes)]

    ring = [
        remote(block(step), block(step), m_send.at[step], m_recv.at[step], {"z": up}) for step in range(planes - 1)
    ]
    across = [
        remote(block(step), block(step), core_send.at[step], core_recv.at[step], {"c": 1 - c}) for step in range(planes)
    ]
    for one in parts:
        one.start()
    for one in parts:
        one.wait()
    ring[0].start()
    across[0].start()
    for one in moves:
        one.start()
    for step in range(planes - 1):
        ring[step].wait_recv()
        if step < planes - 2:
            ring[step + 1].start()
        across[step + 1].start()
    for one in moves:
        one.wait()
    for copy in across:
        copy.wait()
    for copy in ring:
        copy.wait_send()


def start_moves(collective, projections, rest, items):
    planes = lax.axis_size("z")
    kinds = tuple(kind for kind, _ in items)
    any_place = pl.BlockSpec(memory_space=pl.ANY)
    shapes = [moved(kind, a) for kind, a in items]
    shapes.append(jax.ShapeDtypeStruct((2, planes, 4, rest.shape[1], 3 * DEPTH // 2 + TILE), BF16))
    sems = [sem for kind, a in items for sem in move_scratch(kind, a)]
    part = jax.ShapeDtypeStruct((4, rest.shape[1], DEPTH // 2), BF16)
    sems += [sem for a in (part, part, part, rest) for sem in move_scratch("columns", a)]
    sems += swap_kernel_sems(planes) + swap_kernel_sems(planes)
    return pl.pallas_call(
        functools.partial(start_kernel, kinds, planes),
        name="start_moves",
        out_shape=shapes,
        in_specs=[any_place] * (len(items) + 4),
        out_specs=[any_place] * len(shapes),
        scratch_shapes=sems,
        compiler_params=pltpu.CompilerParams(collective_id=collective, has_side_effects=True),
        cost_estimate=cost(85),
    )(*projections, rest, *(a for _, a in items))


def reduce_kernel(a_ref, *refs):
    out_ref, got_ref, sum_ref, last_ref, send, recv = refs[-6:]
    y, x = lax.axis_index("y"), lax.axis_index("x")
    enter_pairs(y, x)
    half = out_ref.shape[0] // 2
    parts = [pl.ds(0, half), pl.ds(half, half)]
    places = [(1 - y, y), (1 - x, x)]
    peers = [{"x": 1 - x}, {"y": 1 - y}]

    def block(part, place, other):
        if part == 0:
            return place * 2 + (1 - x if other else x)
        return (1 - y if other else y) * 2 + place

    def copy(source, target, n, peer):
        return remote(source, target, send.at[n], recv.at[n], peer)

    first = [
        [copy(a_ref.at[block(part, places[part][i], True), parts[part]], got_ref.at[part, i], 2 * part + i, peers[part])
         for i in range(2)] for part in range(2)
    ]
    for i in range(2):
        for part in range(2):
            first[part][i].start()
    onward = [copy(sum_ref.at[part], last_ref.at[part], 4 + part, peers[1 - part]) for part in range(2)]

    def total(part, i):
        own = a_ref[block(part, places[part][i], False), parts[part], :]
        return own.astype(F32) + got_ref[part, i].astype(F32)

    for part in range(2):
        first[part][0].wait_recv()
        sum_ref[part] = total(part, 0).astype(BF16)
        onward[part].start()
    for part in range(2):
        first[part][1].wait_recv()
        out_ref[parts[part], :] = total(part, 1)
    for part in range(2):
        onward[part].wait_recv()
        out_ref[parts[part], :] += last_ref[part].astype(F32)
    for one in first[0] + first[1] + onward:
        one.wait_send()


def reduce_plane(collective, a, after=()):
    rows, features = a.shape[1:]
    half = (rows // 2, features)
    return pl.pallas_call(
        reduce_kernel,
        name="reduce_plane",
        out_shape=jax.ShapeDtypeStruct((rows, features), F32),
        in_specs=[pl.BlockSpec(memory_space=pltpu.VMEM)] + [pl.BlockSpec(memory_space=pl.ANY)] * len(after),
        out_specs=pl.BlockSpec(memory_space=pltpu.VMEM),
        scratch_shapes=[pltpu.VMEM((2, 2) + half, BF16), pltpu.VMEM((2,) + half, BF16), pltpu.VMEM((2,) + half, BF16)]
        + swap_kernel_sems(6),
        compiler_params=pltpu.CompilerParams(collective_id=collective, has_side_effects=True),
        cost_estimate=cost(38),
    )(a, *after)


def add_other(a, other):
    return (a.astype(F32) + other.astype(F32)).astype(BF16)


def halves_of(a, place, axis):
    here = lax.axis_index(axis)
    return [lax.dynamic_index_in_dim(a, at, place, keepdims=False) for at in (here, 1 - here)]


def dot(a, b, dims):
    return lax.dot_general(a, b, dims, preferred_element_type=F32)


def parts_of(a):
    high = a.astype(BF16)
    return high, (a - high.astype(F32)).astype(BF16)


def dot_parts(a, b, dims):
    return dot(a[0], b[0], dims) + (dot(a[1], b[0], dims) + dot(a[0], b[1], dims))


def dot_ones(ones, a):
    high = a.astype(BF16)
    rest = a - high.astype(F32)
    middle = rest.astype(BF16)
    low = (rest - middle.astype(F32)).astype(BF16)
    return dot(ones, high, NN) + (dot(ones, middle, NN) + dot(ones, low, NN))


def places():
    shape = (TILE, TILE)
    return lax.broadcasted_iota(jnp.int32, shape, 0), lax.broadcasted_iota(jnp.int32, shape, 1)


def ones_where(mask):
    return jnp.where(mask, 1.0, 0.0).astype(BF16)


def steps_to_middle(half):
    t, s = places()
    block = 2 * half
    same = (t // block) == (s // block)
    t_right, s_right = (t % block) >= half, (s % block) >= half
    right = t_right & s_right & (s <= t)
    left = jnp.logical_not(t_right | s_right) & (s > t)
    return ones_where(same & (right | left))


def pair_mask(half, turned=False):
    t, s = places()
    if turned:
        t, s = s, t
    block = 2 * half
    return ((t // block) == (s // block)) & ((t % block) >= half) & ((s % block) < half)


def first_row(rows):
    return lax.broadcasted_iota(jnp.int32, (rows, 2 * SLOTS), 1) < SLOTS


def row_sums(a, first):
    return (
        jnp.sum(jnp.where(first, a, 0.0), axis=1, keepdims=True),
        jnp.sum(jnp.where(first, 0.0, a), axis=1, keepdims=True),
    )


def tile_rows(j):
    return pl.ds(pl.multiple_of(j * TILE, TILE), TILE)


def prepare(lf_ref, decay_ref, reach_ref, e_ref, tiles):
    t, s = places()

    @pl.loop(0, tiles)
    def _(j):
        rows = tile_rows(j)
        lf = lf_ref[rows, :]
        decay_ref[rows, :] = dot_ones(ones_where(s <= t), lf)
        reach_ref[rows, :] = dot_ones(ones_where(s > t), lf)
        for level, half in enumerate(HALVES):
            e_ref[level, rows, :] = jnp.exp(dot_ones(steps_to_middle(half), lf))


def far_pairs(tiles):
    out, half = [], tiles // 2
    while half >= 1:
        for start in range(0, tiles, 2 * half):
            out.append((start + half, start, half))
        half //= 2
    return out


def far_decays(right, left, half, decay_ref, reach_ref):
    after, total = [], None
    for j in range(right, right + half):
        part = decay_ref[j * TILE:(j + 1) * TILE, :]
        after.append(jnp.exp(part if total is None else part + total))
        last = part[TILE - 1:TILE, :]
        total = last if total is None else total + last
    before, total = [], None
    for j in range(left + half - 1, left - 1, -1):
        part = reach_ref[j * TILE:(j + 1) * TILE, :]
        before.append(jnp.exp(part if total is None else part + total))
        whole = decay_ref[(j + 1) * TILE - 1:(j + 1) * TILE, :]
        total = whole if total is None else total + whole
    if half == 1:
        return after[0], before[0]
    return jnp.concatenate(after, axis=0), jnp.concatenate(before[::-1], axis=0)


def diagonal_of(block):
    t, s = places()
    return jnp.sum(jnp.where(t == s, block, 0.0), axis=1, keepdims=True)


def weighted_sums(a_ref, out_ref, gain_ref, decay_ref, reach_ref, e_ref, tiles):
    first = first_row(TILE)

    @pl.loop(0, tiles)
    def _(j):
        rows = tile_rows(j)
        gain = gain_ref[rows, :]
        blocks = [a_ref[r, rows, rows] for r in range(2)]
        total = jnp.where(first, diagonal_of(blocks[0]), diagonal_of(blocks[1])) * gain
        for level, half in enumerate(HALVES):
            e = e_ref[level, rows, :]
            x = parts_of(e * gain)
            pairs = pair_mask(half)
            y = [dot_parts(parts_of(jnp.where(pairs, a, 0.0)), x, NN) for a in blocks]
            total = total + e * jnp.where(first, y[0], y[1])
        out_ref[rows, :] = total

    for right, left, half in far_pairs(tiles):
        after, before = far_decays(right, left, half, decay_ref, reach_ref)
        here = slice(right * TILE, (right + half) * TILE)
        there = slice(left * TILE, (left + half) * TILE)
        x = parts_of(before * gain_ref[there, :])
        y = [dot_parts(parts_of(a_ref[r, here, there]), x, NN) for r in range(2)]
        out_ref[here, :] += after * jnp.where(first_row(half * TILE), y[0], y[1])


def split_rows(a, first):
    return parts_of(jnp.where(first, a, 0.0)), parts_of(jnp.where(first, 0.0, a))


def paired_weights(p_ref, out_ref, gain_ref, decay_ref, reach_ref, e_ref, tiles):
    first = first_row(TILE)
    t, s = places()

    @pl.loop(0, tiles)
    def _(j):
        rows = tile_rows(j)
        gain, p = gain_ref[rows, :], p_ref[rows, :]
        sums = row_sums(p * gain, first)
        total = [jnp.where(t == s, sums[r], 0.0) for r in range(2)]
        for level, half in enumerate(HALVES):
            e = e_ref[level, rows, :]
            x = parts_of(e * gain)
            pairs = pair_mask(half)
            pe = split_rows(p * e, first)
            total = [total[r] + jnp.where(pairs, dot_parts(pe[r], x, NT), 0.0) for r in range(2)]
        for r in range(2):
            out_ref[r, rows, rows] = total[r]

    for right, left, half in far_pairs(tiles):
        after, before = far_decays(right, left, half, decay_ref, reach_ref)
        here = slice(right * TILE, (right + half) * TILE)
        there = slice(left * TILE, (left + half) * TILE)
        x = parts_of(before * gain_ref[there, :])
        pe = split_rows(p_ref[here, :] * after, first_row(half * TILE))
        for r in range(2):
            out_ref[r, here, there] = dot_parts(pe[r], x, NT)
            out_ref[r, there, here] = jnp.zeros((half * TILE, half * TILE), F32)


def inner(a, b, r):
    return dot(a[0][r], b[0][r], NT) + dot(a[1][r], b[1][r], NT)


def sigmoid(v):
    return 1.0 / (1.0 + jnp.exp(-v))


def projections(pre_ref, which, length, act):
    depth = DEPTH // 2
    return [
        [act(pre_ref[f, r * length:(r + 1) * length, which * depth:(which + 1) * depth]) for r in range(2)]
        for f in range(2)
    ]


def silu_low(v):
    return (v * sigmoid(v)).astype(BF16)


def low(v):
    return v.astype(BF16)


def forward_kernel(pre_ref, lf_ref, gain_ref, dcol_ref, drow_ref,
                   mixed_ref, s_ref, p_ref, b_ref, a_ref, decay_ref, reach_ref, e_ref):
    length = lf_ref.shape[0]
    tiles = length // TILE
    scale = DEPTH ** -0.5
    q, k = projections(pre_ref, 0, length, silu_low), projections(pre_ref, 1, length, silu_low)
    for r in range(2):
        same = dcol_ref[r] == drow_ref[r]
        a_ref[r] = jnp.where(same, inner(q, k, r), 0.0)
    prepare(lf_ref, decay_ref, reach_ref, e_ref, tiles)
    weighted_sums(a_ref, s_ref, gain_ref, decay_ref, reach_ref, e_ref, tiles)
    first = first_row(length)
    logits = s_ref[...] * scale
    least = -jnp.inf
    top = jnp.where(
        first,
        jnp.max(jnp.where(first, logits, least), axis=1, keepdims=True),
        jnp.max(jnp.where(first, least, logits), axis=1, keepdims=True),
    )
    grown = jnp.exp(logits - top)
    sums = row_sums(grown, first)
    p_ref[...] = grown / jnp.where(first, sums[0], sums[1])
    paired_weights(p_ref, b_ref, gain_ref, decay_ref, reach_ref, e_ref, tiles)
    v = projections(pre_ref, 2, length, low)
    for r in range(2):
        b = jnp.where(dcol_ref[r] == drow_ref[r], b_ref[r], 0.0)
        b_ref[r] = b
        high, rest = parts_of(b)
        for f in range(2):
            mixed = (dot(high, v[f][r], NN) + dot(rest, v[f][r], NN)).astype(BF16)
            for place in range(2):
                mixed_ref[r, place, f] = mixed[place * length // 2:(place + 1) * length // 2]


def to_columns(r, f):
    t, s = places()
    half = SLOTS // 2
    return ones_where((s < half) & (t == s + r * SLOTS + f * half))


def backward_kernel(pre_ref, g_ref, lf_ref, gain_ref, rate_ref, dcol_ref, drow_ref, s_ref, p_ref, b_ref,
                    out_ref, bias_ref, a_ref, at_ref, dot_ref, h_ref, back_ref, decay_ref, reach_ref, e_ref):
    length = lf_ref.shape[0]
    tiles, depth = length // TILE, DEPTH // 2
    scale = DEPTH ** -0.5
    first_all, first = first_row(length), first_row(TILE)
    t, s = places()
    q, k = projections(pre_ref, 0, length, silu_low), projections(pre_ref, 1, length, silu_low)
    v = projections(pre_ref, 2, length, low)
    grads = [[g_ref[r, :, f].reshape(length, depth) for r in range(2)] for f in range(2)]
    for r in range(2):
        same = dcol_ref[r] == drow_ref[r]
        a_ref[r] = jnp.where(same, inner(grads, v, r), 0.0)
        at_ref[0, r] = jnp.where(same, inner(k, q, r), 0.0)
        at_ref[1, r] = jnp.where(same, inner(v, grads, r), 0.0)
    prepare(lf_ref, decay_ref, reach_ref, e_ref, tiles)
    weighted_sums(a_ref, dot_ref, gain_ref, decay_ref, reach_ref, e_ref, tiles)
    p, dots = p_ref[...], dot_ref[...]
    sums = row_sums(p * dots, first_all)
    h = scale * (p * (dots - jnp.where(first_all, sums[0], sums[1])))
    h_ref[...] = h
    dot_ref[...] = h * s_ref[...] + p * dots
    paired_weights(h_ref, a_ref, gain_ref, decay_ref, reach_ref, e_ref, tiles)
    @pl.loop(0, tiles)
    def _(j):
        rows = tile_rows(j)
        h, p = h_ref[rows, :], p_ref[rows, :]
        keys = [at_ref[0, r, rows, rows] for r in range(2)]
        values = [at_ref[1, r, rows, rows] for r in range(2)]
        total = (
            jnp.where(first, diagonal_of(keys[0]), diagonal_of(keys[1])) * h
            + jnp.where(first, diagonal_of(values[0]), diagonal_of(values[1])) * p
        )
        for level, half in enumerate(HALVES):
            e = e_ref[level, rows, :]
            he, pe = parts_of(h * e), parts_of(p * e)
            pairs = pair_mask(half, turned=True)
            y = [
                dot_parts(parts_of(jnp.where(pairs, keys[r], 0.0)), he, NN)
                + dot_parts(parts_of(jnp.where(pairs, values[r], 0.0)), pe, NN)
                for r in range(2)
            ]
            total = total + e * jnp.where(first, y[0], y[1])
        back_ref[rows, :] = total

    for right, left, half in far_pairs(tiles):
        after, before = far_decays(right, left, half, decay_ref, reach_ref)
        here = slice(right * TILE, (right + half) * TILE)
        there = slice(left * TILE, (left + half) * TILE)
        he, pe = parts_of(h_ref[here, :] * after), parts_of(p_ref[here, :] * after)
        y = [
            dot_parts(parts_of(at_ref[0, r, there, here]), he, NN)
            + dot_parts(parts_of(at_ref[1, r, there, here]), pe, NN)
            for r in range(2)
        ]
        back_ref[there, :] += before * jnp.where(first_row(half * TILE), y[0], y[1])

    for r in range(2):
        rows = slice(r * length, (r + 1) * length)
        c = parts_of(jnp.where(dcol_ref[r] == drow_ref[r], a_ref[r], 0.0))
        w = parts_of(b_ref[r])
        for f in range(2):
            gq = dot(c[0], k[f][r], NN) + dot(c[1], k[f][r], NN)
            out_ref[f, rows, :depth] = (gq * slope(pre_ref[f, rows, :depth])).astype(BF16)
            gk = dot(c[0], q[f][r], TN) + dot(c[1], q[f][r], TN)
            out_ref[f, rows, depth:2 * depth] = (gk * slope(pre_ref[f, rows, depth:2 * depth])).astype(BF16)
            gv = dot(w[0], grads[f][r], TN) + dot(w[1], grads[f][r], TN)
            out_ref[f, rows, 2 * depth:3 * depth] = gv.astype(BF16)
    carried = jnp.zeros((1, 2 * SLOTS), F32)
    for j in range(tiles - 1, -1, -1):
        rows = slice(j * TILE, (j + 1) * TILE)
        back = back_ref[rows, :]
        change = dot_ref[rows, :] - gain_ref[rows, :] * back
        upward = dot_ones(ones_where(s >= t), change) + carried
        h_ref[rows, :] = (upward - jnp.exp(lf_ref[rows, :]) * back) * rate_ref[rows, :]
        carried = upward[0:1, :]
    grad_z = h_ref[...]
    bias_ref[...] = jnp.broadcast_to(jnp.sum(grad_z, axis=0, keepdims=True), bias_ref.shape)
    for r in range(2):
        for f in range(2):
            out_ref[f, r * length:(r + 1) * length, 3 * depth:] = dot(grad_z.astype(BF16), to_columns(r, f), NN).astype(BF16)


def slope(v):
    s = sigmoid(v)
    return s * (1.0 + v * (1.0 - s))


def mix_forward(pre, lf, gain, doc, moves, collective):
    length = lf.shape[0]
    lanes = (length, 2 * SLOTS)
    square = (2, length, length)
    in_vmem = pl.BlockSpec(memory_space=pltpu.VMEM)
    return compute(
        forward_kernel, "mix_forward", (pre, lf, gain, doc[:, :, None], doc[:, None, :]), [in_vmem] * 5, [in_vmem] * 4,
        (
            jax.ShapeDtypeStruct((2, 2, 2, length // 2, DEPTH // 2), BF16), jax.ShapeDtypeStruct(lanes, F32),
            jax.ShapeDtypeStruct(lanes, F32), jax.ShapeDtypeStruct(square, F32),
        ),
        24, scratch=[
            pltpu.VMEM(square, F32), pltpu.VMEM(lanes, F32), pltpu.VMEM(lanes, F32),
            pltpu.VMEM((len(HALVES),) + lanes, F32),
        ],
        moves=moves, collective=collective,
    )


def mix_backward(pre, g, lf, gain, rate, doc, s, p, b, moves, collective):
    length = lf.shape[0]
    lanes = (length, 2 * SLOTS)
    square = (2, length, length)
    in_vmem = pl.BlockSpec(memory_space=pltpu.VMEM)
    return compute(
        backward_kernel, "mix_backward", (pre, g, lf, gain, rate, doc[:, :, None], doc[:, None, :], s, p, b),
        [in_vmem] * 10, [in_vmem] * 2,
        (jax.ShapeDtypeStruct(pre.shape, BF16), jax.ShapeDtypeStruct((8, 2 * SLOTS), F32)), 30,
        scratch=[pltpu.VMEM(square, F32), pltpu.VMEM((2,) + square, F32)] + [pltpu.VMEM(lanes, F32)] * 5
        + [pltpu.VMEM((len(HALVES),) + lanes, F32)],
        moves=moves, collective=collective,
    )


def hidden_kernel(nf_ref, w_ref, hidden_ref, slope_ref, silu_ref):
    units = hidden_ref.shape[2]
    both = dot(nf_ref[...], w_ref[0], NN)
    gate, up = both[:, :units], both[:, units:]
    s = sigmoid(gate)
    silu = gate * s
    hidden_ref[0] = (silu * up).astype(BF16)
    slope_ref[0] = (up * (s * (1.0 + gate * (1.0 - s)))).astype(BF16)
    silu_ref[0] = silu.astype(BF16)


def unit_specs(tokens, features, units):
    rows = tokens // 2
    return (
        pl.BlockSpec((rows, features), lambda h, t: (t, 0)),
        pl.BlockSpec((1, features, 2 * units), lambda h, t: (h, 0, 0)),
        pl.BlockSpec((1, rows, units), lambda h, t: (h, t, 0)),
        jax.ShapeDtypeStruct((2, tokens, units), BF16),
    )


def hidden_units(nf, w, moves, collective):
    some, weight, unit, units_all = unit_specs(*nf.shape, w.shape[2] // 2)
    return compute(
        hidden_kernel, "hidden_units", (nf, w), [some, weight], [unit] * 3, [units_all] * 3, 22, grid=(2, 2),
        moves=moves, collective=collective,
    )


def hidden_grads_kernel(cot_ref, slope_ref, silu_ref, w_ref, wd_ref, grads_ref, back_ref, total_ref):
    half, tile = pl.program_id(0), pl.program_id(1)
    rows = cot_ref.shape[0]
    here = pl.ds(pl.multiple_of(tile * rows, rows), rows)
    grad = dot(cot_ref[...], wd_ref[0], NT)
    gate_up = [grad * slope_ref[0].astype(F32), grad * silu_ref[0].astype(F32)]
    grads = jnp.concatenate(gate_up, axis=1).astype(BF16)
    grads_ref[0] = grads
    back = dot(grads, w_ref[0], NT)

    @pl.when(half == 0)
    def _():
        total_ref[here, :] = back

    @pl.when(half == 1)
    def _():
        back_ref[...] = (total_ref[here, :] + back).astype(BF16)


def hidden_grads(cot, slopes, silus, w, wd, moves, collective):
    tokens, features = cot.shape
    units = slopes.shape[2]
    some, weight, unit, _ = unit_specs(tokens, features, units)
    return compute(
        hidden_grads_kernel, "hidden_grads", (cot, slopes, silus, w, wd),
        [some, unit, unit, weight, pl.BlockSpec((1, units, features), lambda h, t: (h, 0, 0))],
        [
            pl.BlockSpec((1, tokens // 2, 2 * units), lambda h, t: (h, t, 0)),
            pl.BlockSpec((tokens // 2, features), lambda h, t: (h * t, 0)),
        ],
        [jax.ShapeDtypeStruct((2, tokens, 2 * units), BF16), jax.ShapeDtypeStruct(cot.shape, BF16)],
        45, grid=(2, 2), scratch=[pltpu.VMEM((tokens, features), F32)], moves=moves, collective=collective,
    )


def out_kernel(a_ref, b_ref, out_ref):
    grads = dot(a_ref[...], b_ref[0], TN).astype(BF16)
    wide = grads.shape[1] // 2
    for f in range(2):
        out_ref[0, f] = grads[:, f * wide:(f + 1) * wide]


def out_grads(a, b):
    planes = lax.axis_size("z")
    tokens, depth = a.shape
    features = b.shape[2]
    rows = max(depth // planes, TILE)
    grads = pl.pallas_call(
        out_kernel,
        name="out_grads",
        grid=(depth // rows,),
        in_specs=[
            pl.BlockSpec((tokens, rows), lambda i: (0, i)), pl.BlockSpec((1, tokens, features), lambda i: (0, 0, 0)),
        ],
        out_specs=pl.BlockSpec((1, 2, rows, features // 2), lambda i: (i, 0, 0, 0)),
        out_shape=jax.ShapeDtypeStruct((depth // rows, 2, rows, features // 2), BF16),
        compiler_params=pltpu.CompilerParams(vmem_limit_bytes=60 << 20),
        cost_estimate=cost(8),
    )(a, b)
    if rows * planes > depth:
        grads = grads.reshape(-1, 2, rows * planes // depth, depth // planes, features // 2).transpose(0, 2, 1, 3, 4)
    return grads.reshape(planes, 2, depth // planes, features // 2)


def weight_kernel(a_ref, b_ref, out_ref):
    out_ref[0, 0] = dot(a_ref[...], b_ref[0], TN).astype(BF16)


def weight_sums_kernel(a_ref, b_ref, sums_ref, out_ref):
    grads = dot(a_ref[...], b_ref[0], TN)
    wide = grads.shape[1]
    out_ref[0, 0, :, :wide - TILE] = grads[:, :wide - TILE].astype(BF16)
    once = jnp.where(pl.program_id(0) == 0, 1.0, 0.0)
    out_ref[0, 0, :, wide - TILE:] = (grads[:, wide - TILE:] + once * sums_ref[...]).astype(BF16)


def weight_grads(a, b, us, sums=None, moves=(), collective=None, after=()):
    planes = lax.axis_size("z")
    tokens, features = a.shape
    rows, columns = features // planes, b.shape[2]
    specs = [pl.BlockSpec((tokens, rows), lambda h, z: (0, z)), pl.BlockSpec((1, tokens, columns), lambda h, z: (h, 0, 0))]
    body, operands = weight_kernel, (a, b)
    if sums is not None:
        body, operands = weight_sums_kernel, (a, b, sums)
        specs.append(pl.BlockSpec((rows, TILE), lambda h, z: (z, 0)))
    out = compute(
        body, "weight_grads", operands, specs, [pl.BlockSpec((1, 1, rows, columns), lambda h, z: (z, h, 0, 0))],
        [jax.ShapeDtypeStruct((planes, 2, rows, columns), BF16)], us, grid=(2, planes),
        moves=moves, collective=collective, after=after,
    )
    return out if moves else out[0]


def down_kernel(hidden_ref, cot_ref, out_ref):
    grads = dot(hidden_ref[0], cot_ref[...], TN)
    rows = out_ref.shape[2]
    for z in range(out_ref.shape[0]):
        out_ref[z, 0] = grads[z * rows:(z + 1) * rows].astype(BF16)


def down_grads(hidden, cot):
    planes = lax.axis_size("z")
    tokens, features = cot.shape
    units = hidden.shape[2]
    wide = features // 2
    return pl.pallas_call(
        down_kernel,
        name="down_grads",
        grid=(2, 2),
        in_specs=[
            pl.BlockSpec((1, tokens, units), lambda h, i: (h, 0, 0)),
            pl.BlockSpec((tokens, wide), lambda h, i: (0, i)),
        ],
        out_specs=pl.BlockSpec((planes, 1, units // planes, wide), lambda h, i: (0, h, 0, i)),
        out_shape=jax.ShapeDtypeStruct((planes, 2, units // planes, features), BF16),
        compiler_params=pltpu.CompilerParams(vmem_limit_bytes=60 << 20),
        cost_estimate=cost(12),
    )(hidden, cot)


def input_kernel(grad_ref, w_ref, x_ref, out_ref, sums_ref):
    tile = pl.program_id(0)
    back = dot(grad_ref[0], w_ref[0], NT) + dot(grad_ref[1], w_ref[1], NT)
    out_ref[...] = back.astype(BF16)
    x = x_ref[...].astype(F32)
    xh = x * lax.rsqrt(jnp.mean(x * x, axis=1, keepdims=True) + EPSILON)
    sums = jnp.sum((back * xh).reshape(-1, 8, back.shape[1]), axis=0)
    sums_ref[...] = jnp.where(tile == 0, sums, sums_ref[...] + sums)


def input_grads(grad, w, x, moves, collective, after):
    tokens, features = x.shape
    rows = tokens // 4
    return compute(
        input_kernel, "input_grads", (grad, w, x),
        [
            pl.BlockSpec((2, rows, grad.shape[2]), lambda t: (0, t, 0)), pl.BlockSpec(w.shape, lambda t: (0, 0, 0)),
            pl.BlockSpec((rows, features), lambda t: (t, 0)),
        ],
        [pl.BlockSpec((rows, features), lambda t: (t, 0)), pl.BlockSpec((8, features), lambda t: (0, 0))],
        [jax.ShapeDtypeStruct(x.shape, BF16), jax.ShapeDtypeStruct((8, features), F32)],
        20, grid=(4,), moves=moves, collective=collective, after=after,
    )


def project_kernel(x_ref, gain_ref, w_ref, normed_ref, pre_ref):
    x = x_ref[...].astype(F32)
    ratio = lax.rsqrt(jnp.mean(x * x, axis=1, keepdims=True) + EPSILON)
    normed = (x * ratio * gain_ref[...]).astype(BF16)
    normed_ref[...] = normed
    for f in range(2):
        pre_ref[f] = dot(normed, w_ref[f], NN)


def project(x, gain, w, moves, collective):
    tokens, features = x.shape
    rows, columns = tokens // 4, w.shape[2]
    some = pl.BlockSpec((rows, features), lambda t: (t, 0))
    return compute(
        project_kernel, "project", (x, gain, w),
        [some, pl.BlockSpec((1, features), lambda t: (0, 0)), pl.BlockSpec(w.shape, lambda t: (0, 0, 0))],
        [some, pl.BlockSpec((2, rows, columns), lambda t: (0, t, 0))],
        [jax.ShapeDtypeStruct(x.shape, BF16), jax.ShapeDtypeStruct((2, tokens, columns), F32)],
        28, grid=(4,), moves=moves, collective=collective,
    )


def gather_planes(a):
    return lax.all_gather(a, ("c", "z"), axis=0, tiled=True).reshape((2, -1) + a.shape[1:])


def sum_planes(a):
    return lax.psum_scatter(a.reshape((-1,) + a.shape[2:]), ("z", "c"), scatter_dimension=0, tiled=True)[0]


def swap(a, axis):
    return lax.ppermute(a, axis, [(0, 1), (1, 0)])


def both_of(a, axis):
    other = swap(a, axis)
    return jnp.where(lax.axis_index(axis) == 0, jnp.stack([a, other]), jnp.stack([other, a]))


def scaled(features):
    return lax.rsqrt(jnp.mean(features * features, axis=-1, keepdims=True) + EPSILON)


def norm_back(grad, gain, features, ratio):
    u, xh = grad * gain, features * ratio
    return ratio * (u - xh * jnp.mean(u * xh, axis=-1, keepdims=True))


def body(inputs, starts, norm_attn, w_query, w_key, w_value, w_forget, gate_bias, w_out, norm_ffn, w_gate, w_up,
         w_down, cotangent):
    positions, features = inputs.shape[1:]
    depth = features // HEADS
    y, x, c, z = (lax.axis_index(name) for name in ("y", "x", "c", "z"))
    planes = lax.axis_size("z")
    head = y * 2 + x
    rows_here = w_query.shape[0]
    hidden_here = w_down.shape[0]

    def own_half(a, axis, at=c):
        return lax.dynamic_index_in_dim(a, at, axis, keepdims=False)

    bias_here = gate_bias.shape[0]

    def column(v):
        v = jnp.pad(v, (0, rows_here - v.shape[0]))
        return jnp.broadcast_to(v[None, :, None], (HEADS, rows_here, 1))

    forget = own_half(w_forget.reshape(rows_here, HEADS, 2, SLOTS // 2), 2).transpose(1, 0, 2)
    rest = jnp.concatenate([forget] + [column(v) for v in (norm_attn, norm_ffn, gate_bias)], axis=-1)
    rest = jnp.pad(rest, ((0, 0), (0, 0), (0, TILE - rest.shape[-1])))
    vectors = 3 * depth // 2 + SLOTS // 2
    width = vectors + 3

    def hidden_columns(w):
        w = own_half(w.reshape(rows_here, planes, 4, 2, hidden_here // 2), 3)
        return w.transpose(2, 0, 1, 3).reshape(4, rows_here, -1)

    x_here = inputs.reshape(positions, features)
    cot_here = cotangent.reshape(positions, features)
    out_half = own_half(w_out.reshape(2, rows_here // 2, features), 0)
    out_half = lax.all_gather(out_half, "z", axis=0)
    full_down = gather_planes(own_half(w_down.reshape(2, hidden_here // 2, features), 0))
    begins, x_rows, hidden_w, mixer_w = start_moves(1, (w_query, w_key, w_value), rest, (
        ("copy_homes", jnp.broadcast_to(starts, (8, positions))), ("copy_homes", x_here),
        ("columns", jnp.concatenate([hidden_columns(w_gate), hidden_columns(w_up)], axis=-1)),
    ))
    hidden_w = gather_planes(hidden_w.reshape(4 * rows_here, -1))
    mixer_w = mixer_w.reshape(2, features, -1)
    gain_attn, gain_ffn = (mixer_w[0, :, vectors + i].astype(F32) for i in range(2))
    bias = mixer_w[0, :, vectors + 2].reshape(4 * planes, rows_here)[:, :bias_here].reshape(-1).astype(F32)
    bias = lax.dynamic_slice_in_dim(bias, head * SLOTS, SLOTS)
    doc = jnp.cumsum(begins[:, 0].reshape(2, 2 * positions).astype(F32), axis=1)

    x_rows = x_rows.reshape(4 * positions, features)
    normed, pre, out_core = project(x_rows, gain_attn[None], mixer_w, [("copy_chips", out_half)], 13)
    z_total = pre[:, :, 3 * depth // 2:vectors].reshape(2, 2, 2 * positions, SLOTS // 2)
    z_total = z_total.transpose(2, 1, 0, 3).reshape(2 * positions, 2 * SLOTS) + jnp.tile(bias, 2)
    log_forget = jax.nn.log_sigmoid(z_total) / 8.0
    gain = -jnp.expm1(log_forget)
    mixed, scores, probs, paired, out_other, cot = mix_forward(
        pre, log_forget, gain, doc, [("swap_core", out_core), ("gather_near", cot_here)], 3
    )
    out_core, out_other = (a.reshape(features // 2, features) for a in (out_core, out_other))
    other = swap(own_half(mixed, 1, 1 - c), "c")
    own = own_half(mixed, 1)
    mixed_chips = jnp.where(c == 0, jnp.stack([own, other]), jnp.stack([other, own]))
    mixed_chips = mixed_chips.transpose(0, 1, 3, 2, 4).reshape(4 * positions, depth)
    (mixed,) = move(4, ("to_homes", mixed.reshape(4, 2 * positions, depth // 2)), us=14)
    mixed = mixed.reshape(2 * HEADS, positions, depth // 2).transpose(1, 0, 2)
    mixed = mixed.reshape(positions, planes, 4, 2, rows_here // 2).transpose(3, 0, 2, 1, 4)
    mixed = mixed.reshape(2, positions, features // 2)
    attended = (
        x_here.astype(F32) + jnp.dot(own_half(mixed, 0), out_core, preferred_element_type=F32)
        + jnp.dot(own_half(mixed, 0, 1 - c), out_other, preferred_element_type=F32)
    )

    ratio_f = scaled(attended)
    (normed_ffn,) = move(5, ("copy_chips", (attended * ratio_f * gain_ffn).astype(BF16)), us=38)
    normed_ffn = normed_ffn.reshape(4 * positions, features)
    hidden, slopes, silus, cot = hidden_units(normed_ffn, hidden_w, [("gather_far", cot)], 6)
    cot = cot.reshape(4 * positions, features)
    grad_down_w = down_grads(hidden, cot)
    block_out = jnp.einsum("ctf,cfd->td", hidden, full_down, preferred_element_type=F32).astype(BF16)
    block_out = block_out.reshape(2, 2, positions, features)
    grad_hidden, grad_normed_ffn, near = hidden_grads(
        cot, slopes, silus, hidden_w, full_down, [("reduce_near", block_out.reshape(4, positions, features))], 7
    )
    half = positions // 2
    own = [
        lax.dynamic_index_in_dim(block_out[:, :, :half], x, 1, keepdims=False),
        lax.dynamic_index_in_dim(block_out[:, :, half:], y, 0, keepdims=False),
    ]
    own = [jnp.where(at == 0, a[::-1], a) for at, a in zip((y, x), own)]
    near = jnp.stack(own).astype(F32) + near.astype(F32)
    grad_hidden_w, far = weight_grads(
        normed_ffn, grad_hidden, 22, moves=[("reduce_far", near[:, 0].astype(BF16))], collective=15
    )
    block_out = (near[:, 1] + far.astype(F32)).reshape(positions, features)
    output = (attended + block_out).astype(BF16)
    grad_normed_ffn = reduce_plane(
        8, grad_normed_ffn.reshape(4, positions, features), after=(grad_down_w, grad_hidden_w)
    )
    grad_down_w, grad_hidden_w = sum_planes(grad_down_w), sum_planes(grad_hidden_w)
    grad_gain_ffn = jnp.sum(grad_normed_ffn * attended * ratio_f, axis=0)
    grad_attended = cot_here.astype(F32) + norm_back(grad_normed_ffn, gain_ffn, attended, ratio_f)

    grad_branch = grad_attended.astype(BF16)
    grad_mixed = [
        jnp.einsum("te,de->td", grad_branch, w, preferred_element_type=F32).astype(BF16) for w in (out_core, out_other)
    ]
    grad_mixed = jnp.where(c == 0, jnp.stack(grad_mixed), jnp.stack(grad_mixed[::-1]))
    grad_mixed = grad_mixed.reshape(2, positions, 4, planes, rows_here // 2).transpose(1, 3, 2, 0, 4)
    grad_mixed = grad_mixed.reshape(positions, HEADS, 2, depth // 2).transpose(1, 2, 0, 3)
    (grad_mixed,) = move(
        9, ("from_homes", grad_mixed.reshape(4, 2 * positions, depth // 2)), after=(grad_down_w,), us=14
    )
    grad_mixed = grad_mixed.reshape(2, 2, 2, positions, depth // 2)
    rate = jax.nn.sigmoid(-z_total) / 8.0
    grad_pre, grad_bias, branch_chips = mix_backward(
        pre, grad_mixed, log_forget, gain, rate, doc, scores, probs, paired, [("copy_chips", grad_branch)], 10
    )
    grad_bias = jnp.sum(grad_bias[0].reshape(2, SLOTS), axis=0)
    grad_out_w = out_grads(mixed_chips, branch_chips.reshape(1, 4 * positions, features))
    grad_normed, sums, grad_hidden_w = input_grads(
        grad_pre, mixer_w, x_rows, [("spread", grad_hidden_w.reshape(1, 4, rows_here, -1))], 14, (grad_out_w,)
    )
    grad_bias = jnp.zeros((HEADS, SLOTS), F32).at[head].set(grad_bias).reshape(4 * planes, bias_here)
    grad_bias = jnp.pad(grad_bias, ((0, 0), (0, rows_here - bias_here))).reshape(-1)
    sums = jnp.stack([jnp.sum(sums, axis=0), grad_gain_ffn, grad_bias], axis=-1)
    first_sum = vectors + TILE - mixer_w.shape[-1]
    sums = jnp.pad(sums, ((0, 0), (first_sum, TILE - first_sum - 3)))
    grad_mixer_w = weight_grads(normed, grad_pre, 15, sums=sums)
    grad_out_w = sum_planes(grad_out_w)
    grad_normed, grad_out_w = move(
        11, ("to_homes", grad_normed.reshape(4, positions, features)), ("keep", grad_out_w), after=(grad_mixer_w,), us=48
    )
    grad_mixer_w = sum_planes(grad_mixer_w)
    grad_normed_here = jnp.sum(grad_normed.astype(F32), axis=0)
    x_here = x_here.astype(F32)
    ratio_a = scaled(x_here)
    grad_input = grad_attended + norm_back(grad_normed_here, gain_attn, x_here, ratio_a)

    grad_hidden_w = grad_hidden_w.reshape(2, 4, rows_here, 2, planes, hidden_here // 2)
    grad_hidden_w = grad_hidden_w.transpose(3, 2, 4, 1, 0, 5).reshape(2, rows_here, -1)
    grad_gate_w, grad_up_w = grad_hidden_w[0].astype(F32), grad_hidden_w[1].astype(F32)
    blocks = 4 * planes
    grad_out_w = lax.ppermute(
        grad_out_w, ("z", "y", "x"), [(at, at % 4 * planes + at // 4) for at in range(blocks)]
    )
    grad_out_w = both_of(grad_out_w, "c").transpose(1, 0, 2).reshape(rows_here, features).astype(F32)
    grad_down_w = both_of(grad_down_w, "c").reshape(hidden_here, features).astype(F32)
    (grad_mixer_w,) = move(12, ("spread", grad_mixer_w.reshape(1, 4, rows_here, -1)), us=18)
    grad_mixer_w = grad_mixer_w[:, :, 0]
    sums = jnp.sum(grad_mixer_w[0, :, :, vectors:width].astype(F32), axis=0)
    grad_mixer_w = grad_mixer_w.transpose(2, 1, 0, 3)
    grad_w = [
        grad_mixer_w[..., i * depth // 2:(i + 1) * depth // 2].reshape(rows_here, features).astype(F32) for i in range(3)
    ]
    grad_forget_w = grad_mixer_w[..., 3 * depth // 2:vectors].reshape(rows_here, HEADS * SLOTS).astype(F32)
    return (
        output.reshape(inputs.shape), grad_input.reshape(inputs.shape), sums[:, 0], grad_w[0], grad_w[1], grad_w[2],
        grad_forget_w, sums[:bias_here, 2], grad_out_w, sums[:, 1], grad_gate_w, grad_up_w, grad_down_w,
    )


def solution(mesh):
    planes = mesh.shape["dp"] // 4
    fine = Mesh(mesh.devices.reshape(planes, 2, 2, 2), ("z", "y", "x", "c"))
    dp = ("z", "y", "x")
    tokens, vector, matrix = P(dp, "c", None), P(dp), P(dp, None)
    in_specs = (
        tokens, P(dp, "c"), vector, matrix, matrix, matrix, matrix, vector, matrix, vector, matrix, matrix, matrix, tokens
    )
    out_specs = (
        tokens, tokens, vector, matrix, matrix, matrix, matrix, vector, matrix, vector, matrix, matrix, matrix
    )
    return jax.shard_map(body, mesh=fine, in_specs=in_specs, out_specs=out_specs, check_vma=False)
```

time: 856 us -> 700 us (0.82)
  Pallas kernels: 661 us -> 530 us
  local copies, waits for them, and re-layouts: 87.3 us -> 76.8 us
  matrix products: 33.2 us -> 23.4 us
    pallas_call x5, Pallas kernels: 215 us -> 147 us  [move(): pl.pallas_call(functools.partial(move_kernel, kinds, len(after)), name=ki...]
    pallas_call x1, Pallas kernels: 129 us -> 82.6 us  [start_moves(): pl.pallas_call(functools.partial(start_kernel, kinds, planes), name='star...]
    pallas_call x2 -> x1, Pallas kernels: 81.6 us -> 40.2 us  [reduce_plane(): pl.pallas_call(reduce_kernel, name='reduce_plane', out_shape=jax.ShapeDty...]
    pallas_call x8, Pallas kernels: 218 us -> 242 us  [compute(): pl.pallas_call(functools.partial(compute_body, counts, kinds, grid, body)...]
    unnamed x89 -> x55, local copies, waits for them, and re-layouts: 37.7 us -> 26.5 us
    dot_general x3 -> x4, matrix products: 21.2 us -> 11.8 us  [the longest x2 6.79 us: body(): jnp.einsum('te,de->td', grad_branch, w, preferred_element_type=F32)]
    convert_element_type x2 -> x9, local copies, waits for them, and re-layouts: 3.74 us -> 13.2 us  [the longest x2 4.11 us: body(): jnp.einsum('te,de->td', grad_branch, w, preferred_element_type=F32)]
  transfers between devices with their start and end apart: 11 -> 11, of which waited for: 2 -> 2; matrix products, arithmetic and copies ran while one was open for 15% -> 17% of each run, Pallas kernels for 60% -> 71%
where the time goes in v3:
time: 700 us; the launch traced here: 695 us
  Pallas kernels  530 us (76%)
  local copies, waits for them, and re-layouts  76.8 us (11%)
  other arithmetic  42.2 us (6%)
  matrix products  23.4 us (3%)
  between operations  15.1 us (2%)
    pallas_call x8, Pallas kernels, compute(): pl.pallas_call(functools.partial(compute_body, counts, kinds, grid, body)...  242 us
    pallas_call x5, Pallas kernels, move(): pl.pallas_call(functools.partial(move_kernel, kinds, len(after)), name=ki...  147 us
    pallas_call x1, Pallas kernels, start_moves(): pl.pallas_call(functools.partial(start_kernel, kinds, planes), name='star...  82.6 us
    pallas_call x1, Pallas kernels, reduce_plane(): pl.pallas_call(reduce_kernel, name='reduce_plane', out_shape=jax.ShapeDty...  40.2 us
    unnamed x55, local copies, waits for them, and re-layouts  26.5 us
  transfers between devices with their start and end apart: 11, of which 2 were waited for; matrix products, arithmetic and copies ran while one was open for 17% of the time, Pallas kernels for 71%

profile of v3, /device:TPU:0, one launch (start us, length us, event | category | flops | bytes accessed | tf_op | source)
XLA Modules:
  0.0 695.0 jit_solution(12247994054293894816)
XLA Ops:
  10.2 1.8 copy.228
  12.0 2.5 copy.226
  14.6 2.1 dynamic-slice_bitcast_fusion.2
  17.0 2.0 copy.227
  23.8 82.6 %start_moves.1 = (s32[4,8,256]{2,1,0:T(8,128)}, bf16[4,256,2048]{2,1,0:T(8,128)(2,1)}, bf16[4,128,1408]{2,1,0:T(8,128)(2,1)}, bf16[2,4,4,128,896]{4,3,2,1,0:T(8,128)(2,1)}) custom-call(bf16[128,2048]{1,0:T(8,128)(2,1)} %refs_0_.1, bf16[128,2048]{1,0:T(8,128)(2,1)} %refs_1_.1, bf16[128,2048]{1,0:T(8,128)(2,1)} %refs_2_.1, ...), custom_call_target="tpu_custom_call" | custom-call | bytes 255000000 | tf_op jit(solution)/shard_map/start_moves/pallas_call | solution.py:439
  112.3 2.7 convert_reduce_fusion.1
  115.0 44.6 %project.1 = (bf16[1024,2048]{1,0:T(8,128)(2,1)}, f32[2,1024,896]{2,1,0:T(8,128)}, bf16[4,4,64,2048]{3,2,1,0:T(8,128)(2,1)}) custom-call(bf16[1024,2048]{1,0:T(8,128)(2,1)} %bitcast.174, f32[1,2048]{1,0:T(1,128)} %bitcast.226, bf16[2,2048,896]{2,1,0:T(8,128)(2,1)} %bitcast.166, bf16[4,64,2048]{2,1,0:T(8,128)(2,1)} %all-gather.5.cloned.1.call-done.refs_3_), custom_call_target="tpu_custom_call" | custom-call | bytes 84000000 | tf_op jit(solution)/shard_map/project/pallas_call | solution.py:335
  162.5 32.1 %mix_forward.1 = (bf16[2,2,2,256,256]{4,3,2,1,0:T(8,128)(2,1)}, f32[512,128]{1,0:T(8,128)}, f32[512,128]{1,0:T(8,128)}, f32[2,512,512]{2,1,0:T(8,128)}, bf16[4,4...) custom-call(f32[2,1024,896]{2,1,0:T(8,128)} %get-tuple-element.57.refs_0_, ...), custom_call_target="tpu_custom_call" | custom-call | bytes 72000000 | tf_op jit(solution)/shard_map/mix_forward/pallas_call | solution.py:335
  194.7 13.7 %to_homes.2 = bf16[4,512,256]{2,1,0:T(8,128)(2,1)} custom-call(bf16[4,512,256]{2,1,0:T(8,128)(2,1)} %bitcast.202), custom_call_target="tpu_custom_call" | custom-call | bytes 42000000 | tf_op jit(solution)/shard_map/to_homes/pallas_call | solution.py:364
  210.2 3.6 convert_add_fusion.1
  216.5 39.3 %copy_chips.1 = bf16[4,256,2048]{2,1,0:T(8,128)(2,1)} custom-call(bf16[256,2048]{1,0:T(8,128)(2,1)} %multiply_convert_fusion.refs_0_), custom_call_target="tpu_custom_call" | custom-call | bytes 114000000 | tf_op jit(solution)/shard_map/copy_chips/pallas_call | solution.py:364
  255.9 22.1 %hidden_units.1 = (bf16[2,1024,704]{2,1,0:T(8,128)(2,1)}, bf16[2,1024,704]{2,1,0:T(8,128)(2,1)}, bf16[2,1024,704]{2,1,0:T(8,128)(2,1)}, bf16[4,256,2048]{2,1,0:T(8,128)(2,1)}) custom-call(bf16[1024,2048]{1,0:T(8,128)(2,1)} %bitcast.162, bf16[2,2048,1408]{2,1,0:T(8,128)(2,1)} %bitcast.158, ...), custom_call_target="tpu_custom_call", output_to_operand_aliasing={{3}: (2, {})} | custom-call | bytes 66000000 | tf_op jit(solution)/shard_map/hidden_units/pallas_call | solution.py:335
  277.9 11.0 %down_grads.1.refs_0_ = bf16[4,2,176,2048]{3,2,1,0:T(8,128)(2,1)} custom-call(bf16[2,1024,704]{2,1,0:T(8,128)(2,1)} %get-tuple-element.64.hidden_ref, bf16[1024,2048]{1,0:T(8,128)(2,1)} %bitcast.160), custom_call_target="tpu_custom_call" | custom-call | bytes 36000000 | tf_op jit(solution)/shard_map/down_grads/pallas_call | solution.py:1008
  289.0 11.6 %bitcast_convert_fusion = bf16[1024,2048]{1,0:T(8,128)(2,1)} fusion(bf16[2,1024,704]{2,1,0:T(8,128)(2,1)} %get-tuple-element.64.hidden_ref, bf16[2,704,2048]{2,1,0:T(8,128)(2,1)} %bitcast.183), kind=kOutput, calls=%fused_computation | convolution fusion | flops 5907677184 | bytes 12845056 | tf_op jit(solution)/shard_map/ctf,cfd->td/dot_general | solution.py:1170
  300.6 35.4 %hidden_grads.1 = (bf16[2,1024,1408]{2,1,0:T(8,128)(2,1)}, bf16[1024,2048]{1,0:T(8,128)(2,1)}, bf16[2,2,128,2048]{3,2,1,0:T(8,128)(2,1)}) custom-call(bf16[1024,2048]{1,0:T(8,128)(2,1)} %bitcast.161, bf16[2,1024,704]{2,1,0:T(8,128)(2,1)} %get-tuple-element.66.refs_1_, bf16[2,1024,704]{2,1,0:T(8,128)(2,1)} %get-tuple-element.67.refs_2_, ...), custom_call_target="tpu_custom_call" | custom-call | bytes 135000000 | tf_op jit(solution)/shard_map/hidden_grads/pallas_call | solution.py:335
  336.1 2.8 fusion.33
  341.5 2.1 copy-done.5
  344.6 20.6 %weight_grads.2 = (bf16[4,2,512,1408]{3,2,1,0:T(8,128)(2,1)}, bf16[2,128,2048]{2,1,0:T(8,128)(2,1)}) custom-call(bf16[1024,2048]{1,0:T(8,128)(2,1)} %bitcast.163, bf16[2,1024,1408]{2,1,0:T(8,128)(2,1)} %get-tuple-element.69.refs_1_, bf16[2,128,2048]{2,1,0:T(8,128)(2,1)} %fusion.12.refs_2_), custom_call_target="tpu_custom_call" | custom-call | bytes 66000000 | tf_op jit(solution)/shard_map/weight_grads/pallas_call | solution.py:335
  365.7 2.2 dynamic-slice_bitcast_fusion.5
  368.1 2.1 collective-permute-done
  370.2 2.0 fusion.14
  374.6 40.2 %reduce_plane.1 = f32[256,2048]{1,0:T(8,128)} custom-call(bf16[4,256,2048]{2,1,0:T(8,128)(2,1)} %bitcast.204, bf16[4,2,176,2048]{3,2,1,0:T(8,128)(2,1)} %down_grads.1.refs_0_, bf16[4,2,512,1408]{3,2,1,0:T(8,128)(2,1)} %get-tuple-element.72.refs_1_), custom_call_target="tpu_custom_call" | custom-call | bytes 114000000 | tf_op jit(solution)/shard_map/reduce_plane/pallas_call | solution.py:498
  414.8 2.4 multiply_reduce_fusion
  420.0 2.1 convolution_convert_fusion
  422.0 2.0 copy.240
  424.1 4.7 convolution_convert_fusion.1
  428.8 2.1 copy.239
  433.7 2.4 copy.242
  436.1 13.6 %from_homes.1 = bf16[4,512,256]{2,1,0:T(8,128)(2,1)} custom-call(bf16[4,512,256]{2,1,0:T(8,128)(2,1)} %bitcast.203, bf16[176,2048]{1,0:T(8,128)(2,1)} %bitcast.209), custom_call_target="tpu_custom_call" | custom-call | bytes 42000000 | tf_op jit(solution)/shard_map/from_homes/pallas_call | solution.py:364
  449.7 46.1 %mix_backward.1 = (bf16[2,1024,896]{2,1,0:T(8,128)(2,1)}, f32[8,128]{1,0:T(8,128)}, bf16[4,256,2048]{2,1,0:T(8,128)(2,1)}) custom-call(f32[2,1024,896]{2,1,0:T(8,128)} %get-tuple-element.57.refs_0_, bf16[2,2,2,256,256]{4,3,2,1,0:T(8,128)(2,1)} %bitcast.193, f32[512,128]{1,0:T(8,128)} %get-tuple-element.170.refs_1_.refs_2_, ...), custom_call_target="tpu_custom_call" | custom-call | bytes 90000000 | tf_op jit(solution)/shard_map/mix_backward/pallas_call | solution.py:335
  495.8 6.5 out_grads.1.refs_4_
  505.2 26.6 %input_grads.1 = (bf16[1024,2048]{1,0:T(8,128)(2,1)}, f32[8,2048]{1,0:T(8,128)}, bf16[2,4,1,128,1408]{4,3,2,1,0:T(8,128)(2,1)}) custom-call(bf16[2,1024,896]{2,1,0:T(8,128)(2,1)} %get-tuple-element.76.refs_0_.refs_1_, bf16[2,2048,896]{2,1,0:T(8,128)(2,1)} %bitcast.167, bf16[1024,2048]{1,0:T(8,128)(2,1)} %bitcast.175, bf16[1,4,128,1408]{3,2,1,0:T(8,128)(2,1)} %bitcast.214, ...), custom_call_target="tpu_custom_call" | custom-call | bytes 60000000 | tf_op jit(solution)/shard_map/input_grads/pallas_call | solution.py:335
  534.1 2.5 pad.21.refs_2_
  536.7 14.8 %weight_grads.3.refs_2_ = bf16[4,2,512,896]{3,2,1,0:T(8,128)(2,1)} custom-call(bf16[1024,2048]{1,0:T(8,128)(2,1)} %get-tuple-element.79.refs_0_, bf16[2,1024,896]{2,1,0:T(8,128)(2,1)} %get-tuple-element.76.refs_0_.refs_1_, f32[2048,128]{1,0:T(8,128)} %pad.21.refs_2_), custom_call_target="tpu_custom_call" | custom-call | bytes 45000000 | tf_op jit(solution)/shard_map/weight_grads/pallas_call | solution.py:335
  552.2 3.6 fusion.8
  556.0 2.0 bitcast_convert_fusion.1
  558.0 47.4 %to_homes.3 = (bf16[4,256,2048]{2,1,0:T(8,128)(2,1)}, bf16[128,1024]{1,0:T(8,128)(2,1)}) custom-call(bf16[4,256,2048]{2,1,0:T(8,128)(2,1)} %bitcast.185, bf16[128,1024]{1,0:T(8,128)(2,1)} %bitcast.221, bf16[4,2,512,896]{3,2,1,0:T(8,128)(2,1)} %weight_grads.3.refs_2_), custom_call_target="tpu_custom_call" | custom-call | bytes 144000000 | tf_op jit(solution)/shard_map/to_homes/pallas_call | solution.py:364
  607.1 3.5 convert_reduce_fusion
  612.4 3.0 fusion.6
  615.4 4.8 copy.251
  620.1 2.2 collective-permute-start.2
  622.4 4.0 slice_convert_fusion.1
  626.4 1.9 copy.252
  628.3 3.4 copy.259
  631.7 3.7 copy.253
  635.4 3.4 copy.260
  640.9 33.0 %spread.1 = bf16[2,4,1,128,896]{4,3,2,1,0:T(8,128)(2,1)} custom-call(bf16[1,4,128,896]{3,2,1,0:T(8,128)(2,1)} %bitcast.217), custom_call_target="tpu_custom_call" | custom-call | bytes 54000000 | tf_op jit(solution)/shard_map/spread/pallas_call | solution.py:364
  673.9 2.7 slice_convert_fusion.3
  (150 shorter events, 56.4 us)
Async XLA Ops:
  7.2 99.3 %copy-start = (bf16[352,2048]{1,0:T(8,128)(2,1)S(1)}, bf16[352,2048]{1,0:T(8,128)(2,1)}, u32[]{:S(2)}) copy-start(bf16[352,2048]{1,0:T(8,128)(2,1)} %param.28) | copy-start | bytes 4325380
  7.2 107.8 %all-gather.5.cloned.1.call-start = ((), (), s32[]{:S(2)}) async-start(), calls=%async_computation.4 | async-start | bytes 1310720 | tf_op jit(solution)/shard_map/all_gather | solution.py:1128
  9.0 246.8 %all-gather.7.cloned.1.call-start = ((), (), s32[]{:S(2)}) async-start(), calls=%async_computation.5 | async-start | bytes 12976128 | tf_op jit(solution)/shard_map/all_gather | solution.py:1071
  16.7 3.8 copy-start.21
  16.7 3.9 copy-start.18
  16.7 4.0 copy-start.19
  20.4 2.7 copy-start.17
  106.4 182.6 %all-gather.9.cloned.1.call-start = ((), (), s32[]{:S(2)}) async-start(), calls=%async_computation.10 | async-start | bytes 6488064 | tf_op jit(solution)/shard_map/all_gather | solution.py:1071
  107.4 328.7 %reduce-scatter.5.cloned.1.call-start = ((), (), s32[]{:S(2)}) async-start(), calls=%async_computation.6 | async-start | bytes 6488064 | tf_op jit(solution)/shard_map/reduce_scatter | solution.py:1075
  111.1 48.4 %copy-start.16 = (f32[2,4,128]{2,1,0:T(4,128)}, f32[2,4,128]{2,1,0:T(4,128)S(1)}, u32[]{:S(2)}) copy-start(f32[2,4,128]{2,1,0:T(4,128)S(1)} %broadcast_add_fusion) | copy-start | bytes 12292
  208.4 1.9 copy-start.4
  210.2 3.6 copy-start.9
  288.9 216.3 %reduce-scatter.7.cloned.1.call-start = ((), (), s32[]{:S(2)}) async-start(), calls=%async_computation.7 | async-start | bytes 12976128 | tf_op jit(solution)/shard_map/reduce_scatter | solution.py:1075
  339.0 1.6 copy-start.14
  341.4 2.1 copy-start.5
  365.2 192.8 %reduce-scatter.9.cloned.1.call-start = ((), (), s32[]{:S(2)}) async-start(), calls=%async_computation.8 | async-start | bytes 2359296 | tf_op jit(solution)/shard_map/reduce_scatter | solution.py:1075
  368.0 2.3 collective-permute-start
  414.8 2.4 copy-start.2
  414.8 2.5 copy-start.6
  417.3 2.7 copy-start.10
  418.0 1.0 copy-start.11
  502.3 0.7 copy-start.20
  502.3 138.6 %reduce-scatter.11.cloned.1.call-start = ((), (), s32[]{:S(2)}) async-start(), calls=%async_computation.9 | async-start | bytes 8257536 | tf_op jit(solution)/shard_map/reduce_scatter | solution.py:1075
  551.8 4.0 collective-permute-start.3
  552.2 3.6 copy-start.12
  605.4 14.7 %collective-permute-start.1 = (bf16[128,1024]{1,0:T(8,128)(2,1)}, bf16[128,1024]{1,0:T(8,128)(2,1)S(1)}, u32[]{:S(2)}, u32[]{:S(2)}) collective-permute-start(bf16[128,1024]{1,0:T(8,128)(2,1)} %get-tuple-element.83), channel_id=1, source_target_pairs={{0,0},{2,8},{4,16},{6,24},{8,2},{10,10},{12,18},{14,26},{16,4},{18... | collective-permute-start | bytes 786440 | tf_op jit(solution)/shard_map/ppermute | solution.py:1234
  607.1 3.5 copy-start.15
  607.1 4.0 copy-start.8
  610.5 1.6 copy-start.3
  610.5 1.9 copy-start.7
  620.1 18.6 %collective-permute-start.2 = (bf16[128,1024]{1,0:T(8,128)(2,1)S(1)}, bf16[128,1024]{1,0:T(8,128)(2,1)S(1)}, u32[]{:S(2)}, u32[]{:S(2)}) collective-permute-start(bf16[128,1024]{1,0:T(8,128)(2,1)S(1)} %collective-permute-done.1), channel_id=1, source_target_pairs={{0,1},{1,0},{2,3},{3,2},{4,5},{5,4},{6,7},{7,6},{8,9},{9,8},{10,11... | collective-permute-start | bytes 786440 | tf_op jit(solution)/shard_map/ppermute | solution.py:1079
  685.3 2.6 copy-start.1
  685.7 1.3 copy-start.13
Sparse Core Ops, SparseCore 0:
  10.2 30.6 all-gather.4
  106.5 108.4 all-gather.6
  217.2 58.7 all-gather.8
  289.0 63.9 reduce-scatter.4
  365.3 118.3 reduce-scatter.6
  502.4 34.7 reduce-scatter.8
  551.6 89.2 reduce-scatter.10

commit v4 on v3

--- a/solution.py
+++ b/solution.py
@@ -34,7 +34,7 @@
     return {**chip, "c": c}, {**chip, "c": c}, y * 2 + x
 
 
-def enter_plane(y, x, c, more=()):
+def enter_plane(y, x, c, more=(), greeted=0):
     barrier = pltpu.get_barrier_semaphore()
     peers = list(more)
     for flip in range(1, 8):
@@ -43,18 +43,11 @@
         })
     for peer in peers:
         pl.semaphore_signal(barrier, inc=1, device_id=peer, device_id_type=MESH)
-    pl.semaphore_wait(barrier, len(peers))
+    pl.semaphore_wait(barrier, len(peers) + greeted)
 
 
 def swap_kernel_sems(count):
     return [pltpu.SemaphoreType.DMA((count,)), pltpu.SemaphoreType.DMA((count,))]
-
-
-def enter_pairs(y, x):
-    barrier = pltpu.get_barrier_semaphore()
-    for peer in ({"y": 1 - y}, {"x": 1 - x}):
-        pl.semaphore_signal(barrier, inc=1, device_id=peer, device_id_type=MESH)
-    pl.semaphore_wait(barrier, 2)
 
 
 def remote(source, target, send, recv, peer):
@@ -178,6 +171,29 @@
     def wait(self):
         for copy in self.all:
             copy.wait()
+
+
+def home_of_rows(y, x, z, planes):
+    chip = y * 2 + x
+    here = z * 4 + chip
+    return here, chip * planes + z, lax.rem(here, planes) * 4 + here // planes
+
+
+def device(block, core):
+    return {"z": block // 4, "y": lax.rem(block, 4) // 2, "x": lax.rem(block, 2), "c": core}
+
+
+def greet_homes(y, x, c, z, planes):
+    here, goal, origin = home_of_rows(y, x, z, planes)
+
+    @pl.when(goal != here)
+    def _():
+        for block in (goal, origin):
+            pl.semaphore_signal(
+                pltpu.get_barrier_semaphore(), inc=1, device_id=device(block, c), device_id_type=MESH
+            )
+
+    return jnp.where(goal != here, 2, 0)
 
 
 class Swap:
@@ -373,16 +389,36 @@
     )(*(a for _, a in items), *after)
 
 
+def hidden_columns(core, planes, weights, out_ref):
+    for chip in range(4):
+        pieces = []
+        for w_ref in weights:
+            piece = w_ref.shape[1] // (8 * planes)
+            for z in range(planes):
+                start = (z * 4 + chip) * 2 * piece
+                both = w_ref[:, start:start + 2 * piece].astype(F32)
+                pieces.append(jnp.where(core == 0, both[:, :piece], both[:, piece:]))
+        out_ref[chip] = jnp.concatenate(pieces, axis=1).astype(BF16)
+
+
 def start_kernel(kinds, planes, *refs):
     count = len(kinds)
-    projections, rest_ref, sources = refs[:3], refs[3], refs[4:4 + count]
-    results, m_ref, sems = refs[4 + count:4 + 2 * count], refs[4 + 2 * count], refs[5 + 2 * count:]
+    projections, rest_ref, gate_ref, up_ref, sources = refs[:3], refs[3], refs[4], refs[5], refs[6:6 + count]
+    results, h_ref, m_ref = refs[6 + count:6 + 2 * count], refs[6 + 2 * count], refs[7 + 2 * count]
+    hidden_ref, gate_room, up_room, load, *sems = refs[8 + 2 * count:]
     y, x, c, z = (lax.axis_index(name) for name in ("y", "x", "c", "z"))
     up, down = lax.rem(z + 1, planes), lax.rem(z + planes - 1, planes)
     wide = DEPTH // 2
+    loads = [
+        pltpu.make_async_copy(w_ref, room, load.at[n]) for n, (w_ref, room) in enumerate(((gate_ref, gate_room), (up_ref, up_room)))
+    ]
+    for copy in loads:
+        copy.start()
     enter_plane(y, x, c, [{"z": up}, {"z": down}])
     moves = all_moves(kinds, sources, results, sems, y, x, c)
     sems = sems[4 * count:]
+    moves.append(one_move("columns", hidden_ref, h_ref, y, x, c, *sems[:4]))
+    sems = sems[4:]
 
     def part(n, source, columns):
         return Moves(
@@ -407,6 +443,9 @@
     ]
     for one in parts:
         one.start()
+    for copy in loads:
+        copy.wait()
+    hidden_columns(c, planes, (gate_room, up_room), hidden_ref)
     for one in parts:
         one.wait()
     ring[0].start()
@@ -426,13 +465,16 @@
         copy.wait_send()
 
 
-def start_moves(collective, projections, rest, items):
+def start_moves(collective, projections, rest, gate, up, items):
     planes = lax.axis_size("z")
     kinds = tuple(kind for kind, _ in items)
     any_place = pl.BlockSpec(memory_space=pl.ANY)
     shapes = [moved(kind, a) for kind, a in items]
+    hidden = jax.ShapeDtypeStruct((4, gate.shape[0], gate.shape[1] // 4), BF16)
+    shapes.append(hidden)
     shapes.append(jax.ShapeDtypeStruct((2, planes, 4, rest.shape[1], 3 * DEPTH // 2 + TILE), BF16))
-    sems = [sem for kind, a in items for sem in move_scratch(kind, a)]
+    sems = [pltpu.VMEM(hidden.shape, BF16), pltpu.VMEM(gate.shape, BF16), pltpu.VMEM(up.shape, BF16), pltpu.SemaphoreType.DMA((2,))]
+    sems += [sem for kind, a in items for sem in move_scratch(kind, a)] + move_scratch("columns", hidden)
     part = jax.ShapeDtypeStruct((4, rest.shape[1], DEPTH // 2), BF16)
     sems += [sem for a in (part, part, part, rest) for sem in move_scratch("columns", a)]
     sems += swap_kernel_sems(planes) + swap_kernel_sems(planes)
@@ -440,81 +482,214 @@
         functools.partial(start_kernel, kinds, planes),
         name="start_moves",
         out_shape=shapes,
-        in_specs=[any_place] * (len(items) + 4),
+        in_specs=[any_place] * (6 + len(items)),
         out_specs=[any_place] * len(shapes),
         scratch_shapes=sems,
-        compiler_params=pltpu.CompilerParams(collective_id=collective, has_side_effects=True),
+        compiler_params=pltpu.CompilerParams(collective_id=collective, has_side_effects=True, vmem_limit_bytes=60 << 20),
         cost_estimate=cost(85),
-    )(*projections, rest, *(a for _, a in items))
-
-
-def reduce_kernel(a_ref, *refs):
-    out_ref, got_ref, sum_ref, last_ref, send, recv = refs[-6:]
-    y, x = lax.axis_index("y"), lax.axis_index("x")
-    enter_pairs(y, x)
-    half = out_ref.shape[0] // 2
+    )(*projections, rest, gate, up, *(a for _, a in items))
+
+
+class PlaneSum:
+    def __init__(self, a_ref, rooms, y, x):
+        self.near_ref, self.onward_ref, self.far_ref, *sems = rooms
+        self.near = ReduceNear(a_ref, self.near_ref, y, x, *sems[:2])
+        self.far = ReduceFar(self.onward_ref, self.far_ref, y, x, *sems[2:])
+
+    def start(self):
+        self.near.start()
+
+    def go_on(self, own):
+        self.near.wait()
+        for part in range(2):
+            self.onward_ref[part] = (own(part, 0).astype(F32) + self.near_ref[part, 0].astype(F32)).astype(BF16)
+        self.far.start()
+
+    def total(self, own, part, some):
+        return (
+            own(part, 1)[some, :].astype(F32) + self.near_ref[part, 1, some, :].astype(F32)
+            + self.far_ref[part, some, :].astype(F32)
+        )
+
+
+def sum_rooms(rows, features):
+    half = (rows // 2, features)
+    sem = pltpu.SemaphoreType.DMA
+    return [
+        pltpu.VMEM((2, 2) + half, BF16), pltpu.VMEM((2,) + half, BF16), pltpu.VMEM((2,) + half, BF16),
+        sem((4,)), sem((4,)), sem((2,)), sem((2,)),
+    ]
+
+
+def end_kernel(planes, g_ref, gn_ref, block_ref, w_ref, grad_attended_ref, x_ref, gain_ref, attended_ref, *refs):
+    outs, w_out_ref, grad_ref, output_ref, refs = refs[:4], refs[4], refs[5], refs[6], refs[7:]
+    own_ref, core_ref, ring_ref, sum_ref, land_ref, w_land_ref, shares_ref, mine_ref, refs = *refs[:8], refs[8:]
+    load, core_send, core_recv, ring_send, ring_recv, spread_send, spread_recv, w_send, w_recv, w_local = refs[:10]
+    mine_load, shares_load, shares_send, shares_recv, *rooms = refs[10:]
+    y, x, c, z = (lax.axis_index(name) for name in ("y", "x", "c", "z"))
+    chip, other = y * 2 + x, {"c": 1 - c}
+    up, down = {"z": lax.rem(z + 1, planes)}, {"z": lax.rem(z + planes - 1, planes)}
+    here, goal, _ = home_of_rows(y, x, z, planes)
+    enter_plane(y, x, c, [up, down], greet_homes(y, x, c, z, planes))
+    rows = own_ref.shape[1]
+    half, size = rows // 2, rows // 4
     parts = [pl.ds(0, half), pl.ds(half, half)]
-    places = [(1 - y, y), (1 - x, x)]
-    peers = [{"x": 1 - x}, {"y": 1 - y}]
-
-    def block(part, place, other):
-        if part == 0:
-            return place * 2 + (1 - x if other else x)
-        return (1 - y if other else y) * 2 + place
-
-    def copy(source, target, n, peer):
-        return remote(source, target, send.at[n], recv.at[n], peer)
-
-    first = [
-        [copy(a_ref.at[block(part, places[part][i], True), parts[part]], got_ref.at[part, i], 2 * part + i, peers[part])
-         for i in range(2)] for part in range(2)
+    blocks = [[(1 - y) * 2 + x, chip], [y * 2 + 1 - x, chip]]
+    token_parts = halves_at(block_ref.shape[1])
+
+    def place(step):
+        return lax.rem(z + 2 * planes - 1 - step, planes)
+
+    loads = [pltpu.make_async_copy(g_ref.at[place(s), c], own_ref.at[s], load.at[s]) for s in range(planes)]
+    across = [
+        remote(g_ref.at[place(s), 1 - c], core_ref.at[s], core_send.at[s], core_recv.at[s], other) for s in range(planes)
     ]
-    for i in range(2):
+    shares_across = [
+        remote(gn_ref.at[2 * i + 1 - c], shares_ref.at[2 * c + i], shares_send.at[i], shares_recv.at[i], other)
+        for i in range(2)
+    ]
+    shares_own = [
+        pltpu.make_async_copy(gn_ref.at[2 * i + c], shares_ref.at[2 * c + i], shares_load.at[i]) for i in range(2)
+    ]
+    mine = [
+        pltpu.make_async_copy(
+            block_ref.at[blocks[part][i], token_parts[part]], mine_ref.at[part, i], mine_load.at[2 * part + i]
+        ) for part in range(2) for i in range(2)
+    ]
+    out_sum = PlaneSum(block_ref, rooms[:7], y, x)
+    in_sum = PlaneSum(shares_ref, rooms[7:], y, x)
+    out_sum.start()
+    for s in range(planes):
+        across[s].start()
+        loads[s].start()
+        if s == 0:
+            for copy in shares_across + shares_own + mine:
+                copy.start()
+    w_stay = pltpu.make_async_copy(w_ref, w_land_ref.at[c], w_local)
+    w_sent = remote(w_ref, w_land_ref.at[c], w_send.at[0], w_recv.at[0], device(goal, c))
+    w_passed = remote(w_land_ref.at[c], w_land_ref.at[c], w_send.at[1], w_recv.at[1], other)
+    pl.when(goal == here)(w_stay.start)
+
+    def ring(s, part):
+        return remote(
+            sum_ref.at[s, parts[part]], ring_ref.at[s, parts[part]], ring_send.at[s, part], ring_recv.at[s, part], up
+        )
+
+    def out_own(part, i):
+        return mine_ref.at[part, i][...]
+
+    def in_own(part, i):
+        return shares_ref[blocks[part][i], token_parts[part], :]
+
+    for s in range(planes):
+        if s == 1:
+            for copy in mine:
+                copy.wait()
+            out_sum.go_on(out_own)
+            pl.when(goal != here)(w_sent.start)
+        if s == planes - 1:
+            in_sum.go_on(in_own)
+        across[s].wait_recv()
+        loads[s].wait()
         for part in range(2):
-            first[part][i].start()
-    onward = [copy(sum_ref.at[part], last_ref.at[part], 4 + part, peers[1 - part]) for part in range(2)]
-
-    def total(part, i):
-        own = a_ref[block(part, places[part][i], False), parts[part], :]
-        return own.astype(F32) + got_ref[part, i].astype(F32)
-
+            total = own_ref[s, parts[part], :].astype(F32) + core_ref[s, parts[part], :].astype(F32)
+            if s > 0:
+                ring(s - 1, part).wait_recv()
+                total = total + ring_ref[s - 1, parts[part], :].astype(F32)
+            sum_ref[s, parts[part], :] = total.astype(BF16)
+            if s < planes - 1:
+                ring(s, part).start()
+        if s == 0:
+            for copy in shares_across:
+                copy.wait_recv()
+            for copy in shares_own:
+                copy.wait()
+            in_sum.start()
+
+    sent, passed = [], []
+    for flip in range(4):
+        peer = {"y": lax.rem(y + flip // 2, 2), "x": lax.rem(x + flip % 2, 2)}
+        at = peer["y"] * 2 + peer["x"]
+        some = sum_ref.at[planes - 1, pl.ds(pl.multiple_of(at * size, size), size)]
+        if flip:
+            sent.append(remote(some, land_ref.at[c, chip], spread_send.at[flip], spread_recv.at[flip], peer))
+            sent[-1].start()
+        source = land_ref.at[c, at] if flip else some
+        passed.append(remote(source, land_ref.at[c, at], spread_send.at[4 + flip], spread_recv.at[4 + flip], other))
+    passed[0].start()
+    land_ref[c, chip] = sum_ref[planes - 1, pl.ds(pl.multiple_of(chip * size, size), size), :]
+    pl.when(goal == here)(w_stay.wait)
+    pl.when(goal != here)(w_sent.wait)
+    w_passed.start()
+    out_sum.far.wait()
+    tokens = output_ref.shape[0] // 2
+    some = slice(0, tokens)
     for part in range(2):
-        first[part][0].wait_recv()
-        sum_ref[part] = total(part, 0).astype(BF16)
-        onward[part].start()
+        here_rows = slice(part * tokens, (part + 1) * tokens)
+        output_ref[here_rows, :] = (attended_ref[here_rows, :] + out_sum.total(out_own, part, some)).astype(BF16)
+    for copy, onward in zip(sent, passed[1:]):
+        copy.wait_recv()
+        onward.start()
+    in_sum.far.wait()
     for part in range(2):
-        first[part][1].wait_recv()
-        out_ref[parts[part], :] = total(part, 1)
-    for part in range(2):
-        onward[part].wait_recv()
-        out_ref[parts[part], :] += last_ref[part].astype(F32)
-    for one in first[0] + first[1] + onward:
-        one.wait_send()
-
-
-def reduce_plane(collective, a, after=()):
-    rows, features = a.shape[1:]
-    half = (rows // 2, features)
+        here_rows = slice(part * tokens, (part + 1) * tokens)
+        input_back(in_sum.total(in_own, part, some), here_rows, grad_attended_ref, x_ref, gain_ref, grad_ref)
+    for copy in passed:
+        copy.wait_recv()
+    wide = DEPTH // 2
+    for at in range(4):
+        for core in range(2):
+            block = land_ref[core, at].astype(F32)
+            columns = pl.ds((2 * at + core) * wide, wide)
+            for n in range(3):
+                outs[n][:, columns] = block[:, n * wide:(n + 1) * wide]
+            outs[3][core, at] = block[:, 3 * wide:]
+    w_passed.wait()
+    wide = w_land_ref.shape[2]
+    for core in range(2):
+        w_out_ref[:, core * wide:(core + 1) * wide] = w_land_ref[core].astype(F32)
+    for copy in sent + passed + across + shares_across:
+        copy.wait_send()
+    for s in range(planes - 1):
+        for part in range(2):
+            ring(s, part).wait_send()
+
+
+def input_back(grad, some, attended_ref, x_ref, gain_ref, out_ref):
+    x = x_ref[some, :].astype(F32)
+    ratio = lax.rsqrt(jnp.mean(x * x, axis=1, keepdims=True) + EPSILON)
+    u, xh = grad * gain_ref[...], x * ratio
+    back = ratio * (u - xh * jnp.mean(u * xh, axis=1, keepdims=True))
+    out_ref[some, :] = attended_ref[some, :] + back
+
+
+def end_moves(collective, grads, gn, block_out, w, grad_attended, x, gain, attended):
+    planes, _, rows, columns = grads.shape
+    here, features = rows // 4, x.shape[1]
+    any_place, in_vmem = pl.BlockSpec(memory_space=pl.ANY), pl.BlockSpec(memory_space=pltpu.VMEM)
+    matrix = jax.ShapeDtypeStruct((here, features), F32)
+    blocks = pltpu.VMEM((planes, rows, columns), BF16)
+    sem = pltpu.SemaphoreType.DMA
+    half = (x.shape[0] // 2, features)
     return pl.pallas_call(
-        reduce_kernel,
-        name="reduce_plane",
-        out_shape=jax.ShapeDtypeStruct((rows, features), F32),
-        in_specs=[pl.BlockSpec(memory_space=pltpu.VMEM)] + [pl.BlockSpec(memory_space=pl.ANY)] * len(after),
-        out_specs=pl.BlockSpec(memory_space=pltpu.VMEM),
-        scratch_shapes=[pltpu.VMEM((2, 2) + half, BF16), pltpu.VMEM((2,) + half, BF16), pltpu.VMEM((2,) + half, BF16)]
-        + swap_kernel_sems(6),
-        compiler_params=pltpu.CompilerParams(collective_id=collective, has_side_effects=True),
-        cost_estimate=cost(38),
-    )(a, *after)
-
-
-def add_other(a, other):
-    return (a.astype(F32) + other.astype(F32)).astype(BF16)
-
-
-def halves_of(a, place, axis):
-    here = lax.axis_index(axis)
-    return [lax.dynamic_index_in_dim(a, at, place, keepdims=False) for at in (here, 1 - here)]
+        functools.partial(end_kernel, planes),
+        name="end_moves",
+        out_shape=[
+            matrix, matrix, matrix, jax.ShapeDtypeStruct((2, 4, here, TILE), F32), matrix,
+            jax.ShapeDtypeStruct(x.shape, F32), jax.ShapeDtypeStruct(x.shape, BF16),
+        ],
+        in_specs=[any_place] * 4 + [in_vmem] * 4,
+        out_specs=[in_vmem] * 7,
+        scratch_shapes=[
+            blocks, blocks, pltpu.VMEM((planes - 1, rows, columns), BF16), blocks,
+            pltpu.VMEM((2, 4, here, columns), BF16), pltpu.VMEM((2,) + w.shape, BF16), pltpu.VMEM(gn.shape, gn.dtype),
+            pltpu.VMEM((2, 2) + half, BF16),
+            sem((planes,)), sem((planes,)), sem((planes,)), sem((planes - 1, 2)), sem((planes - 1, 2)), sem((8,)), sem((8,)),
+            sem((2,)), sem((2,)), sem, sem((4,)), sem((2,)), sem((2,)), sem((2,)),
+        ] + sum_rooms(*x.shape) + sum_rooms(*x.shape),
+        compiler_params=pltpu.CompilerParams(collective_id=collective, has_side_effects=True, vmem_limit_bytes=60 << 20),
+        cost_estimate=cost(95),
+    )(grads, gn, block_out, w, grad_attended, x, gain, attended)
 
 
 def dot(a, b, dims):
@@ -919,7 +1094,7 @@
         back_ref[...] = (total_ref[here, :] + back).astype(BF16)
 
 
-def hidden_grads(cot, slopes, silus, w, wd, moves, collective):
+def hidden_grads(cot, slopes, silus, w, wd):
     tokens, features = cot.shape
     units = slopes.shape[2]
     some, weight, unit, _ = unit_specs(tokens, features, units)
@@ -931,66 +1106,88 @@
             pl.BlockSpec((tokens // 2, features), lambda h, t: (h * t, 0)),
         ],
         [jax.ShapeDtypeStruct((2, tokens, 2 * units), BF16), jax.ShapeDtypeStruct(cot.shape, BF16)],
-        45, grid=(2, 2), scratch=[pltpu.VMEM((tokens, features), F32)], moves=moves, collective=collective,
-    )
-
-
-def out_kernel(a_ref, b_ref, out_ref):
-    grads = dot(a_ref[...], b_ref[0], TN).astype(BF16)
-    wide = grads.shape[1] // 2
-    for f in range(2):
-        out_ref[0, f] = grads[:, f * wide:(f + 1) * wide]
-
-
-def out_grads(a, b):
+        34, grid=(2, 2), scratch=[pltpu.VMEM((tokens, features), F32)],
+    )
+
+
+def out_kernel(own_ref, other_ref, grad_ref, out_ref):
+    core = lax.axis_index("c")
+    grads = None
+    for a_ref, at_y in ((own_ref, core), (other_ref, 1 - core)):
+        for x in range(2):
+            part = dot(a_ref[x, 0], grad_ref[2 * at_y + x], TN)
+            grads = part if grads is None else grads + part
+    rows, wide = out_ref.shape[2:]
+    for z in range(out_ref.shape[0]):
+        for f in range(2):
+            out_ref[z, f] = grads[z * rows:(z + 1) * rows, f * wide:(f + 1) * wide].astype(BF16)
+
+
+def out_grads(own, other, grad):
     planes = lax.axis_size("z")
-    tokens, depth = a.shape
-    features = b.shape[2]
-    rows = max(depth // planes, TILE)
-    grads = pl.pallas_call(
-        out_kernel,
-        name="out_grads",
-        grid=(depth // rows,),
-        in_specs=[
-            pl.BlockSpec((tokens, rows), lambda i: (0, i)), pl.BlockSpec((1, tokens, features), lambda i: (0, 0, 0)),
-        ],
-        out_specs=pl.BlockSpec((1, 2, rows, features // 2), lambda i: (i, 0, 0, 0)),
-        out_shape=jax.ShapeDtypeStruct((depth // rows, 2, rows, features // 2), BF16),
-        compiler_params=pltpu.CompilerParams(vmem_limit_bytes=60 << 20),
-        cost_estimate=cost(8),
-    )(a, b)
-    if rows * planes > depth:
-        grads = grads.reshape(-1, 2, rows * planes // depth, depth // planes, features // 2).transpose(0, 2, 1, 3, 4)
-    return grads.reshape(planes, 2, depth // planes, features // 2)
+    features = grad.shape[2]
+    wide = own.shape[3]
+    rows = 2 * wide // planes
+    some = pl.BlockSpec((2, 1) + own.shape[2:], lambda f: (0, f, 0, 0))
+    return compute(
+        out_kernel, "out_grads", (own, other, grad), [some, some, pl.BlockSpec(grad.shape, lambda f: (0, 0, 0))],
+        [pl.BlockSpec((planes // 2, 2, rows, features // 2), lambda f: (f, 0, 0, 0))],
+        [jax.ShapeDtypeStruct((planes, 2, rows, features // 2), BF16)], 8, grid=(2,),
+    )[0]
+
+
+def block_kernel(hidden_ref, wd_ref, out_ref):
+    out_ref[...] = (dot(hidden_ref[0], wd_ref[0], NN) + dot(hidden_ref[1], wd_ref[1], NN)).astype(BF16)
+
+
+def block_outputs(hidden, wd, moves, collective):
+    tokens, features = hidden.shape[1], wd.shape[2]
+    rows = tokens // 2
+    return compute(
+        block_kernel, "block_outputs", (hidden, wd),
+        [pl.BlockSpec((2, rows, hidden.shape[2]), lambda t: (0, t, 0)), pl.BlockSpec(wd.shape, lambda t: (0, 0, 0))],
+        [pl.BlockSpec((rows, features), lambda t: (t, 0))], [jax.ShapeDtypeStruct((tokens, features), BF16)],
+        12, grid=(2,), moves=moves, collective=collective,
+    )
 
 
 def weight_kernel(a_ref, b_ref, out_ref):
     out_ref[0, 0] = dot(a_ref[...], b_ref[0], TN).astype(BF16)
 
 
-def weight_sums_kernel(a_ref, b_ref, sums_ref, out_ref):
-    grads = dot(a_ref[...], b_ref[0], TN)
-    wide = grads.shape[1]
-    out_ref[0, 0, :, :wide - TILE] = grads[:, :wide - TILE].astype(BF16)
-    once = jnp.where(pl.program_id(0) == 0, 1.0, 0.0)
-    out_ref[0, 0, :, wide - TILE:] = (grads[:, wide - TILE:] + once * sums_ref[...]).astype(BF16)
-
-
-def weight_grads(a, b, us, sums=None, moves=(), collective=None, after=()):
+def weight_grads(a, b, us, moves=(), collective=None):
     planes = lax.axis_size("z")
     tokens, features = a.shape
     rows, columns = features // planes, b.shape[2]
-    specs = [pl.BlockSpec((tokens, rows), lambda h, z: (0, z)), pl.BlockSpec((1, tokens, columns), lambda h, z: (h, 0, 0))]
-    body, operands = weight_kernel, (a, b)
-    if sums is not None:
-        body, operands = weight_sums_kernel, (a, b, sums)
-        specs.append(pl.BlockSpec((rows, TILE), lambda h, z: (z, 0)))
-    out = compute(
-        body, "weight_grads", operands, specs, [pl.BlockSpec((1, 1, rows, columns), lambda h, z: (z, h, 0, 0))],
-        [jax.ShapeDtypeStruct((planes, 2, rows, columns), BF16)], us, grid=(2, planes),
-        moves=moves, collective=collective, after=after,
-    )
-    return out if moves else out[0]
+    return compute(
+        weight_kernel, "weight_grads", (a, b),
+        [pl.BlockSpec((tokens, rows), lambda h, z: (0, z)), pl.BlockSpec((1, tokens, columns), lambda h, z: (h, 0, 0))],
+        [pl.BlockSpec((1, 1, rows, columns), lambda h, z: (z, h, 0, 0))],
+        [jax.ShapeDtypeStruct((planes, 2, rows, columns), BF16)], us, grid=(2, planes), moves=moves, collective=collective,
+    )
+
+
+def mixer_weight_kernel(a_ref, b_ref, sums_ref, out_ref):
+    grads = dot(a_ref[...], b_ref[0], TN)
+    wide = grads.shape[1] - TILE
+    out_ref[0, 0, :, :wide] = grads[:, :wide].astype(BF16)
+    once = jnp.where(pl.program_id(0) == 0, 1.0, 0.0)
+    out_ref[0, 0, :, wide:] = (grads[:, wide:] + once * sums_ref[...]).astype(BF16)
+
+
+def mixer_weight_grads(a, b, sums, moves, collective):
+    planes = lax.axis_size("z")
+    tokens, features = a.shape
+    rows, columns = features // planes, b.shape[2]
+    return compute(
+        mixer_weight_kernel, "mixer_weight_grads", (a, b, sums),
+        [
+            pl.BlockSpec((tokens, rows), lambda h, z: (0, z)), pl.BlockSpec((1, tokens, columns), lambda h, z: (h, 0, 0)),
+            pl.BlockSpec((rows, TILE), lambda h, z: (z, 0)),
+        ],
+        [pl.BlockSpec((1, 1, rows, columns), lambda h, z: (z, h, 0, 0))],
+        [jax.ShapeDtypeStruct((planes, 2, rows, columns), BF16)], 20, grid=(2, planes), moves=moves, collective=collective,
+    )
 
 
 def down_kernel(hidden_ref, cot_ref, out_ref):
@@ -1030,7 +1227,7 @@
     sums_ref[...] = jnp.where(tile == 0, sums, sums_ref[...] + sums)
 
 
-def input_grads(grad, w, x, moves, collective, after):
+def input_grads(grad, w, x):
     tokens, features = x.shape
     rows = tokens // 4
     return compute(
@@ -1041,7 +1238,7 @@
         ],
         [pl.BlockSpec((rows, features), lambda t: (t, 0)), pl.BlockSpec((8, features), lambda t: (0, 0))],
         [jax.ShapeDtypeStruct(x.shape, BF16), jax.ShapeDtypeStruct((8, features), F32)],
-        20, grid=(4,), moves=moves, collective=collective, after=after,
+        14, grid=(4,),
     )
 
 
@@ -1067,6 +1264,26 @@
     )
 
 
+def hidden_rows_kernel(planes, a_ref, gate_ref, up_ref):
+    piece = gate_ref.shape[1] // (8 * planes)
+    for core in range(2):
+        for chip in range(4):
+            block = a_ref[core, chip].astype(F32)
+            for n, out_ref in enumerate((gate_ref, up_ref)):
+                for z in range(planes):
+                    start = ((z * 4 + chip) * 2 + core) * piece
+                    out_ref[:, start:start + piece] = block[:, (n * planes + z) * piece:(n * planes + z + 1) * piece]
+
+
+def hidden_rows(a, columns):
+    rows = a.shape[2]
+    in_vmem = pl.BlockSpec(memory_space=pltpu.VMEM)
+    return compute(
+        functools.partial(hidden_rows_kernel, lax.axis_size("z")), "hidden_rows", (a,), [in_vmem], [in_vmem] * 2,
+        [jax.ShapeDtypeStruct((rows, columns), F32)] * 2, 6,
+    )
+
+
 def gather_planes(a):
     return lax.all_gather(a, ("c", "z"), axis=0, tiled=True).reshape((2, -1) + a.shape[1:])
 
@@ -1118,19 +1335,15 @@
     vectors = 3 * depth // 2 + SLOTS // 2
     width = vectors + 3
 
-    def hidden_columns(w):
-        w = own_half(w.reshape(rows_here, planes, 4, 2, hidden_here // 2), 3)
-        return w.transpose(2, 0, 1, 3).reshape(4, rows_here, -1)
-
     x_here = inputs.reshape(positions, features)
     cot_here = cotangent.reshape(positions, features)
     out_half = own_half(w_out.reshape(2, rows_here // 2, features), 0)
     out_half = lax.all_gather(out_half, "z", axis=0)
     full_down = gather_planes(own_half(w_down.reshape(2, hidden_here // 2, features), 0))
-    begins, x_rows, hidden_w, mixer_w = start_moves(1, (w_query, w_key, w_value), rest, (
-        ("copy_homes", jnp.broadcast_to(starts, (8, positions))), ("copy_homes", x_here),
-        ("columns", jnp.concatenate([hidden_columns(w_gate), hidden_columns(w_up)], axis=-1)),
-    ))
+    begins, x_rows, hidden_w, mixer_w = start_moves(
+        1, (w_query, w_key, w_value), rest, w_gate, w_up,
+        (("copy_homes", jnp.broadcast_to(starts, (8, positions))), ("copy_homes", x_here)),
+    )
     hidden_w = gather_planes(hidden_w.reshape(4 * rows_here, -1))
     mixer_w = mixer_w.reshape(2, features, -1)
     gain_attn, gain_ffn = (mixer_w[0, :, vectors + i].astype(F32) for i in range(2))
@@ -1148,11 +1361,10 @@
         pre, log_forget, gain, doc, [("swap_core", out_core), ("gather_near", cot_here)], 3
     )
     out_core, out_other = (a.reshape(features // 2, features) for a in (out_core, out_other))
-    other = swap(own_half(mixed, 1, 1 - c), "c")
-    own = own_half(mixed, 1)
-    mixed_chips = jnp.where(c == 0, jnp.stack([own, other]), jnp.stack([other, own]))
-    mixed_chips = mixed_chips.transpose(0, 1, 3, 2, 4).reshape(4 * positions, depth)
-    (mixed,) = move(4, ("to_homes", mixed.reshape(4, 2 * positions, depth // 2)), us=14)
+    mixed_own = own_half(mixed, 1)
+    mixed, mixed_other = move(
+        4, ("to_homes", mixed.reshape(4, 2 * positions, depth // 2)), ("swap_core", own_half(mixed, 1, 1 - c)), us=14
+    )
     mixed = mixed.reshape(2 * HEADS, positions, depth // 2).transpose(1, 0, 2)
     mixed = mixed.reshape(positions, planes, 4, 2, rows_here // 2).transpose(3, 0, 2, 1, 4)
     mixed = mixed.reshape(2, positions, features // 2)
@@ -1167,26 +1379,20 @@
     hidden, slopes, silus, cot = hidden_units(normed_ffn, hidden_w, [("gather_far", cot)], 6)
     cot = cot.reshape(4 * positions, features)
     grad_down_w = down_grads(hidden, cot)
-    block_out = jnp.einsum("ctf,cfd->td", hidden, full_down, preferred_element_type=F32).astype(BF16)
-    block_out = block_out.reshape(2, 2, positions, features)
-    grad_hidden, grad_normed_ffn, near = hidden_grads(
-        cot, slopes, silus, hidden_w, full_down, [("reduce_near", block_out.reshape(4, positions, features))], 7
+    grad_hidden, shares = hidden_grads(cot, slopes, silus, hidden_w, full_down)
+    shares = shares.reshape(2, 2, positions, features)
+    grad_hidden_w, near = weight_grads(
+        normed_ffn, grad_hidden, 24, [("reduce_near", shares.reshape(4, positions, features))], 7
     )
     half = positions // 2
     own = [
-        lax.dynamic_index_in_dim(block_out[:, :, :half], x, 1, keepdims=False),
-        lax.dynamic_index_in_dim(block_out[:, :, half:], y, 0, keepdims=False),
+        lax.dynamic_index_in_dim(shares[:, :, :half], x, 1, keepdims=False),
+        lax.dynamic_index_in_dim(shares[:, :, half:], y, 0, keepdims=False),
     ]
     own = [jnp.where(at == 0, a[::-1], a) for at, a in zip((y, x), own)]
     near = jnp.stack(own).astype(F32) + near.astype(F32)
-    grad_hidden_w, far = weight_grads(
-        normed_ffn, grad_hidden, 22, moves=[("reduce_far", near[:, 0].astype(BF16))], collective=15
-    )
-    block_out = (near[:, 1] + far.astype(F32)).reshape(positions, features)
-    output = (attended + block_out).astype(BF16)
-    grad_normed_ffn = reduce_plane(
-        8, grad_normed_ffn.reshape(4, positions, features), after=(grad_down_w, grad_hidden_w)
-    )
+    block_out, far = block_outputs(hidden, full_down, [("reduce_far", near[:, 0].astype(BF16))], 8)
+    grad_normed_ffn = (near[:, 1] + far.astype(F32)).reshape(positions, features)
     grad_down_w, grad_hidden_w = sum_planes(grad_down_w), sum_planes(grad_hidden_w)
     grad_gain_ffn = jnp.sum(grad_normed_ffn * attended * ratio_f, axis=0)
     grad_attended = cot_here.astype(F32) + norm_back(grad_normed_ffn, gain_ffn, attended, ratio_f)
@@ -1207,43 +1413,27 @@
         pre, grad_mixed, log_forget, gain, rate, doc, scores, probs, paired, [("copy_chips", grad_branch)], 10
     )
     grad_bias = jnp.sum(grad_bias[0].reshape(2, SLOTS), axis=0)
-    grad_out_w = out_grads(mixed_chips, branch_chips.reshape(1, 4 * positions, features))
-    grad_normed, sums, grad_hidden_w = input_grads(
-        grad_pre, mixer_w, x_rows, [("spread", grad_hidden_w.reshape(1, 4, rows_here, -1))], 14, (grad_out_w,)
-    )
+    grad_out_w = out_grads(mixed_own, mixed_other, branch_chips)
+    grad_normed, sums = input_grads(grad_pre, mixer_w, x_rows)
     grad_bias = jnp.zeros((HEADS, SLOTS), F32).at[head].set(grad_bias).reshape(4 * planes, bias_here)
     grad_bias = jnp.pad(grad_bias, ((0, 0), (0, rows_here - bias_here))).reshape(-1)
     sums = jnp.stack([jnp.sum(sums, axis=0), grad_gain_ffn, grad_bias], axis=-1)
     first_sum = vectors + TILE - mixer_w.shape[-1]
     sums = jnp.pad(sums, ((0, 0), (first_sum, TILE - first_sum - 3)))
-    grad_mixer_w = weight_grads(normed, grad_pre, 15, sums=sums)
+    grad_mixer_w, grad_hidden_w = mixer_weight_grads(
+        normed, grad_pre, sums, [("spread", grad_hidden_w.reshape(1, 4, rows_here, -1))], 14
+    )
     grad_out_w = sum_planes(grad_out_w)
-    grad_normed, grad_out_w = move(
-        11, ("to_homes", grad_normed.reshape(4, positions, features)), ("keep", grad_out_w), after=(grad_mixer_w,), us=48
-    )
-    grad_mixer_w = sum_planes(grad_mixer_w)
-    grad_normed_here = jnp.sum(grad_normed.astype(F32), axis=0)
-    x_here = x_here.astype(F32)
-    ratio_a = scaled(x_here)
-    grad_input = grad_attended + norm_back(grad_normed_here, gain_attn, x_here, ratio_a)
-
-    grad_hidden_w = grad_hidden_w.reshape(2, 4, rows_here, 2, planes, hidden_here // 2)
-    grad_hidden_w = grad_hidden_w.transpose(3, 2, 4, 1, 0, 5).reshape(2, rows_here, -1)
-    grad_gate_w, grad_up_w = grad_hidden_w[0].astype(F32), grad_hidden_w[1].astype(F32)
-    blocks = 4 * planes
-    grad_out_w = lax.ppermute(
-        grad_out_w, ("z", "y", "x"), [(at, at % 4 * planes + at // 4) for at in range(blocks)]
-    )
-    grad_out_w = both_of(grad_out_w, "c").transpose(1, 0, 2).reshape(rows_here, features).astype(F32)
+    grad_gate_w, grad_up_w = hidden_rows(grad_hidden_w[:, :, 0], w_gate.shape[1])
+    *grad_w, rest, grad_out_w, grad_input, output = end_moves(
+        11, grad_mixer_w, grad_normed.reshape(4, positions, features), block_out.reshape(4, positions, features),
+        grad_out_w, grad_attended, x_here, gain_attn[None], attended,
+    )
+
+    columns = SLOTS // 2
+    sums = jnp.sum(rest[0, :, :, columns:columns + 3], axis=0)
+    grad_forget_w = rest[..., :columns].transpose(2, 1, 0, 3).reshape(rows_here, HEADS * SLOTS)
     grad_down_w = both_of(grad_down_w, "c").reshape(hidden_here, features).astype(F32)
-    (grad_mixer_w,) = move(12, ("spread", grad_mixer_w.reshape(1, 4, rows_here, -1)), us=18)
-    grad_mixer_w = grad_mixer_w[:, :, 0]
-    sums = jnp.sum(grad_mixer_w[0, :, :, vectors:width].astype(F32), axis=0)
-    grad_mixer_w = grad_mixer_w.transpose(2, 1, 0, 3)
-    grad_w = [
-        grad_mixer_w[..., i * depth // 2:(i + 1) * depth // 2].reshape(rows_here, features).astype(F32) for i in range(3)
-    ]
-    grad_forget_w = grad_mixer_w[..., 3 * depth // 2:vectors].reshape(rows_here, HEADS * SLOTS).astype(F32)
     return (
         output.reshape(inputs.shape), grad_input.reshape(inputs.shape), sums[:, 0], grad_w[0], grad_w[1], grad_w[2],
         grad_forget_w, sums[:bias_here, 2], grad_out_w, sums[:, 1], grad_gate_w, grad_up_w, grad_down_w,

time: 700 us -> 643 us (0.919)
  local copies, waits for them, and re-layouts: 76.8 us -> 42.3 us
  other arithmetic: 42.2 us -> 19.5 us
  Pallas kernels: 530 us -> 547 us
  matrix products: 23.4 us -> 10.3 us
    pallas_call x5 -> x3, Pallas kernels: 147 us -> 66.4 us  [move(): pl.pallas_call(functools.partial(move_kernel, kinds, len(after)), name=ki...]
    pallas_call x2 -> x1, Pallas kernels: 46.8 us -> 98.1 us  [end_moves(): pl.pallas_call(functools.partial(end_kernel, planes), name='end_moves', o...]
    pallas_call x8 -> x11, Pallas kernels: 242 us -> 279 us  [compute(): pl.pallas_call(functools.partial(compute_body, counts, kinds, grid, body)...]
    dot_general x1 -> x0, matrix products: 11.6 us -> none  [body(): jnp.einsum('ctf,cfd->td', hidden, full_down, preferred_element_type=F32)]
    pallas_call x1, Pallas kernels: 82.6 us -> 92.5 us  [start_moves(): pl.pallas_call(functools.partial(start_kernel, kinds, planes), name='star...]
    unnamed x55 -> x46, local copies, waits for them, and re-layouts: 26.5 us -> 16.7 us
    convert_element_type x4 -> x0, other arithmetic: 8.64 us -> none  [the longest x1 4.03 us: body(): grad_hidden_w[1].astype(F32)]
    convert_element_type x7 -> x0, local copies, waits for them, and re-layouts: 8.27 us -> none  [the longest x1 3.71 us: body(): grad_hidden_w[1].astype(F32)]
  transfers between devices with their start and end apart: 11 -> 7, of which waited for: 2 -> 1; matrix products, arithmetic and copies ran while one was open for 17% -> 8% of each run, Pallas kernels for 71% -> 70%
where the time goes in v4:
time: 643 us; the launch traced here: 636 us
  Pallas kernels  547 us (85%)
  local copies, waits for them, and re-layouts  42.3 us (7%)
  other arithmetic  19.5 us (3%)
  between operations  14.9 us (2%)
  matrix products  10.3 us (2%)
    pallas_call x11, Pallas kernels, compute(): pl.pallas_call(functools.partial(compute_body, counts, kinds, grid, body)...  279 us
    pallas_call x1, Pallas kernels, end_moves(): pl.pallas_call(functools.partial(end_kernel, planes), name='end_moves', o...  98.1 us
    pallas_call x1, Pallas kernels, start_moves(): pl.pallas_call(functools.partial(start_kernel, kinds, planes), name='star...  92.5 us
    pallas_call x3, Pallas kernels, move(): pl.pallas_call(functools.partial(move_kernel, kinds, len(after)), name=ki...  66.4 us
    unnamed x46, local copies, waits for them, and re-layouts  16.7 us
  transfers between devices with their start and end apart: 7, of which 1 were waited for; matrix products, arithmetic and copies ran while one was open for 8% of the time, Pallas kernels for 70%

profile of v4, /device:TPU:0, one launch (start us, length us, event | category | flops | bytes accessed | tf_op | source)
XLA Modules:
  0.0 636.0 jit_solution(6348073449689155741)
XLA Ops:
  7.3 1.8 constant_dynamic-slice_fusion.1
  13.9 92.5 %start_moves.1 = (s32[4,8,256]{2,1,0:T(8,128)}, bf16[4,256,2048]{2,1,0:T(8,128)(2,1)}, bf16[4,128,1408]{2,1,0:T(8,128)(2,1)}, bf16[2,4,4,128,896]{4,3,2,1,0:T(8,128)(2,1)}) custom-call(bf16[128,2048]{1,0:T(8,128)(2,1)} %refs_0_.1, bf16[128,2048]{1,0:T(8,128)(2,1)} %refs_1_.1, bf16[128,2048]{1,0:T(8,128)(2,1)} %refs_2_.1, ...), custom_call_target="tpu_custom_call" | custom-call | bytes 255000000 | tf_op jit(solution)/shard_map/start_moves/pallas_call | solution.py:481
  107.7 1.4 slice_reduce_fusion
  111.2 1.1 reduce_window_sum.34.refs_3_.refs_5_
  112.3 2.7 convert_reduce_fusion
  115.0 44.7 %project.1 = (bf16[1024,2048]{1,0:T(8,128)(2,1)}, f32[2,1024,896]{2,1,0:T(8,128)}, bf16[4,4,64,2048]{3,2,1,0:T(8,128)(2,1)}) custom-call(bf16[1024,2048]{1,0:T(8,128)(2,1)} %bitcast.135, f32[1,2048]{1,0:T(1,128)} %bitcast.171, bf16[2,2048,896]{2,1,0:T(8,128)(2,1)} %bitcast.126, bf16[4,64,2048]{2,1,0:T(8,128)(2,1)} %all-gather.5.cloned.1.call-done.refs_3_), custom_call_target="tpu_custom_call" | custom-call | bytes 84000000 | tf_op jit(solution)/shard_map/project/pallas_call | solution.py:351
  159.7 1.3 slice.70
  161.4 1.1 exponential-minus-one_negate_fusion
  162.6 32.1 %mix_forward.1 = (bf16[2,2,2,256,256]{4,3,2,1,0:T(8,128)(2,1)}, f32[512,128]{1,0:T(8,128)}, f32[512,128]{1,0:T(8,128)}, f32[2,512,512]{2,1,0:T(8,128)}, bf16[4,4...) custom-call(f32[2,1024,896]{2,1,0:T(8,128)} %get-tuple-element.69.refs_0_, ...), custom_call_target="tpu_custom_call" | custom-call | bytes 72000000 | tf_op jit(solution)/shard_map/mix_forward/pallas_call | solution.py:351
  194.6 2.2 dynamic-slice_bitcast_fusion.2
  196.9 13.7 %to_homes.1 = (bf16[4,512,256]{2,1,0:T(8,128)(2,1)}, bf16[2,2,256,256]{3,2,1,0:T(8,128)(2,1)}) custom-call(bf16[4,512,256]{2,1,0:T(8,128)(2,1)} %bitcast.149, bf16[2,2,256,256]{3,2,1,0:T(8,128)(2,1)} %get-tuple-element.172.refs_1_), custom_call_target="tpu_custom_call" | custom-call | bytes 42000000 | tf_op jit(solution)/shard_map/to_homes/pallas_call | solution.py:380
  210.6 1.8 copy.87
  212.5 3.7 convolution_add_fusion.1
  216.2 1.4 multiply_reduce_fusion.1
  217.6 1.4 multiply_convert_fusion.refs_0_
  219.0 39.2 %copy_chips.1 = bf16[4,256,2048]{2,1,0:T(8,128)(2,1)} custom-call(bf16[256,2048]{1,0:T(8,128)(2,1)} %multiply_convert_fusion.refs_0_), custom_call_target="tpu_custom_call" | custom-call | bytes 114000000 | tf_op jit(solution)/shard_map/copy_chips/pallas_call | solution.py:380
  258.3 22.0 %hidden_units.1 = (bf16[2,1024,704]{2,1,0:T(8,128)(2,1)}, bf16[2,1024,704]{2,1,0:T(8,128)(2,1)}, bf16[2,1024,704]{2,1,0:T(8,128)(2,1)}, bf16[4,256,2048]{2,1,0:T(8,128)(2,1)}) custom-call(bf16[1024,2048]{1,0:T(8,128)(2,1)} %bitcast.120, bf16[2,2048,1408]{2,1,0:T(8,128)(2,1)} %bitcast.118, ...), custom_call_target="tpu_custom_call", output_to_operand_aliasing={{3}: (2, {})} | custom-call | bytes 66000000 | tf_op jit(solution)/shard_map/hidden_units/pallas_call | solution.py:351
  280.3 10.9 %down_grads.1 = bf16[4,2,176,2048]{3,2,1,0:T(8,128)(2,1)} custom-call(bf16[2,1024,704]{2,1,0:T(8,128)(2,1)} %get-tuple-element.83.refs_0_.hidden_ref, bf16[1024,2048]{1,0:T(8,128)(2,1)} %bitcast.122), custom_call_target="tpu_custom_call" | custom-call | bytes 36000000 | tf_op jit(solution)/shard_map/down_grads/pallas_call | solution.py:1205
  291.3 34.5 %hidden_grads.1 = (bf16[2,1024,1408]{2,1,0:T(8,128)(2,1)}, bf16[1024,2048]{1,0:T(8,128)(2,1)}) custom-call(bf16[1024,2048]{1,0:T(8,128)(2,1)} %bitcast.123, bf16[2,1024,704]{2,1,0:T(8,128)(2,1)} %get-tuple-element.78.refs_1_, bf16[2,1024,704]{2,1,0:T(8,128)(2,1)} %get-tuple-element.79.refs_2_, bf16[2,2048,1408]{2,1,0:T(8,128)(2,1)} %bitcast.119, ...), custom_call_target="tpu_custom_call" | custom-call | bytes 102000000 | tf_op jit(solution)/shard_map/hidden_grads/pallas_call | solution.py:351
  325.8 29.4 %weight_grads.1 = (bf16[4,2,512,1408]{3,2,1,0:T(8,128)(2,1)}, bf16[2,2,128,2048]{3,2,1,0:T(8,128)(2,1)}) custom-call(bf16[1024,2048]{1,0:T(8,128)(2,1)} %bitcast.121, bf16[2,1024,1408]{2,1,0:T(8,128)(2,1)} %get-tuple-element.81.refs_1_, bf16[4,256,2048]{2,1,0:T(8,128)(2,1)} %bitcast.133), custom_call_target="tpu_custom_call" | custom-call | bytes 72000000 | tf_op jit(solution)/shard_map/weight_grads/pallas_call | solution.py:351
  355.2 2.7 fusion.25
  358.7 1.1 copy-done.11
  360.6 2.3 copy-done.3
  362.9 1.1 fusion.5.refs_2_
  364.0 20.1 %block_outputs.1 = (bf16[1024,2048]{1,0:T(8,128)(2,1)}, bf16[2,128,2048]{2,1,0:T(8,128)(2,1)}) custom-call(bf16[2,1024,704]{2,1,0:T(8,128)(2,1)} %get-tuple-element.83.refs_0_.hidden_ref, bf16[2,704,2048]{2,1,0:T(8,128)(2,1)} %bitcast.132, bf16[2,128,2048]{2,1,0:T(8,128)(2,1)} %fusion.5.refs_2_), custom_call_target="tpu_custom_call" | custom-call | bytes 36000000 | tf_op jit(solution)/shard_map/block_outputs/pallas_call | solution.py:351
  384.1 2.1 fusion
  387.5 2.0 fusion.23
  390.7 1.3 convolution_convert_fusion
  392.2 3.9 convolution_convert_fusion.1
  396.6 1.3 copy.93
  397.9 13.4 %from_homes.1 = bf16[4,512,256]{2,1,0:T(8,128)(2,1)} custom-call(bf16[4,512,256]{2,1,0:T(8,128)(2,1)} %bitcast.152, bf16[176,2048]{1,0:T(8,128)(2,1)} %bitcast.155), custom_call_target="tpu_custom_call" | custom-call | bytes 42000000 | tf_op jit(solution)/shard_map/from_homes/pallas_call | solution.py:380
  411.3 45.8 %mix_backward.1 = (bf16[2,1024,896]{2,1,0:T(8,128)(2,1)}, f32[8,128]{1,0:T(8,128)}, bf16[4,256,2048]{2,1,0:T(8,128)(2,1)}) custom-call(f32[2,1024,896]{2,1,0:T(8,128)} %get-tuple-element.69.refs_0_, bf16[2,2,2,256,256]{4,3,2,1,0:T(8,128)(2,1)} %bitcast.148, f32[512,128]{1,0:T(8,128)} %get-tuple-element.168.refs_1_.refs_2_, ...), custom_call_target="tpu_custom_call" | custom-call | bytes 90000000 | tf_op jit(solution)/shard_map/mix_backward/pallas_call | solution.py:351
  457.1 5.9 out_grads.1
  463.0 1.1 copy-done.9
  466.4 14.4 %input_grads.1 = (bf16[1024,2048]{1,0:T(8,128)(2,1)}, f32[8,2048]{1,0:T(8,128)}) custom-call(bf16[2,1024,896]{2,1,0:T(8,128)(2,1)} %get-tuple-element.88.refs_0_.refs_1_, bf16[2,2048,896]{2,1,0:T(8,128)(2,1)} %bitcast.127, bf16[1024,2048]{1,0:T(8,128)(2,1)} %bitcast.136), custom_call_target="tpu_custom_call" | custom-call | bytes 42000000 | tf_op jit(solution)/shard_map/input_grads/pallas_call | solution.py:351
  482.1 1.3 pad.21.refs_2_
  483.6 2.0 bitcast_convert_fusion
  485.7 24.5 %mixer_weight_grads.1 = (bf16[4,2,512,896]{3,2,1,0:T(8,128)(2,1)}, bf16[2,4,1,128,1408]{4,3,2,1,0:T(8,128)(2,1)}) custom-call(bf16[1024,2048]{1,0:T(8,128)(2,1)} %get-tuple-element.68.refs_0_, bf16[2,1024,896]{2,1,0:T(8,128)(2,1)} %get-tuple-element.88.refs_0_.refs_1_, f32[2048,128]{1,0:T(8,128)} %pad.21.refs_2_, bf16[1,4,128,1408]{3,2,1,0:T(8,128)(2,1)} %bitcast.160), custom_call_target="tpu_custom_call" | custom-call | bytes 60000000 | tf_op jit(solution)/shard_map/mixer_weight_grads/pallas_call | solution.py:351
  510.1 1.8 reduce-scatter.8.cloned.1.call-done
  511.9 98.1 %end_moves.1 = (f32[128,2048]{1,0:T(8,128)}, f32[128,2048]{1,0:T(8,128)}, f32[128,2048]{1,0:T(8,128)}, f32[2,4,128,128]{3,2,1,0:T(8,128)}, f32[128,2048]{1,0:T(8...) custom-call(bf16[4,2,512,896]{3,2,1,0:T(8,128)(2,1)} %get-tuple-element.92.g_ref, bf16[4,256,2048]{2,1,0:T(8,128)(2,1)} %bitcast.142, ...), custom_call_target="tpu_custom_call" | custom-call | bytes 285000000 | tf_op jit(solution)/shard_map/end_moves/pallas_call | solution.py:674
  610.0 1.1 slice_reduce_fusion.1
  611.1 1.1 slice_bitcast_fusion.1
  614.5 5.6 hidden_rows.1
  620.1 2.3 copy.107
  622.4 1.3 copy.108
  624.3 1.0 copy.109
  626.9 1.0 copy.111
  627.9 1.0 copy.112
  (106 shorter events, 21.8 us)
Async XLA Ops:
  7.2 99.3 %copy-start = (bf16[352,2048]{1,0:T(8,128)(2,1)S(1)}, bf16[352,2048]{1,0:T(8,128)(2,1)}, u32[]{:S(2)}) copy-start(bf16[352,2048]{1,0:T(8,128)(2,1)} %param.28) | copy-start | bytes 4325380
  7.2 6.1 copy-start.17
  7.2 107.8 %all-gather.5.cloned.1.call-start = ((), (), s32[]{:S(2)}) async-start(), calls=%async_computation.3 | async-start | bytes 1310720 | tf_op jit(solution)/shard_map/all_gather | solution.py:1341
  9.1 249.2 %all-gather.7.cloned.1.call-start = ((), (), s32[]{:S(2)}) async-start(), calls=%async_computation.4 | async-start | bytes 12976128 | tf_op jit(solution)/shard_map/all_gather | solution.py:1288
  106.5 184.8 %all-gather.9.cloned.1.call-start = ((), (), s32[]{:S(2)}) async-start(), calls=%async_computation.8 | async-start | bytes 6488064 | tf_op jit(solution)/shard_map/all_gather | solution.py:1288
  107.5 290.4 %reduce-scatter.4.cloned.1.call-start = ((), (), s32[]{:S(2)}) async-start(), calls=%async_computation.5 | async-start | bytes 6488064 | tf_op jit(solution)/shard_map/reduce_scatter | solution.py:1292
  111.2 48.5 %copy-start.16 = (f32[2,4,128]{2,1,0:T(4,128)}, f32[2,4,128]{2,1,0:T(4,128)S(1)}, u32[]{:S(2)}) copy-start(f32[2,4,128]{2,1,0:T(4,128)S(1)} %broadcast_add_fusion) | copy-start | bytes 12292
  210.6 1.9 copy-start.4
  212.5 3.7 copy-start.5
  217.6 169.3 %copy-start.2 = (f32[256,2048]{1,0:T(8,128)}, f32[256,2048]{1,0:T(8,128)S(1)}, u32[]{:S(2)}) copy-start(f32[256,2048]{1,0:T(8,128)S(1)} %get-tuple-element.175.attended_ref) | copy-start | bytes 6291460
  291.2 194.4 %reduce-scatter.6.cloned.1.call-start = ((), (), s32[]{:S(2)}) async-start(), calls=%async_computation.6 | async-start | bytes 12976128 | tf_op jit(solution)/shard_map/reduce_scatter | solution.py:1292
  355.2 156.7 %reduce-scatter.8.cloned.1.call-start = ((), (), s32[]{:S(2)}) async-start(), calls=%async_computation.7 | async-start | bytes 2359296 | tf_op jit(solution)/shard_map/reduce_scatter | solution.py:1292
  358.2 1.6 copy-start.11
  360.6 2.3 copy-start.3
  386.3 1.2 copy-start.7
  387.5 3.2 copy-start.6
  389.5 1.0 copy-start.8
  463.0 1.1 copy-start.9
  463.0 1.1 copy-start.18
  464.1 19.3 %collective-permute-start = (bf16[176,2048]{1,0:T(8,128)(2,1)S(1)}, bf16[176,2048]{1,0:T(8,128)(2,1)S(1)}, u32[]{:S(2)}, u32[]{:S(2)}) collective-permute-start(bf16[176,2048]{1,0:T(8,128)(2,1)S(1)} %bitcast.156), channel_id=1, source_target_pairs={{0,1},{1,0},{2,3},{3,2},{4,5},{5,4},{6,7},{7,6},{8,9},{9,8},{10,11... | collective-permute-start | bytes 2162696 | tf_op jit(solution)/shard_map/ppermute | solution.py:1296
  614.5 7.9 %copy-start.10 = (f32[256,2048]{1,0:T(8,128)S(1)}, f32[256,2048]{1,0:T(8,128)}, u32[]{:S(2)}) copy-start(f32[256,2048]{1,0:T(8,128)} %get-tuple-element.98) | copy-start | bytes 6291460
  622.4 2.0 copy-start.15
  624.3 1.6 copy-start.14
  624.3 2.6 copy-start.13
  625.9 1.9 copy-start.12
  625.9 2.9 copy-start.1
Sparse Core Ops, SparseCore 0:
  10.2 36.6 all-gather.4
  106.6 108.0 all-gather.6
  216.9 58.7 all-gather.8
  291.4 63.4 reduce-scatter.3
  357.0 117.6 reduce-scatter.5
  477.4 34.4 reduce-scatter.7

commit v5 on v4

--- a/solution.py
+++ b/solution.py
@@ -281,6 +281,8 @@
         return jax.ShapeDtypeStruct((2, 4, a.shape[0]) + a.shape[2:], a.dtype)
     if kind == "reduce_near":
         return jax.ShapeDtypeStruct((2, 2, a.shape[1] // 2) + a.shape[2:], a.dtype)
+    if kind == "swap_half":
+        return jax.ShapeDtypeStruct(a.shape[:1] + a.shape[2:], a.dtype)
     if kind in ("swap_core", "keep", "gather_far", "reduce_far"):
         return jax.ShapeDtypeStruct(a.shape, a.dtype)
     block = a.shape if kind in ("copy_homes", "copy_chips", "gather_near") else a.shape[1:]
@@ -300,6 +302,8 @@
         return (ReduceNear if kind == "reduce_near" else ReduceFar)(a_ref, out_ref, y, x, *sems[:2])
     if kind == "swap_core":
         return Swap(a_ref, out_ref, c, *sems[:2])
+    if kind == "swap_half":
+        return Swap(a_ref.at[:, 1 - c], out_ref, c, *sems[:2])
     if kind == "keep":
         return Stay(a_ref, out_ref, *sems[2:])
 
@@ -522,9 +526,9 @@
 
 
 def end_kernel(planes, g_ref, gn_ref, block_ref, w_ref, grad_attended_ref, x_ref, gain_ref, attended_ref, *refs):
-    outs, w_out_ref, grad_ref, output_ref, refs = refs[:4], refs[4], refs[5], refs[6], refs[7:]
-    own_ref, core_ref, ring_ref, sum_ref, land_ref, w_land_ref, shares_ref, mine_ref, refs = *refs[:8], refs[8:]
-    load, core_send, core_recv, ring_send, ring_recv, spread_send, spread_recv, w_send, w_recv, w_local = refs[:10]
+    land_ref, w_land_ref, grad_ref, output_ref, refs = *refs[:4], refs[4:]
+    own_ref, core_ref, ring_ref, sum_ref, shares_ref, mine_ref, refs = *refs[:6], refs[6:]
+    load, core_send, core_recv, ring_send, ring_recv, spread_send, spread_recv, w_send, w_recv, local = refs[:10]
     mine_load, shares_load, shares_send, shares_recv, *rooms = refs[10:]
     y, x, c, z = (lax.axis_index(name) for name in ("y", "x", "c", "z"))
     chip, other = y * 2 + x, {"c": 1 - c}
@@ -542,7 +546,12 @@
 
     loads = [pltpu.make_async_copy(g_ref.at[place(s), c], own_ref.at[s], load.at[s]) for s in range(planes)]
     across = [
-        remote(g_ref.at[place(s), 1 - c], core_ref.at[s], core_send.at[s], core_recv.at[s], other) for s in range(planes)
+        [
+            remote(
+                g_ref.at[place(s), 1 - c, parts[part]], core_ref.at[s, parts[part]], core_send.at[s, part],
+                core_recv.at[s, part], other,
+            ) for part in range(2)
+        ] for s in range(planes)
     ]
     shares_across = [
         remote(gn_ref.at[2 * i + 1 - c], shares_ref.at[2 * c + i], shares_send.at[i], shares_recv.at[i], other)
@@ -558,14 +567,10 @@
     ]
     out_sum = PlaneSum(block_ref, rooms[:7], y, x)
     in_sum = PlaneSum(shares_ref, rooms[7:], y, x)
+    for copy in across[0] + loads[:1]:
+        copy.start()
     out_sum.start()
-    for s in range(planes):
-        across[s].start()
-        loads[s].start()
-        if s == 0:
-            for copy in shares_across + shares_own + mine:
-                copy.start()
-    w_stay = pltpu.make_async_copy(w_ref, w_land_ref.at[c], w_local)
+    w_stay = pltpu.make_async_copy(w_ref, w_land_ref.at[c], local.at[0])
     w_sent = remote(w_ref, w_land_ref.at[c], w_send.at[0], w_recv.at[0], device(goal, c))
     w_passed = remote(w_land_ref.at[c], w_land_ref.at[c], w_send.at[1], w_recv.at[1], other)
     pl.when(goal == here)(w_stay.start)
@@ -581,17 +586,12 @@
     def in_own(part, i):
         return shares_ref[blocks[part][i], token_parts[part], :]
 
+    tokens = output_ref.shape[0] // 2
+    every = slice(0, tokens)
     for s in range(planes):
-        if s == 1:
-            for copy in mine:
-                copy.wait()
-            out_sum.go_on(out_own)
-            pl.when(goal != here)(w_sent.start)
-        if s == planes - 1:
-            in_sum.go_on(in_own)
-        across[s].wait_recv()
         loads[s].wait()
         for part in range(2):
+            across[s][part].wait_recv()
             total = own_ref[s, parts[part], :].astype(F32) + core_ref[s, parts[part], :].astype(F32)
             if s > 0:
                 ring(s - 1, part).wait_recv()
@@ -600,11 +600,24 @@
             if s < planes - 1:
                 ring(s, part).start()
         if s == 0:
+            for n in range(1, planes):
+                for part in range(2):
+                    across[n][part].start()
+                loads[n].start()
+            for copy in shares_across + shares_own + mine:
+                copy.start()
             for copy in shares_across:
                 copy.wait_recv()
             for copy in shares_own:
                 copy.wait()
             in_sum.start()
+        if s == 1:
+            for copy in mine:
+                copy.wait()
+            out_sum.go_on(out_own)
+            pl.when(goal != here)(w_sent.start)
+        if s == planes - 2:
+            in_sum.go_on(in_own)
 
     sent, passed = [], []
     for flip in range(4):
@@ -617,38 +630,29 @@
         source = land_ref.at[c, at] if flip else some
         passed.append(remote(source, land_ref.at[c, at], spread_send.at[4 + flip], spread_recv.at[4 + flip], other))
     passed[0].start()
-    land_ref[c, chip] = sum_ref[planes - 1, pl.ds(pl.multiple_of(chip * size, size), size), :]
+    stay = pltpu.make_async_copy(
+        sum_ref.at[planes - 1, pl.ds(pl.multiple_of(chip * size, size), size)], land_ref.at[c, chip], local.at[1]
+    )
+    stay.start()
+    out_sum.far.wait()
+    for part in range(2):
+        here_rows = slice(part * tokens, (part + 1) * tokens)
+        output_ref[here_rows, :] = (attended_ref[here_rows, :] + out_sum.total(out_own, part, every)).astype(BF16)
     pl.when(goal == here)(w_stay.wait)
     pl.when(goal != here)(w_sent.wait)
     w_passed.start()
-    out_sum.far.wait()
-    tokens = output_ref.shape[0] // 2
-    some = slice(0, tokens)
-    for part in range(2):
-        here_rows = slice(part * tokens, (part + 1) * tokens)
-        output_ref[here_rows, :] = (attended_ref[here_rows, :] + out_sum.total(out_own, part, some)).astype(BF16)
     for copy, onward in zip(sent, passed[1:]):
         copy.wait_recv()
         onward.start()
     in_sum.far.wait()
     for part in range(2):
         here_rows = slice(part * tokens, (part + 1) * tokens)
-        input_back(in_sum.total(in_own, part, some), here_rows, grad_attended_ref, x_ref, gain_ref, grad_ref)
+        input_back(in_sum.total(in_own, part, every), here_rows, grad_attended_ref, x_ref, gain_ref, grad_ref)
     for copy in passed:
         copy.wait_recv()
-    wide = DEPTH // 2
-    for at in range(4):
-        for core in range(2):
-            block = land_ref[core, at].astype(F32)
-            columns = pl.ds((2 * at + core) * wide, wide)
-            for n in range(3):
-                outs[n][:, columns] = block[:, n * wide:(n + 1) * wide]
-            outs[3][core, at] = block[:, 3 * wide:]
     w_passed.wait()
-    wide = w_land_ref.shape[2]
-    for core in range(2):
-        w_out_ref[:, core * wide:(core + 1) * wide] = w_land_ref[core].astype(F32)
-    for copy in sent + passed + across + shares_across:
+    stay.wait()
+    for copy in sent + passed + shares_across + [copy for both in across for copy in both]:
         copy.wait_send()
     for s in range(planes - 1):
         for part in range(2):
@@ -667,7 +671,6 @@
     planes, _, rows, columns = grads.shape
     here, features = rows // 4, x.shape[1]
     any_place, in_vmem = pl.BlockSpec(memory_space=pl.ANY), pl.BlockSpec(memory_space=pltpu.VMEM)
-    matrix = jax.ShapeDtypeStruct((here, features), F32)
     blocks = pltpu.VMEM((planes, rows, columns), BF16)
     sem = pltpu.SemaphoreType.DMA
     half = (x.shape[0] // 2, features)
@@ -675,17 +678,17 @@
         functools.partial(end_kernel, planes),
         name="end_moves",
         out_shape=[
-            matrix, matrix, matrix, jax.ShapeDtypeStruct((2, 4, here, TILE), F32), matrix,
+            jax.ShapeDtypeStruct((2, 4, here, columns), BF16), jax.ShapeDtypeStruct((2,) + w.shape, BF16),
             jax.ShapeDtypeStruct(x.shape, F32), jax.ShapeDtypeStruct(x.shape, BF16),
         ],
         in_specs=[any_place] * 4 + [in_vmem] * 4,
-        out_specs=[in_vmem] * 7,
+        out_specs=[any_place] * 2 + [in_vmem] * 2,
         scratch_shapes=[
             blocks, blocks, pltpu.VMEM((planes - 1, rows, columns), BF16), blocks,
-            pltpu.VMEM((2, 4, here, columns), BF16), pltpu.VMEM((2,) + w.shape, BF16), pltpu.VMEM(gn.shape, gn.dtype),
+            pltpu.VMEM(gn.shape, gn.dtype),
             pltpu.VMEM((2, 2) + half, BF16),
-            sem((planes,)), sem((planes,)), sem((planes,)), sem((planes - 1, 2)), sem((planes - 1, 2)), sem((8,)), sem((8,)),
-            sem((2,)), sem((2,)), sem, sem((4,)), sem((2,)), sem((2,)), sem((2,)),
+            sem((planes,)), sem((planes, 2)), sem((planes, 2)), sem((planes - 1, 2)), sem((planes - 1, 2)), sem((8,)), sem((8,)),
+            sem((2,)), sem((2,)), sem((2,)), sem((4,)), sem((2,)), sem((2,)), sem((2,)),
         ] + sum_rooms(*x.shape) + sum_rooms(*x.shape),
         compiler_params=pltpu.CompilerParams(collective_id=collective, has_side_effects=True, vmem_limit_bytes=60 << 20),
         cost_estimate=cost(95),
@@ -876,6 +879,19 @@
     ]
 
 
+def document_numbers(begins_ref, length):
+    starts = [
+        jnp.concatenate([begins_ref[2 * r, :1, :], begins_ref[2 * r + 1, :1, :]], axis=1).astype(F32) for r in range(2)
+    ]
+    place = lax.broadcasted_iota(jnp.int32, (8, length), 0)
+    starts = jnp.where(place == 0, starts[0], jnp.where(place == 1, starts[1], 0.0)).astype(BF16)
+    s = lax.broadcasted_iota(jnp.int32, (length, length), 0)
+    t = lax.broadcasted_iota(jnp.int32, (length, length), 1)
+    counts = dot(starts, ones_where(s <= t), NN)
+    turned = counts.T
+    return [(turned[:, r:r + 1], counts[r:r + 1, :]) for r in range(2)]
+
+
 def silu_low(v):
     return (v * sigmoid(v)).astype(BF16)
 
@@ -884,14 +900,15 @@
     return v.astype(BF16)
 
 
-def forward_kernel(pre_ref, lf_ref, gain_ref, dcol_ref, drow_ref,
+def forward_kernel(pre_ref, lf_ref, gain_ref, begins_ref,
                    mixed_ref, s_ref, p_ref, b_ref, a_ref, decay_ref, reach_ref, e_ref):
     length = lf_ref.shape[0]
     tiles = length // TILE
     scale = DEPTH ** -0.5
+    documents = document_numbers(begins_ref, length)
     q, k = projections(pre_ref, 0, length, silu_low), projections(pre_ref, 1, length, silu_low)
     for r in range(2):
-        same = dcol_ref[r] == drow_ref[r]
+        same = documents[r][0] == documents[r][1]
         a_ref[r] = jnp.where(same, inner(q, k, r), 0.0)
     prepare(lf_ref, decay_ref, reach_ref, e_ref, tiles)
     weighted_sums(a_ref, s_ref, gain_ref, decay_ref, reach_ref, e_ref, tiles)
@@ -909,7 +926,7 @@
     paired_weights(p_ref, b_ref, gain_ref, decay_ref, reach_ref, e_ref, tiles)
     v = projections(pre_ref, 2, length, low)
     for r in range(2):
-        b = jnp.where(dcol_ref[r] == drow_ref[r], b_ref[r], 0.0)
+        b = jnp.where(documents[r][0] == documents[r][1], b_ref[r], 0.0)
         b_ref[r] = b
         high, rest = parts_of(b)
         for f in range(2):
@@ -924,18 +941,19 @@
     return ones_where((s < half) & (t == s + r * SLOTS + f * half))
 
 
-def backward_kernel(pre_ref, g_ref, lf_ref, gain_ref, rate_ref, dcol_ref, drow_ref, s_ref, p_ref, b_ref,
+def backward_kernel(pre_ref, g_ref, lf_ref, gain_ref, rate_ref, begins_ref, s_ref, p_ref, b_ref,
                     out_ref, bias_ref, a_ref, at_ref, dot_ref, h_ref, back_ref, decay_ref, reach_ref, e_ref):
     length = lf_ref.shape[0]
     tiles, depth = length // TILE, DEPTH // 2
     scale = DEPTH ** -0.5
     first_all, first = first_row(length), first_row(TILE)
     t, s = places()
+    documents = document_numbers(begins_ref, length)
     q, k = projections(pre_ref, 0, length, silu_low), projections(pre_ref, 1, length, silu_low)
     v = projections(pre_ref, 2, length, low)
     grads = [[g_ref[r, :, f].reshape(length, depth) for r in range(2)] for f in range(2)]
     for r in range(2):
-        same = dcol_ref[r] == drow_ref[r]
+        same = documents[r][0] == documents[r][1]
         a_ref[r] = jnp.where(same, inner(grads, v, r), 0.0)
         at_ref[0, r] = jnp.where(same, inner(k, q, r), 0.0)
         at_ref[1, r] = jnp.where(same, inner(v, grads, r), 0.0)
@@ -983,7 +1001,7 @@
 
     for r in range(2):
         rows = slice(r * length, (r + 1) * length)
-        c = parts_of(jnp.where(dcol_ref[r] == drow_ref[r], a_ref[r], 0.0))
+        c = parts_of(jnp.where(documents[r][0] == documents[r][1], a_ref[r], 0.0))
         w = parts_of(b_ref[r])
         for f in range(2):
             gq = dot(c[0], k[f][r], NN) + dot(c[1], k[f][r], NN)
@@ -1012,13 +1030,13 @@
     return s * (1.0 + v * (1.0 - s))
 
 
-def mix_forward(pre, lf, gain, doc, moves, collective):
+def mix_forward(pre, lf, gain, begins, moves, collective):
     length = lf.shape[0]
     lanes = (length, 2 * SLOTS)
     square = (2, length, length)
     in_vmem = pl.BlockSpec(memory_space=pltpu.VMEM)
     return compute(
-        forward_kernel, "mix_forward", (pre, lf, gain, doc[:, :, None], doc[:, None, :]), [in_vmem] * 5, [in_vmem] * 4,
+        forward_kernel, "mix_forward", (pre, lf, gain, begins), [in_vmem] * 4, [in_vmem] * 4,
         (
             jax.ShapeDtypeStruct((2, 2, 2, length // 2, DEPTH // 2), BF16), jax.ShapeDtypeStruct(lanes, F32),
             jax.ShapeDtypeStruct(lanes, F32), jax.ShapeDtypeStruct(square, F32),
@@ -1031,14 +1049,14 @@
     )
 
 
-def mix_backward(pre, g, lf, gain, rate, doc, s, p, b, moves, collective):
+def mix_backward(pre, g, lf, gain, rate, begins, s, p, b, moves, collective):
     length = lf.shape[0]
     lanes = (length, 2 * SLOTS)
     square = (2, length, length)
     in_vmem = pl.BlockSpec(memory_space=pltpu.VMEM)
     return compute(
-        backward_kernel, "mix_backward", (pre, g, lf, gain, rate, doc[:, :, None], doc[:, None, :], s, p, b),
-        [in_vmem] * 10, [in_vmem] * 2,
+        backward_kernel, "mix_backward", (pre, g, lf, gain, rate, begins, s, p, b),
+        [in_vmem] * 9, [in_vmem] * 2,
         (jax.ShapeDtypeStruct(pre.shape, BF16), jax.ShapeDtypeStruct((8, 2 * SLOTS), F32)), 30,
         scratch=[pltpu.VMEM(square, F32), pltpu.VMEM((2,) + square, F32)] + [pltpu.VMEM(lanes, F32)] * 5
         + [pltpu.VMEM((len(HALVES),) + lanes, F32)],
@@ -1110,27 +1128,29 @@
     )
 
 
-def out_kernel(own_ref, other_ref, grad_ref, out_ref):
+def out_kernel(mixed_ref, other_ref, grad_ref, out_ref):
     core = lax.axis_index("c")
     grads = None
-    for a_ref, at_y in ((own_ref, core), (other_ref, 1 - core)):
-        for x in range(2):
-            part = dot(a_ref[x, 0], grad_ref[2 * at_y + x], TN)
-            grads = part if grads is None else grads + part
+    for x in range(2):
+        part = dot(mixed_ref[x, core, 0], grad_ref[2 * core + x], TN) + dot(other_ref[x, 0], grad_ref[2 * (1 - core) + x], TN)
+        grads = part if grads is None else grads + part
     rows, wide = out_ref.shape[2:]
     for z in range(out_ref.shape[0]):
         for f in range(2):
             out_ref[z, f] = grads[z * rows:(z + 1) * rows, f * wide:(f + 1) * wide].astype(BF16)
 
 
-def out_grads(own, other, grad):
+def out_grads(mixed, other, grad):
     planes = lax.axis_size("z")
     features = grad.shape[2]
-    wide = own.shape[3]
+    wide = mixed.shape[4]
     rows = 2 * wide // planes
-    some = pl.BlockSpec((2, 1) + own.shape[2:], lambda f: (0, f, 0, 0))
     return compute(
-        out_kernel, "out_grads", (own, other, grad), [some, some, pl.BlockSpec(grad.shape, lambda f: (0, 0, 0))],
+        out_kernel, "out_grads", (mixed, other, grad),
+        [
+            pl.BlockSpec((2, 2, 1) + mixed.shape[3:], lambda f: (0, 0, f, 0, 0)),
+            pl.BlockSpec((2, 1) + other.shape[2:], lambda f: (0, f, 0, 0)), pl.BlockSpec(grad.shape, lambda f: (0, 0, 0)),
+        ],
         [pl.BlockSpec((planes // 2, 2, rows, features // 2), lambda f: (f, 0, 0, 0))],
         [jax.ShapeDtypeStruct((planes, 2, rows, features // 2), BF16)], 8, grid=(2,),
     )[0]
@@ -1242,30 +1262,42 @@
     )
 
 
-def project_kernel(x_ref, gain_ref, w_ref, normed_ref, pre_ref):
+def project_kernel(vectors, x_ref, w_ref, normed_ref, pre_ref, gains_ref):
+    @pl.when(pl.program_id(0) == 0)
+    def _():
+        first = vectors // TILE * TILE
+        columns = w_ref[0, :, first:first + TILE].astype(F32).T
+        gains_ref[...] = columns[vectors - first:vectors - first + 8, :]
+
     x = x_ref[...].astype(F32)
     ratio = lax.rsqrt(jnp.mean(x * x, axis=1, keepdims=True) + EPSILON)
-    normed = (x * ratio * gain_ref[...]).astype(BF16)
+    normed = (x * ratio * gains_ref[0:1, :]).astype(BF16)
     normed_ref[...] = normed
     for f in range(2):
         pre_ref[f] = dot(normed, w_ref[f], NN)
 
 
-def project(x, gain, w, moves, collective):
+def project(x, w, vectors, moves, collective):
     tokens, features = x.shape
     rows, columns = tokens // 4, w.shape[2]
     some = pl.BlockSpec((rows, features), lambda t: (t, 0))
     return compute(
-        project_kernel, "project", (x, gain, w),
-        [some, pl.BlockSpec((1, features), lambda t: (0, 0)), pl.BlockSpec(w.shape, lambda t: (0, 0, 0))],
-        [some, pl.BlockSpec((2, rows, columns), lambda t: (0, t, 0))],
-        [jax.ShapeDtypeStruct(x.shape, BF16), jax.ShapeDtypeStruct((2, tokens, columns), F32)],
+        functools.partial(project_kernel, vectors), "project", (x, w),
+        [some, pl.BlockSpec(w.shape, lambda t: (0, 0, 0))],
+        [some, pl.BlockSpec((2, rows, columns), lambda t: (0, t, 0)), pl.BlockSpec((8, features), lambda t: (0, 0))],
+        [
+            jax.ShapeDtypeStruct(x.shape, BF16), jax.ShapeDtypeStruct((2, tokens, columns), F32),
+            jax.ShapeDtypeStruct((8, features), F32),
+        ],
         28, grid=(4,), moves=moves, collective=collective,
     )
 
 
-def hidden_rows_kernel(planes, a_ref, gate_ref, up_ref):
+def finish_kernel(planes, a_ref, mixer_ref, w_ref, gate_ref, up_ref, *refs):
+    *mixer_out, forget_ref, w_out_ref, sums_ref = refs
     piece = gate_ref.shape[1] // (8 * planes)
+    wide, slots = DEPTH // 2, SLOTS // 2
+    sums = None
     for core in range(2):
         for chip in range(4):
             block = a_ref[core, chip].astype(F32)
@@ -1273,14 +1305,26 @@
                 for z in range(planes):
                     start = ((z * 4 + chip) * 2 + core) * piece
                     out_ref[:, start:start + piece] = block[:, (n * planes + z) * piece:(n * planes + z + 1) * piece]
-
-
-def hidden_rows(a, columns):
+            at = 2 * chip + core
+            for n, out_ref in enumerate(mixer_out):
+                out_ref[:, at * wide:(at + 1) * wide] = mixer_ref[core, chip, :, n * wide:(n + 1) * wide].astype(F32)
+            last = mixer_ref[core, chip, :, 3 * wide:].astype(F32)
+            forget_ref[:, at * slots:(at + 1) * slots] = last[:, :slots]
+            if core == 0:
+                sums = last if sums is None else sums + last
+        columns = w_ref.shape[2]
+        w_out_ref[:, core * columns:(core + 1) * columns] = w_ref[core].astype(F32)
+    sums_ref[...] = sums.T[slots:slots + 8, :]
+
+
+def finish(a, mixer, w, columns):
     rows = a.shape[2]
     in_vmem = pl.BlockSpec(memory_space=pltpu.VMEM)
+    widths = [columns, columns] + [HEADS * DEPTH] * 3 + [HEADS * SLOTS, HEADS * DEPTH]
     return compute(
-        functools.partial(hidden_rows_kernel, lax.axis_size("z")), "hidden_rows", (a,), [in_vmem], [in_vmem] * 2,
-        [jax.ShapeDtypeStruct((rows, columns), F32)] * 2, 6,
+        functools.partial(finish_kernel, lax.axis_size("z")), "finish", (a, mixer, w), [in_vmem] * 3,
+        [in_vmem] * 8, [jax.ShapeDtypeStruct((rows, width), F32) for width in widths] + [jax.ShapeDtypeStruct((8, rows), F32)],
+        10,
     )
 
 
@@ -1346,24 +1390,21 @@
     )
     hidden_w = gather_planes(hidden_w.reshape(4 * rows_here, -1))
     mixer_w = mixer_w.reshape(2, features, -1)
-    gain_attn, gain_ffn = (mixer_w[0, :, vectors + i].astype(F32) for i in range(2))
-    bias = mixer_w[0, :, vectors + 2].reshape(4 * planes, rows_here)[:, :bias_here].reshape(-1).astype(F32)
+    x_rows = x_rows.reshape(4 * positions, features)
+    normed, pre, gains, out_core = project(x_rows, mixer_w, vectors, [("copy_chips", out_half)], 13)
+    bias = gains[2].reshape(4 * planes, rows_here)[:, :bias_here].reshape(-1)
     bias = lax.dynamic_slice_in_dim(bias, head * SLOTS, SLOTS)
-    doc = jnp.cumsum(begins[:, 0].reshape(2, 2 * positions).astype(F32), axis=1)
-
-    x_rows = x_rows.reshape(4 * positions, features)
-    normed, pre, out_core = project(x_rows, gain_attn[None], mixer_w, [("copy_chips", out_half)], 13)
     z_total = pre[:, :, 3 * depth // 2:vectors].reshape(2, 2, 2 * positions, SLOTS // 2)
     z_total = z_total.transpose(2, 1, 0, 3).reshape(2 * positions, 2 * SLOTS) + jnp.tile(bias, 2)
     log_forget = jax.nn.log_sigmoid(z_total) / 8.0
     gain = -jnp.expm1(log_forget)
     mixed, scores, probs, paired, out_other, cot = mix_forward(
-        pre, log_forget, gain, doc, [("swap_core", out_core), ("gather_near", cot_here)], 3
+        pre, log_forget, gain, begins, [("swap_core", out_core), ("gather_near", cot_here)], 3
     )
     out_core, out_other = (a.reshape(features // 2, features) for a in (out_core, out_other))
-    mixed_own = own_half(mixed, 1)
+    mixed_rows = mixed
     mixed, mixed_other = move(
-        4, ("to_homes", mixed.reshape(4, 2 * positions, depth // 2)), ("swap_core", own_half(mixed, 1, 1 - c)), us=14
+        4, ("to_homes", mixed.reshape(4, 2 * positions, depth // 2)), ("swap_half", mixed), us=14
     )
     mixed = mixed.reshape(2 * HEADS, positions, depth // 2).transpose(1, 0, 2)
     mixed = mixed.reshape(positions, planes, 4, 2, rows_here // 2).transpose(3, 0, 2, 1, 4)
@@ -1374,7 +1415,7 @@
     )
 
     ratio_f = scaled(attended)
-    (normed_ffn,) = move(5, ("copy_chips", (attended * ratio_f * gain_ffn).astype(BF16)), us=38)
+    (normed_ffn,) = move(5, ("copy_chips", (attended * ratio_f * gains[1]).astype(BF16)), us=38)
     normed_ffn = normed_ffn.reshape(4 * positions, features)
     hidden, slopes, silus, cot = hidden_units(normed_ffn, hidden_w, [("gather_far", cot)], 6)
     cot = cot.reshape(4 * positions, features)
@@ -1395,7 +1436,7 @@
     grad_normed_ffn = (near[:, 1] + far.astype(F32)).reshape(positions, features)
     grad_down_w, grad_hidden_w = sum_planes(grad_down_w), sum_planes(grad_hidden_w)
     grad_gain_ffn = jnp.sum(grad_normed_ffn * attended * ratio_f, axis=0)
-    grad_attended = cot_here.astype(F32) + norm_back(grad_normed_ffn, gain_ffn, attended, ratio_f)
+    grad_attended = cot_here.astype(F32) + norm_back(grad_normed_ffn, gains[1], attended, ratio_f)
 
     grad_branch = grad_attended.astype(BF16)
     grad_mixed = [
@@ -1410,10 +1451,10 @@
     grad_mixed = grad_mixed.reshape(2, 2, 2, positions, depth // 2)
     rate = jax.nn.sigmoid(-z_total) / 8.0
     grad_pre, grad_bias, branch_chips = mix_backward(
-        pre, grad_mixed, log_forget, gain, rate, doc, scores, probs, paired, [("copy_chips", grad_branch)], 10
+        pre, grad_mixed, log_forget, gain, rate, begins, scores, probs, paired, [("copy_chips", grad_branch)], 10
     )
     grad_bias = jnp.sum(grad_bias[0].reshape(2, SLOTS), axis=0)
-    grad_out_w = out_grads(mixed_own, mixed_other, branch_chips)
+    grad_out_w = out_grads(mixed_rows, mixed_other, branch_chips)
     grad_normed, sums = input_grads(grad_pre, mixer_w, x_rows)
     grad_bias = jnp.zeros((HEADS, SLOTS), F32).at[head].set(grad_bias).reshape(4 * planes, bias_here)
     grad_bias = jnp.pad(grad_bias, ((0, 0), (0, rows_here - bias_here))).reshape(-1)
@@ -1424,19 +1465,17 @@
         normed, grad_pre, sums, [("spread", grad_hidden_w.reshape(1, 4, rows_here, -1))], 14
     )
     grad_out_w = sum_planes(grad_out_w)
-    grad_gate_w, grad_up_w = hidden_rows(grad_hidden_w[:, :, 0], w_gate.shape[1])
-    *grad_w, rest, grad_out_w, grad_input, output = end_moves(
+    mixer_rows, out_rows, grad_input, output = end_moves(
         11, grad_mixer_w, grad_normed.reshape(4, positions, features), block_out.reshape(4, positions, features),
-        grad_out_w, grad_attended, x_here, gain_attn[None], attended,
-    )
-
-    columns = SLOTS // 2
-    sums = jnp.sum(rest[0, :, :, columns:columns + 3], axis=0)
-    grad_forget_w = rest[..., :columns].transpose(2, 1, 0, 3).reshape(rows_here, HEADS * SLOTS)
+        grad_out_w, grad_attended, x_here, gains[:1], attended,
+    )
+    grad_gate_w, grad_up_w, *grad_w, grad_forget_w, grad_out_w, sums = finish(
+        grad_hidden_w[:, :, 0], mixer_rows, out_rows, w_gate.shape[1]
+    )
     grad_down_w = both_of(grad_down_w, "c").reshape(hidden_here, features).astype(F32)
     return (
-        output.reshape(inputs.shape), grad_input.reshape(inputs.shape), sums[:, 0], grad_w[0], grad_w[1], grad_w[2],
-        grad_forget_w, sums[:bias_here, 2], grad_out_w, sums[:, 1], grad_gate_w, grad_up_w, grad_down_w,
+        output.reshape(inputs.shape), grad_input.reshape(inputs.shape), sums[0], grad_w[0], grad_w[1], grad_w[2],
+        grad_forget_w, sums[2, :bias_here], grad_out_w, sums[1], grad_gate_w, grad_up_w, grad_down_w,
     )
 
 

time: 643 us -> 626 us (0.974)
  local copies, waits for them, and re-layouts: 42.3 us -> 31.4 us
    unnamed x46 -> x33, local copies, waits for them, and re-layouts: 16.7 us -> 9.51 us
  transfers between devices with their start and end apart: 7 -> 7, of which waited for: 1 -> 1; matrix products, arithmetic and copies ran while one was open for 8% -> 7% of each run, Pallas kernels for 70% -> 71%
where the time goes in v5:
time: 626 us; the launch traced here: 620 us
  Pallas kernels  546 us (87%)
  local copies, waits for them, and re-layouts  31.4 us (5%)
  between operations  14.8 us (2%)
  other arithmetic  14.1 us (2%)
  matrix products  10.1 us (2%)
    pallas_call x11, Pallas kernels, compute(): pl.pallas_call(functools.partial(compute_body, counts, kinds, grid, body)...  279 us
    pallas_call x1, Pallas kernels, end_moves(): pl.pallas_call(functools.partial(end_kernel, planes), name='end_moves', o...  96.8 us
    pallas_call x1, Pallas kernels, start_moves(): pl.pallas_call(functools.partial(start_kernel, kinds, planes), name='star...  92.5 us
    pallas_call x3, Pallas kernels, move(): pl.pallas_call(functools.partial(move_kernel, kinds, len(after)), name=ki...  66.9 us
  transfers between devices with their start and end apart: 7, of which 1 were waited for; matrix products, arithmetic and copies ran while one was open for 7% of the time, Pallas kernels for 71%

profile of v5, /device:TPU:0, one launch (start us, length us, event | category | flops | bytes accessed | tf_op | source)
XLA Modules:
  0.0 619.9 jit_solution(16062201266326890999)
XLA Ops:
  7.3 1.8 constant_dynamic-slice_fusion.1
  9.1 1.0 copy.70
  12.5 0.9 fusion.19.refs_3_
  13.9 92.5 %start_moves.1 = (s32[4,8,256]{2,1,0:T(8,128)}, bf16[4,256,2048]{2,1,0:T(8,128)(2,1)}, bf16[4,128,1408]{2,1,0:T(8,128)(2,1)}, bf16[2,4,4,128,896]{4,3,2,1,0:T(8,128)(2,1)}) custom-call(bf16[128,2048]{1,0:T(8,128)(2,1)} %refs_0_.1, bf16[128,2048]{1,0:T(8,128)(2,1)} %refs_1_.1, bf16[128,2048]{1,0:T(8,128)(2,1)} %refs_2_.1, ...), custom_call_target="tpu_custom_call" | custom-call | bytes 255000000 | tf_op jit(solution)/shard_map/start_moves/pallas_call | solution.py:485
  106.5 0.9 constant_dynamic-slice_fusion
  108.1 43.6 %project.1 = (bf16[1024,2048]{1,0:T(8,128)(2,1)}, f32[2,1024,896]{2,1,0:T(8,128)}, f32[8,2048]{1,0:T(8,128)}, bf16[4,4,64,2048]{3,2,1,0:T(8,128)(2,1)}) custom-call(bf16[1024,2048]{1,0:T(8,128)(2,1)} %bitcast.130, bf16[2,2048,896]{2,1,0:T(8,128)(2,1)} %bitcast.123, bf16[4,64,2048]{2,1,0:T(8,128)(2,1)} %all-gather.5.cloned.1.call-done.refs_2_), custom_call_target="tpu_custom_call" | custom-call | bytes 84000000 | tf_op jit(solution)/shard_map/project/pallas_call | solution.py:355
  151.7 1.3 slice.55
  153.5 1.6 fusion.26
  155.3 1.1 exponential-minus-one_negate_fusion
  156.4 31.9 %mix_forward.1 = (bf16[2,2,2,256,256]{4,3,2,1,0:T(8,128)(2,1)}, f32[512,128]{1,0:T(8,128)}, f32[512,128]{1,0:T(8,128)}, f32[2,512,512]{2,1,0:T(8,128)}, bf16[4,4...) custom-call(f32[2,1024,896]{2,1,0:T(8,128)} %get-tuple-element.73.refs_0_, ...), custom_call_target="tpu_custom_call" | custom-call | bytes 72000000 | tf_op jit(solution)/shard_map/mix_forward/pallas_call | solution.py:355
  188.3 13.8 %to_homes.1 = (bf16[4,512,256]{2,1,0:T(8,128)(2,1)}, bf16[2,2,256,256]{3,2,1,0:T(8,128)(2,1)}) custom-call(bf16[4,512,256]{2,1,0:T(8,128)(2,1)} %bitcast.133, bf16[2,2,2,256,256]{4,3,2,1,0:T(8,128)(2,1)} %get-tuple-element.77.refs_1_.refs_0_), custom_call_target="tpu_custom_call" | custom-call | bytes 42000000 | tf_op jit(solution)/shard_map/to_homes/pallas_call | solution.py:384
  202.1 1.6 copy.74
  203.8 3.6 convolution_add_fusion.1
  207.4 1.4 multiply_reduce_fusion.1
  208.8 1.4 multiply_convert_fusion.refs_0_
  210.2 39.4 %copy_chips.1 = bf16[4,256,2048]{2,1,0:T(8,128)(2,1)} custom-call(bf16[256,2048]{1,0:T(8,128)(2,1)} %multiply_convert_fusion.refs_0_), custom_call_target="tpu_custom_call" | custom-call | bytes 114000000 | tf_op jit(solution)/shard_map/copy_chips/pallas_call | solution.py:384
  249.6 22.2 %hidden_units.1 = (bf16[2,1024,704]{2,1,0:T(8,128)(2,1)}, bf16[2,1024,704]{2,1,0:T(8,128)(2,1)}, bf16[2,1024,704]{2,1,0:T(8,128)(2,1)}, bf16[4,256,2048]{2,1,0:T(8,128)(2,1)}) custom-call(bf16[1024,2048]{1,0:T(8,128)(2,1)} %bitcast.117, bf16[2,2048,1408]{2,1,0:T(8,128)(2,1)} %bitcast.115, ...), custom_call_target="tpu_custom_call", output_to_operand_aliasing={{3}: (2, {})} | custom-call | bytes 66000000 | tf_op jit(solution)/shard_map/hidden_units/pallas_call | solution.py:355
  271.8 11.0 %down_grads.1 = bf16[4,2,176,2048]{3,2,1,0:T(8,128)(2,1)} custom-call(bf16[2,1024,704]{2,1,0:T(8,128)(2,1)} %get-tuple-element.88.refs_0_.hidden_ref, bf16[1024,2048]{1,0:T(8,128)(2,1)} %bitcast.119), custom_call_target="tpu_custom_call" | custom-call | bytes 36000000 | tf_op jit(solution)/shard_map/down_grads/pallas_call | solution.py:1225
  282.8 33.7 %hidden_grads.1 = (bf16[2,1024,1408]{2,1,0:T(8,128)(2,1)}, bf16[1024,2048]{1,0:T(8,128)(2,1)}) custom-call(bf16[1024,2048]{1,0:T(8,128)(2,1)} %bitcast.120, bf16[2,1024,704]{2,1,0:T(8,128)(2,1)} %get-tuple-element.83.refs_1_, bf16[2,1024,704]{2,1,0:T(8,128)(2,1)} %get-tuple-element.84.refs_2_, bf16[2,2048,1408]{2,1,0:T(8,128)(2,1)} %bitcast.116, ...), custom_call_target="tpu_custom_call" | custom-call | bytes 102000000 | tf_op jit(solution)/shard_map/hidden_grads/pallas_call | solution.py:355
  316.6 29.6 %weight_grads.1 = (bf16[4,2,512,1408]{3,2,1,0:T(8,128)(2,1)}, bf16[2,2,128,2048]{3,2,1,0:T(8,128)(2,1)}) custom-call(bf16[1024,2048]{1,0:T(8,128)(2,1)} %bitcast.118, bf16[2,1024,1408]{2,1,0:T(8,128)(2,1)} %get-tuple-element.86.refs_1_, bf16[4,256,2048]{2,1,0:T(8,128)(2,1)} %bitcast.128), custom_call_target="tpu_custom_call" | custom-call | bytes 72000000 | tf_op jit(solution)/shard_map/weight_grads/pallas_call | solution.py:355
  346.3 2.7 fusion.25
  349.8 1.1 copy-done.11
  350.9 0.8 convert_add_fusion
  351.7 2.3 copy-done.3
  354.0 1.1 fusion.5.refs_2_
  355.1 19.7 %block_outputs.1 = (bf16[1024,2048]{1,0:T(8,128)(2,1)}, bf16[2,128,2048]{2,1,0:T(8,128)(2,1)}) custom-call(bf16[2,1024,704]{2,1,0:T(8,128)(2,1)} %get-tuple-element.88.refs_0_.hidden_ref, bf16[2,704,2048]{2,1,0:T(8,128)(2,1)} %bitcast.127, bf16[2,128,2048]{2,1,0:T(8,128)(2,1)} %fusion.5.refs_2_), custom_call_target="tpu_custom_call" | custom-call | bytes 36000000 | tf_op jit(solution)/shard_map/block_outputs/pallas_call | solution.py:355
  374.8 2.1 fusion
  378.2 2.0 fusion.23
  380.2 1.0 copy-done.8
  381.2 1.3 convolution_convert_fusion
  382.7 3.8 convolution_convert_fusion.1
  387.0 1.3 copy.80
  388.3 13.8 %from_homes.1 = bf16[4,512,256]{2,1,0:T(8,128)(2,1)} custom-call(bf16[4,512,256]{2,1,0:T(8,128)(2,1)} %bitcast.147, bf16[176,2048]{1,0:T(8,128)(2,1)} %bitcast.150), custom_call_target="tpu_custom_call" | custom-call | bytes 42000000 | tf_op jit(solution)/shard_map/from_homes/pallas_call | solution.py:384
  402.1 46.3 %mix_backward.1 = (bf16[2,1024,896]{2,1,0:T(8,128)(2,1)}, f32[8,128]{1,0:T(8,128)}, bf16[4,256,2048]{2,1,0:T(8,128)(2,1)}) custom-call(f32[2,1024,896]{2,1,0:T(8,128)} %get-tuple-element.73.refs_0_, bf16[2,2,2,256,256]{4,3,2,1,0:T(8,128)(2,1)} %bitcast.144, f32[512,128]{1,0:T(8,128)} %get-tuple-element.120.refs_1_.refs_2_, ...), custom_call_target="tpu_custom_call" | custom-call | bytes 90000000 | tf_op jit(solution)/shard_map/mix_backward/pallas_call | solution.py:355
  448.4 6.0 out_grads.1
  454.4 1.1 copy-done.9
  457.9 14.4 %input_grads.1 = (bf16[1024,2048]{1,0:T(8,128)(2,1)}, f32[8,2048]{1,0:T(8,128)}) custom-call(bf16[2,1024,896]{2,1,0:T(8,128)(2,1)} %get-tuple-element.93.refs_0_.refs_1_, bf16[2,2048,896]{2,1,0:T(8,128)(2,1)} %bitcast.124, bf16[1024,2048]{1,0:T(8,128)(2,1)} %bitcast.131), custom_call_target="tpu_custom_call" | custom-call | bytes 42000000 | tf_op jit(solution)/shard_map/input_grads/pallas_call | solution.py:355
  472.3 0.9 reduce_sum.47
  473.5 1.3 pad.21.refs_2_
  475.1 2.0 bitcast_convert_fusion
  477.1 24.4 %mixer_weight_grads.1 = (bf16[4,2,512,896]{3,2,1,0:T(8,128)(2,1)}, bf16[2,4,1,128,1408]{4,3,2,1,0:T(8,128)(2,1)}) custom-call(bf16[1024,2048]{1,0:T(8,128)(2,1)} %get-tuple-element.72.refs_0_, bf16[2,1024,896]{2,1,0:T(8,128)(2,1)} %get-tuple-element.93.refs_0_.refs_1_, f32[2048,128]{1,0:T(8,128)} %pad.21.refs_2_, bf16[1,4,128,1408]{3,2,1,0:T(8,128)(2,1)} %bitcast.155), custom_call_target="tpu_custom_call" | custom-call | bytes 60000000 | tf_op jit(solution)/shard_map/mixer_weight_grads/pallas_call | solution.py:355
  501.5 2.1 reduce-scatter.8.cloned.1.call-done
  503.6 96.8 %end_moves.1 = (bf16[2,4,128,896]{3,2,1,0:T(8,128)(2,1)}, bf16[2,128,1024]{2,1,0:T(8,128)(2,1)}, f32[256,2048]{1,0:T(8,128)}, bf16[256,2048]{1,0:T(8,128)(2,1)}) custom-call(bf16[4,2,512,896]{3,2,1,0:T(8,128)(2,1)} %get-tuple-element.97.g_ref, bf16[4,256,2048]{2,1,0:T(8,128)(2,1)} %bitcast.138, bf16[4,256,2048]{2,1,0:T(8,128)(2,1)} %bitcast.137, ...), custom_call_target="tpu_custom_call" | custom-call | bytes 285000000 | tf_op jit(solution)/shard_map/end_moves/pallas_call | solution.py:677
  600.4 7.6 %finish.1 = (f32[128,5632]{1,0:T(8,128)}, f32[128,5632]{1,0:T(8,128)}, f32[128,2048]{1,0:T(8,128)}, f32[128,2048]{1,0:T(8,128)}, f32[128,2048]{1,0:T(8,128)}, /*...) custom-call(bf16[2,4,128,1408]{3,2,1,0:T(8,128)(2,1)} %bitcast.149, ...), custom_call_target="tpu_custom_call" | custom-call | bytes 30000000 | tf_op jit(solution)/shard_map/finish/pallas_call | solution.py:355
  608.0 1.4 slice_bitcast_fusion.1
  609.3 1.2 slice_bitcast_fusion.2
  610.5 1.0 copy.87
  611.5 1.3 copy.88
  (81 shorter events, 10.3 us)
Async XLA Ops:
  7.2 99.3 %copy-start = (bf16[352,2048]{1,0:T(8,128)(2,1)S(1)}, bf16[352,2048]{1,0:T(8,128)(2,1)}, u32[]{:S(2)}) copy-start(bf16[352,2048]{1,0:T(8,128)(2,1)} %param.28) | copy-start | bytes 4325380
  7.2 6.1 copy-start.13
  7.2 100.9 %all-gather.5.cloned.1.call-start = ((), (), s32[]{:S(2)}) async-start(), calls=%async_computation.3 | async-start | bytes 1310720 | tf_op jit(solution)/shard_map/all_gather | solution.py:1385
  9.1 240.6 %all-gather.7.cloned.1.call-start = ((), (), s32[]{:S(2)}) async-start(), calls=%async_computation.4 | async-start | bytes 12976128 | tf_op jit(solution)/shard_map/all_gather | solution.py:1332
  106.5 176.4 %all-gather.9.cloned.1.call-start = ((), (), s32[]{:S(2)}) async-start(), calls=%async_computation.8 | async-start | bytes 6488064 | tf_op jit(solution)/shard_map/all_gather | solution.py:1332
  107.5 280.8 %reduce-scatter.4.cloned.1.call-start = ((), (), s32[]{:S(2)}) async-start(), calls=%async_computation.5 | async-start | bytes 6488064 | tf_op jit(solution)/shard_map/reduce_scatter | solution.py:1336
  202.1 1.7 copy-start.4
  203.7 3.6 copy-start.5
  208.8 168.8 %copy-start.2 = (f32[256,2048]{1,0:T(8,128)}, f32[256,2048]{1,0:T(8,128)S(1)}, u32[]{:S(2)}) copy-start(f32[256,2048]{1,0:T(8,128)S(1)} %get-tuple-element.130.attended_ref) | copy-start | bytes 6291460
  282.8 194.4 %reduce-scatter.6.cloned.1.call-start = ((), (), s32[]{:S(2)}) async-start(), calls=%async_computation.6 | async-start | bytes 12976128 | tf_op jit(solution)/shard_map/reduce_scatter | solution.py:1336
  346.2 157.4 %reduce-scatter.8.cloned.1.call-start = ((), (), s32[]{:S(2)}) async-start(), calls=%async_computation.7 | async-start | bytes 2359296 | tf_op jit(solution)/shard_map/reduce_scatter | solution.py:1336
  349.3 1.6 copy-start.11
  351.7 2.3 copy-start.3
  376.9 1.3 copy-start.7
  378.2 3.0 copy-start.6
  380.2 1.0 copy-start.8
  454.4 1.1 copy-start.9
  454.4 1.1 copy-start.14
  455.6 19.3 %collective-permute-start = (bf16[176,2048]{1,0:T(8,128)(2,1)S(1)}, bf16[176,2048]{1,0:T(8,128)(2,1)S(1)}, u32[]{:S(2)}, u32[]{:S(2)}) collective-permute-start(bf16[176,2048]{1,0:T(8,128)(2,1)S(1)} %bitcast.151), channel_id=1, source_target_pairs={{0,1},{1,0},{2,3},{3,2},{4,5},{5,4},{6,7},{7,6},{8,9},{9,8},{10,11... | collective-permute-start | bytes 2162696 | tf_op jit(solution)/shard_map/ppermute | solution.py:1340
  600.4 10.1 %copy-start.12 = (bf16[256,2048]{1,0:T(8,128)(2,1)S(1)}, bf16[256,2048]{1,0:T(8,128)(2,1)}, u32[]{:S(2)}) copy-start(bf16[256,2048]{1,0:T(8,128)(2,1)} %get-tuple-element.102) | copy-start | bytes 3145732
  608.0 3.5 copy-start.10
  610.5 2.3 copy-start.1
Sparse Core Ops, SparseCore 0:
  10.2 36.6 all-gather.4
  106.6 108.1 all-gather.6
  216.9 58.7 all-gather.8
  282.9 63.7 reduce-scatter.3
  348.8 117.6 reduce-scatter.5
  469.2 34.3 reduce-scatter.7
